TPU v7x, 32 devices: a whole 2x2x4 slice. The times are simulated.
32 devices in a mesh: row: 4 (over z), col: 2 (over y), layer: 4 (over x, core).
Axes of the slice: x: 2, y: 2, z: 4, core: 2. Of those that a mesh axis runs over, the one named last changes fastest.
Arguments:
- a_blocks: bfloat16 [256, 128, 128], P(('row', 'col', 'layer')), may hold values from -0.5 to 0.5
- a_codes: int32 [256], P(('row', 'col', 'layer')), may hold values from -1 to 47, as said below
- b_blocks: bfloat16 [512, 128, 128], P(('row', 'col', 'layer')), may hold values from -6 to 6
- b_codes: int32 [512], P(('row', 'col', 'layer')), may hold values from -1 to 23, as said below
Outputs:
- product: bfloat16 [2048, 1024], P(('row', 'layer'), 'col')
Inputs may be any that keep to these rules, and one draw needn't show every extreme that they name: `a_codes`: slots that one owner receives (same o, same r and l, all q) carry distinct codes; in every group of 2 owners some owner receives 8 live slots, and every owner at least one. `b_codes`: slots that one owner receives (same o, same c and l, all q) carry distinct codes; in every group of 4 owners some owner receives 16 live slots, and every owner at least one.
All inputs are finite; a program needn't handle non-finite values.
Results may differ from a plain program's by a relative error of at most 0.001.
Values may be sent and summed in bfloat16 or wider, within the bound.
No kernel may reach another device: no remote copies, remote signals or barrier semaphores. Data moves between devices by JAX's collectives and lax.ppermute only.
A program may use at most 64 MiB of HBM per device.

v0:
```python
import jax
import jax.numpy as jnp
from jax import lax
from jax.sharding import PartitionSpec as P

RB = 4
CB = 4
KB = 6


def from_behind(block, axis, distance):
    devices = range(lax.axis_size(axis))
    route = [((i - distance) % len(devices), i) for i in devices]
    return lax.ppermute(block, axis, route)


def dense_left(block_stack, block_codes, part_index, pieces):
    block_width = block_stack.shape[1]
    is_live = block_codes >= 0
    row_of = block_codes // (pieces * KB)
    part_of = block_codes // KB % pieces
    inner_of = block_codes % KB
    selected = is_live & (part_of == part_index)
    row_hits = row_of[:, None] == jnp.arange(RB)[None, :]
    inner_hit = inner_of[:, None] == jnp.arange(KB)[None, :]
    weight = (selected[:, None, None] & row_hits[:, :, None] & inner_hit[:, None, :]).astype(
        jnp.bfloat16
    )
    dense_tile = jnp.einsum(
        "aik,axy->ixky", weight, block_stack, preferred_element_type=jnp.float32
    )
    return dense_tile.astype(jnp.bfloat16).reshape(RB * block_width, KB * block_width)


def dense_right(block_stack, block_codes):
    block_width = block_stack.shape[1]
    is_live = block_codes >= 0
    inner_of = block_codes // CB
    column_of = block_codes % CB
    inner_hit = inner_of[:, None] == jnp.arange(KB)[None, :]
    column_hit = column_of[:, None] == jnp.arange(CB)[None, :]
    weight = (is_live[:, None, None] & inner_hit[:, :, None] & column_hit[:, None, :]).astype(
        jnp.bfloat16
    )
    dense_tile = jnp.einsum(
        "skj,sxy->kxjy", weight, block_stack, preferred_element_type=jnp.float32
    )
    return dense_tile.astype(jnp.bfloat16).reshape(KB * block_width, CB * block_width)


def shards(a_blocks, a_codes, b_blocks, b_codes):
    row_count = lax.axis_size("row")
    col_count = lax.axis_size("col")
    pieces = row_count // col_count
    block_width = a_blocks.shape[1]
    row_index = lax.axis_index("row")
    col_index = lax.axis_index("col")
    a_stack, a_tags = (
        lax.all_to_all(a_blocks, "col", split_axis=0, concat_axis=0, tiled=True),
        lax.all_to_all(a_codes, "col", split_axis=0, concat_axis=0, tiled=True),
    )
    b_stack, b_tags = (
        lax.all_to_all(b_blocks, "row", split_axis=0, concat_axis=0, tiled=True),
        lax.all_to_all(b_codes, "row", split_axis=0, concat_axis=0, tiled=True),
    )

    def multiply(accumulated, left_stack, left_codes, right_stack, right_codes, piece_index):
        left_tile = dense_left(left_stack, left_codes, piece_index // col_count, pieces)
        right_tile = dense_right(right_stack, right_codes)
        return accumulated + jnp.dot(left_tile, right_tile, preferred_element_type=jnp.float32)

    start_sum = jnp.zeros((RB * block_width, CB * block_width), jnp.float32)

    def advance(visit_step, loop_state):
        accumulated, left_stack, left_codes, right_stack, right_codes = loop_state
        piece_index = (row_index + col_index + visit_step) % row_count
        accumulated = multiply(
            accumulated, left_stack, left_codes, right_stack, right_codes, piece_index
        )
        left_stack, left_codes = from_behind((left_stack, left_codes), "col", -1)
        right_stack, right_codes = from_behind((right_stack, right_codes), "row", -1)
        return (accumulated, left_stack, left_codes, right_stack, right_codes)

    loop_state = lax.fori_loop(
        0, row_count - 1, advance, (start_sum, a_stack, a_tags, b_stack, b_tags)
    )
    accumulated, left_stack, left_codes, right_stack, right_codes = loop_state
    last_piece = (row_index + col_index + row_count - 1) % row_count
    accumulated = multiply(
        accumulated, left_stack, left_codes, right_stack, right_codes, last_piece
    )
    reduced = lax.psum_scatter(accumulated, "layer", scatter_dimension=0, tiled=True)
    return reduced.astype(jnp.bfloat16)


def solution(mesh):
    placed = (
        P(("row", "col", "layer"), None, None),
        P(("row", "col", "layer")),
        P(("row", "col", "layer"), None, None),
        P(("row", "col", "layer")),
    )
    return jax.shard_map(
        shards, mesh=mesh, in_specs=placed, out_specs=P(("row", "layer"), "col"), check_vma=False
    )
```

profile of v0, /device:TPU:0, one launch (start us, length us, event | category | flops | bytes accessed | tf_op | source)
XLA Modules:
  0.0 129.4 jit_solution(7895519232165412908)
XLA Ops:
  6.5 1.3 %all_to_all.23 = s32[2,4,1]{1,0,2:T(2,128)} reshape(s32[8]{0:T(128)} %param.7) | data formatting | bytes 64 | tf_op jit(solution)/shard_map/all_to_all | solution.py:60
  7.8 4.2 %all-to-all-start.1 = ((s32[2,4,1]{1,2,0:T(1,128)}), s32[2,4,1]{1,2,0:T(1,128)S(1)}, u32[]{:S(2)}, u32[]{:S(2)}) async-start(s32[2,4,1]{1,2,0:T(1,128)} %bitcast), calls=%async_computation.1 | async-start | bytes 2048 | tf_op jit(solution)/shard_map/all_to_all | solution.py:60
  12.1 0.7 all_to_all.27
  12.8 2.9 %all-to-all-done.1 = s32[2,4,1]{1,2,0:T(1,128)S(1)} async-done(((s32[2,4,1]{1,2,0:T(1,128)}), s32[2,4,1]{1,2,0:T(1,128)S(1)}, u32[]{:S(2)}, u32[]{:S(2)}) %all-to-all-start.1) | async-done | bytes 64 | tf_op jit(solution)/shard_map/all_to_all | solution.py:60
  15.7 10.6 %all_to_all.34 = s32[4,4,1]{1,2,0:T(1,128)S(1)} all-to-all(s32[4,4,1]{1,2,0:T(1,128)S(1)} %bitcast.87), channel_id=1, replica_groups=mesh['row'=4,'col'=2,'layer'=4] {'row'}, dimensions={0} | all-to-all | bytes 128 | tf_op jit(solution)/shard_map/all_to_all | solution.py:64
  26.3 8.6 %all_to_all.35 = bf16[8,128,128]{2,1,0:T(8,128)(2,1)S(1)} all-to-all(bf16[8,128,128]{2,1,0:T(8,128)(2,1)} %param.6), channel_id=1, replica_groups=mesh['row'=4,'col'=2,'layer'=4] {'col'}, dimensions={0} | all-to-all | bytes 524288 | tf_op jit(solution)/shard_map/all_to_all | solution.py:59
  34.9 3.5 %all-to-all-start.2 = ((bf16[16,128,128]{2,1,0:T(8,128)(2,1)}), bf16[16,128,128]{2,1,0:T(8,128)(2,1)S(1)}, u32[]{:S(2)}, u32[]{:S(2)}) async-start(bf16[16,128,128]{2,1,0:T(8,128)(2,1)} %param.8), calls=%async_computation.2 | async-start | bytes 1048576 | tf_op jit(solution)/shard_map/all_to_all | solution.py:63
  39.1 0.7 reduce.6
  39.9 0.7 reduce.7
  40.8 8.6 %all-to-all-done.2 = bf16[16,128,128]{2,1,0:T(8,128)(2,1)S(1)} async-done(((bf16[16,128,128]{2,1,0:T(8,128)(2,1)}), bf16[16,128,128]{2,1,0:T(8,128)(2,1)S(1)}, u32[]{:S(2)}, u32[]{:S(2)}) %all-to-all-start.2) | async-done | bytes 524320 | tf_op jit(solution)/shard_map/all_to_all | solution.py:63
  49.8 39.0 %while.25 = (s32[]{:T(128)}, f32[512,512]{1,0:T(8,128)S(1)}, bf16[8,128,128]{2,0,1:T(8,128)(2,1)S(1)}, s32[8]{0:T(128)S(1)}, bf16[16,128,128]{2,0,1:T(8,128)(2,1...) while((s32[]{:T(128)}, f32[512,512]{1,0:T(8,128)S(1)}, ...), condition=%wide.region_1.2_spmd.clone, body=%wide.region_0.1_spmd.clone.sunk | while | flops 422839840 | bytes 12323018 | solution.py:84
  50.2 1.7 %collective-permute-start.1 = (s32[8]{0:T(128)S(1)}, s32[8]{0:T(128)S(1)}, u32[]{:S(2)}, u32[]{:S(2)}) collective-permute-start(s32[8]{0:T(128)S(1)} %copy.61), channel_id=1, source_target_pairs={{4,0},{0,4},{5,1},{1,5},{6,2},{2,6},{7,3},{3,7},{12,8},{8,12},{13,... | collective-permute-start | bytes 104 | tf_op jit(solution)/shard_map/while/body/eval_jaxpr/ppermute | solution.py:14
  51.9 1.5 %collective-permute-start.2 = (bf16[16,128,128]{2,0,1:T(8,128)(2,1)S(1)}, bf16[16,128,128]{2,0,1:T(8,128)(2,1)S(1)}, u32[]{:S(2)}, u32[]{:S(2)}) collective-permute-start(bf16[16,128,128]{2,0,1:T(8,128)(2,1)S(1)} %copy.62), channel_id=1, source_target_pairs={{8,0},{16,8},{24,16},{0,24},{9,1},{17,9},{25,17},{1,25},{10,2},{18... | collective-permute-start | bytes 1572872 | tf_op jit(solution)/shard_map/while/body/eval_jaxpr/ppermute | solution.py:14
  54.0 0.6 copy.51
  55.0 0.7 convolution_add_fusion.3
  56.3 5.7 %collective-permute-done.3 = s32[16]{0:T(128)S(1)} collective-permute-done((s32[16]{0:T(128)S(1)}, s32[16]{0:T(128)S(1)}, u32[]{:S(2)}, u32[]{:S(2)}) %collective-permute-start.3) | collective-permute-done | bytes 96 | tf_op jit(solution)/shard_map/while/body/eval_jaxpr/ppermute | solution.py:14
  62.0 0.6 collective-permute-start
  62.7 1.5 %collective-permute-start.1 = (s32[8]{0:T(128)S(1)}, s32[8]{0:T(128)S(1)}, u32[]{:S(2)}, u32[]{:S(2)}) collective-permute-start(s32[8]{0:T(128)S(1)} %copy.61), channel_id=1, source_target_pairs={{4,0},{0,4},{5,1},{1,5},{6,2},{2,6},{7,3},{3,7},{12,8},{8,12},{13,... | collective-permute-start | bytes 104 | tf_op jit(solution)/shard_map/while/body/eval_jaxpr/ppermute | solution.py:14
  64.2 4.4 %collective-permute-start.2 = (bf16[16,128,128]{2,0,1:T(8,128)(2,1)S(1)}, bf16[16,128,128]{2,0,1:T(8,128)(2,1)S(1)}, u32[]{:S(2)}, u32[]{:S(2)}) collective-permute-start(bf16[16,128,128]{2,0,1:T(8,128)(2,1)S(1)} %copy.62), channel_id=1, source_target_pairs={{8,0},{16,8},{24,16},{0,24},{9,1},{17,9},{25,17},{1,25},{10,2},{18... | collective-permute-start | bytes 1572872 | tf_op jit(solution)/shard_map/while/body/eval_jaxpr/ppermute | solution.py:14
  69.0 0.6 copy.51
  70.1 0.7 convolution_add_fusion.3
  70.8 4.7 %collective-permute-done.3 = s32[16]{0:T(128)S(1)} collective-permute-done((s32[16]{0:T(128)S(1)}, s32[16]{0:T(128)S(1)}, u32[]{:S(2)}, u32[]{:S(2)}) %collective-permute-start.3) | collective-permute-done | bytes 96 | tf_op jit(solution)/shard_map/while/body/eval_jaxpr/ppermute | solution.py:14
  75.5 0.9 collective-permute-start
  76.4 1.2 collective-permute-start.1
  77.7 4.4 %collective-permute-start.2 = (bf16[16,128,128]{2,0,1:T(8,128)(2,1)S(1)}, bf16[16,128,128]{2,0,1:T(8,128)(2,1)S(1)}, u32[]{:S(2)}, u32[]{:S(2)}) collective-permute-start(bf16[16,128,128]{2,0,1:T(8,128)(2,1)S(1)} %copy.62), channel_id=1, source_target_pairs={{8,0},{16,8},{24,16},{0,24},{9,1},{17,9},{25,17},{1,25},{10,2},{18... | collective-permute-start | bytes 1572872 | tf_op jit(solution)/shard_map/while/body/eval_jaxpr/ppermute | solution.py:14
  82.5 0.6 copy.51
  83.6 0.7 convolution_add_fusion.3
  84.3 4.4 %collective-permute-done.3 = s32[16]{0:T(128)S(1)} collective-permute-done((s32[16]{0:T(128)S(1)}, s32[16]{0:T(128)S(1)}, u32[]{:S(2)}, u32[]{:S(2)}) %collective-permute-start.3) | collective-permute-done | bytes 96 | tf_op jit(solution)/shard_map/while/body/eval_jaxpr/ppermute | solution.py:14
  90.0 1.9 %copy.19 = bf16[4,128,6,128]{1,0,3,2:T(4,128)(2,1)} copy(bf16[4,128,6,128]{3,2,0,1:T(8,128)(2,1)S(1)} %fusion.19) | data formatting | bytes 1572864 | tf_op jit(solution)/shard_map/convert_element_type | solution.py:32
  91.9 2.7 %convolution_add_fusion.1 = f32[512,512]{1,0:T(8,128)} fusion(f32[512,512]{1,0:T(8,128)S(1)} %get-tuple-element.256, bf16[96,8,4,128]{3,2,1,0:T(4,128)(2,1)S(1)} %bitcast.85, bf16[96,8,4,128]{3,2,1,0:T(4,128)(2,1)} %bitcast.86), kind=kOutput, calls=%fused_computation.41 | convolution fusion | flops 402915328 | bytes 3670016 | tf_op jit(solution)/shard_map/dot_general | solution.py:70
  94.6 26.3 %reduce-scatter.2.cloned.1.call-done = f32[128,512]{1,0:T(8,128)} async-done(((f32[512,512]{1,0:T(8,128)}), f32[128,512]{1,0:T(8,128)}) %reduce-scatter.2.cloned.1.call-update) | async-done | bytes 262160 | tf_op jit(solution)/shard_map/reduce_scatter | solution.py:92
  121.0 1.6 %convert_element_type.55 = bf16[128,512]{1,0:T(8,128)(2,1)} convert(f32[128,512]{1,0:T(8,128)} %reduce-scatter.2.cloned.1.call-done) | non-fusion elementwise | flops 65536 | bytes 393216 | tf_op jit(solution)/shard_map/convert_element_type | solution.py:93
  (74 shorter events, 6.2 us)
Async XLA Ops:
  7.8 7.9 %all-to-all-start.1 = ((s32[2,4,1]{1,2,0:T(1,128)}), s32[2,4,1]{1,2,0:T(1,128)S(1)}, u32[]{:S(2)}, u32[]{:S(2)}) async-start(s32[2,4,1]{1,2,0:T(1,128)} %bitcast), calls=%async_computation.1 | async-start | bytes 2048 | tf_op jit(solution)/shard_map/all_to_all | solution.py:60
  34.9 14.5 %all-to-all-start.2 = ((bf16[16,128,128]{2,1,0:T(8,128)(2,1)}), bf16[16,128,128]{2,1,0:T(8,128)(2,1)S(1)}, u32[]{:S(2)}, u32[]{:S(2)}) async-start(bf16[16,128,128]{2,1,0:T(8,128)(2,1)} %param.8), calls=%async_computation.2 | async-start | bytes 1048576 | tf_op jit(solution)/shard_map/all_to_all | solution.py:63
  38.4 82.5 %reduce-scatter.2.cloned.1.call-start = ((), (), s32[]{:S(2)}) async-start(), calls=%async_computation.5 | async-start | bytes 1310720 | tf_op jit(solution)/shard_map/reduce_scatter | solution.py:92
  49.8 12.2 %collective-permute-start = (bf16[8,128,128]{2,0,1:T(8,128)(2,1)S(1)}, bf16[8,128,128]{2,0,1:T(8,128)(2,1)S(1)}, u32[]{:S(2)}, u32[]{:S(2)}) collective-permute-start(bf16[8,128,128]{2,0,1:T(8,128)(2,1)S(1)} %copy.60), channel_id=1, source_target_pairs={{4,0},{0,4},{5,1},{1,5},{6,2},{2,6},{7,3},{3,7},{12,8},{8,12},{13,... | collective-permute-start | bytes 786440 | tf_op jit(solution)/shard_map/while/body/eval_jaxpr/ppermute | solution.py:14
  50.2 6.1 %collective-permute-start.1 = (s32[8]{0:T(128)S(1)}, s32[8]{0:T(128)S(1)}, u32[]{:S(2)}, u32[]{:S(2)}) collective-permute-start(s32[8]{0:T(128)S(1)} %copy.61), channel_id=1, source_target_pairs={{4,0},{0,4},{5,1},{1,5},{6,2},{2,6},{7,3},{3,7},{12,8},{8,12},{13,... | collective-permute-start | bytes 104 | tf_op jit(solution)/shard_map/while/body/eval_jaxpr/ppermute | solution.py:14
  51.9 10.0 %collective-permute-start.2 = (bf16[16,128,128]{2,0,1:T(8,128)(2,1)S(1)}, bf16[16,128,128]{2,0,1:T(8,128)(2,1)S(1)}, u32[]{:S(2)}, u32[]{:S(2)}) collective-permute-start(bf16[16,128,128]{2,0,1:T(8,128)(2,1)S(1)} %copy.62), channel_id=1, source_target_pairs={{8,0},{16,8},{24,16},{0,24},{9,1},{17,9},{25,17},{1,25},{10,2},{18... | collective-permute-start | bytes 1572872 | tf_op jit(solution)/shard_map/while/body/eval_jaxpr/ppermute | solution.py:14
  53.5 8.5 %collective-permute-start.3 = (s32[16]{0:T(128)S(1)}, s32[16]{0:T(128)S(1)}, u32[]{:S(2)}, u32[]{:S(2)}) collective-permute-start(s32[16]{0:T(128)S(1)} %copy.63), channel_id=1, source_target_pairs={{8,0},{16,8},{24,16},{0,24},{9,1},{17,9},{25,17},{1,25},{10,2},{18... | collective-permute-start | bytes 200 | tf_op jit(solution)/shard_map/while/body/eval_jaxpr/ppermute | solution.py:14
  62.0 13.5 %collective-permute-start = (bf16[8,128,128]{2,0,1:T(8,128)(2,1)S(1)}, bf16[8,128,128]{2,0,1:T(8,128)(2,1)S(1)}, u32[]{:S(2)}, u32[]{:S(2)}) collective-permute-start(bf16[8,128,128]{2,0,1:T(8,128)(2,1)S(1)} %copy.60), channel_id=1, source_target_pairs={{4,0},{0,4},{5,1},{1,5},{6,2},{2,6},{7,3},{3,7},{12,8},{8,12},{13,... | collective-permute-start | bytes 786440 | tf_op jit(solution)/shard_map/while/body/eval_jaxpr/ppermute | solution.py:14
  62.7 8.1 %collective-permute-start.1 = (s32[8]{0:T(128)S(1)}, s32[8]{0:T(128)S(1)}, u32[]{:S(2)}, u32[]{:S(2)}) collective-permute-start(s32[8]{0:T(128)S(1)} %copy.61), channel_id=1, source_target_pairs={{4,0},{0,4},{5,1},{1,5},{6,2},{2,6},{7,3},{3,7},{12,8},{8,12},{13,... | collective-permute-start | bytes 104 | tf_op jit(solution)/shard_map/while/body/eval_jaxpr/ppermute | solution.py:14
  64.2 11.3 %collective-permute-start.2 = (bf16[16,128,128]{2,0,1:T(8,128)(2,1)S(1)}, bf16[16,128,128]{2,0,1:T(8,128)(2,1)S(1)}, u32[]{:S(2)}, u32[]{:S(2)}) collective-permute-start(bf16[16,128,128]{2,0,1:T(8,128)(2,1)S(1)} %copy.62), channel_id=1, source_target_pairs={{8,0},{16,8},{24,16},{0,24},{9,1},{17,9},{25,17},{1,25},{10,2},{18... | collective-permute-start | bytes 1572872 | tf_op jit(solution)/shard_map/while/body/eval_jaxpr/ppermute | solution.py:14
  68.5 7.0 %collective-permute-start.3 = (s32[16]{0:T(128)S(1)}, s32[16]{0:T(128)S(1)}, u32[]{:S(2)}, u32[]{:S(2)}) collective-permute-start(s32[16]{0:T(128)S(1)} %copy.63), channel_id=1, source_target_pairs={{8,0},{16,8},{24,16},{0,24},{9,1},{17,9},{25,17},{1,25},{10,2},{18... | collective-permute-start | bytes 200 | tf_op jit(solution)/shard_map/while/body/eval_jaxpr/ppermute | solution.py:14
  75.5 13.2 %collective-permute-start = (bf16[8,128,128]{2,0,1:T(8,128)(2,1)S(1)}, bf16[8,128,128]{2,0,1:T(8,128)(2,1)S(1)}, u32[]{:S(2)}, u32[]{:S(2)}) collective-permute-start(bf16[8,128,128]{2,0,1:T(8,128)(2,1)S(1)} %copy.60), channel_id=1, source_target_pairs={{4,0},{0,4},{5,1},{1,5},{6,2},{2,6},{7,3},{3,7},{12,8},{8,12},{13,... | collective-permute-start | bytes 786440 | tf_op jit(solution)/shard_map/while/body/eval_jaxpr/ppermute | solution.py:14
  76.4 7.9 %collective-permute-start.1 = (s32[8]{0:T(128)S(1)}, s32[8]{0:T(128)S(1)}, u32[]{:S(2)}, u32[]{:S(2)}) collective-permute-start(s32[8]{0:T(128)S(1)} %copy.61), channel_id=1, source_target_pairs={{4,0},{0,4},{5,1},{1,5},{6,2},{2,6},{7,3},{3,7},{12,8},{8,12},{13,... | collective-permute-start | bytes 104 | tf_op jit(solution)/shard_map/while/body/eval_jaxpr/ppermute | solution.py:14
  77.7 11.1 %collective-permute-start.2 = (bf16[16,128,128]{2,0,1:T(8,128)(2,1)S(1)}, bf16[16,128,128]{2,0,1:T(8,128)(2,1)S(1)}, u32[]{:S(2)}, u32[]{:S(2)}) collective-permute-start(bf16[16,128,128]{2,0,1:T(8,128)(2,1)S(1)} %copy.62), channel_id=1, source_target_pairs={{8,0},{16,8},{24,16},{0,24},{9,1},{17,9},{25,17},{1,25},{10,2},{18... | collective-permute-start | bytes 1572872 | tf_op jit(solution)/shard_map/while/body/eval_jaxpr/ppermute | solution.py:14
  82.0 6.7 %collective-permute-start.3 = (s32[16]{0:T(128)S(1)}, s32[16]{0:T(128)S(1)}, u32[]{:S(2)}, u32[]{:S(2)}) collective-permute-start(s32[16]{0:T(128)S(1)} %copy.63), channel_id=1, source_target_pairs={{8,0},{16,8},{24,16},{0,24},{9,1},{17,9},{25,17},{1,25},{10,2},{18... | collective-permute-start | bytes 200 | tf_op jit(solution)/shard_map/while/body/eval_jaxpr/ppermute | solution.py:14
Sparse Core Ops, SparseCore 0:
  94.8 26.1 reduce-scatter.1
where the time goes:
time: 130 us; the launch traced here: 129 us
  waiting for transfers between devices  53.2 us (41%)
  starting transfers between devices  24.5 us (19%)
  blocking collectives  19.2 us (15%)
  between operations  13.5 us (10%)
  matrix products  7.73 us (6%)
  local copies, waits for them, and re-layouts  7.49 us (6%)
  other arithmetic  3.35 us (3%)
    reduce_scatter x1, waiting for transfers between devices, shards(): lax.psum_scatter(accumulated, 'layer', scatter_dimension=0, tiled=True)  26.3 us
    ppermute x12, starting transfers between devices, from_behind(): return lax.ppermute(block, axis, route)  16.7 us
    ppermute x12, waiting for transfers between devices, from_behind(): return lax.ppermute(block, axis, route)  15.4 us
    all_to_all x1, blocking collectives, shards(): lax.all_to_all(b_codes, 'row', split_axis=0, concat_axis=0, tiled=True)  10.6 us
    all_to_all x1, blocking collectives, shards(): lax.all_to_all(a_blocks, 'col', split_axis=0, concat_axis=0, tiled=True)  8.6 us
    all_to_all x1, waiting for transfers between devices, shards(): lax.all_to_all(b_blocks, 'row', split_axis=0, concat_axis=0, tiled=True)  8.58 us
    dot_general x4, matrix products, multiply(): jnp.dot(left_tile, right_tile, preferred_element_type=jnp.float32)  4.81 us
    all_to_all x1, starting transfers between devices, shards(): lax.all_to_all(a_codes, 'col', split_axis=0, concat_axis=0, tiled=True)  4.23 us
  transfers between devices with their start and end apart: 15, of which 7 were waited for; matrix products, arithmetic and copies ran while one was open for 7% of the time, Pallas kernels for 0%

commit v1 on v0

--- a/solution.py
+++ b/solution.py
@@ -1,6 +1,10 @@
+import functools
+
 import jax
 import jax.numpy as jnp
 from jax import lax
+from jax.experimental import pallas as pl
+from jax.experimental.pallas import tpu as pltpu
 from jax.sharding import PartitionSpec as P
 
 RB = 4
@@ -93,6 +97,173 @@
     return reduced.astype(jnp.bfloat16)
 
 
+WIDE = 16
+
+
+def middle_plan(mesh_shape):
+    return (mesh_shape["row"], mesh_shape["col"], mesh_shape["layer"]) == (4, 2, 4)
+
+
+def pack_body(codes_ref, a_ref, b_ref, a_out, b_out):
+    a_slots, width, _ = a_ref.shape
+    b_slots = b_ref.shape[0]
+
+    def code_rows(first, count):
+        rows = lax.broadcasted_iota(jnp.int32, (WIDE, width), 0)
+        values = jnp.full((WIDE, width), -1, jnp.int32)
+        for slot in range(count):
+            values = jnp.where(rows == slot, codes_ref[first + slot], values)
+        return values.astype(jnp.float32).astype(jnp.bfloat16)
+
+    for slot in range(a_slots):
+        a_out[pl.ds(slot * width, width), :] = a_ref[slot]
+    a_out[pl.ds(a_slots * width, WIDE), :] = code_rows(0, a_slots)
+    for slot in range(b_slots):
+        b_out[pl.ds(slot * width, width), :] = b_ref[slot]
+    b_out[pl.ds(b_slots * width, WIDE), :] = code_rows(a_slots, b_slots)
+
+
+def pack(codes, a_blocks, b_blocks):
+    a_slots, width, _ = a_blocks.shape
+    b_slots = b_blocks.shape[0]
+    return pl.pallas_call(
+        pack_body,
+        out_shape=(
+            jax.ShapeDtypeStruct((a_slots * width + WIDE, width), jnp.bfloat16),
+            jax.ShapeDtypeStruct((b_slots * width + WIDE, width), jnp.bfloat16),
+        ),
+        in_specs=[
+            pl.BlockSpec(memory_space=pltpu.SMEM),
+            pl.BlockSpec(memory_space=pltpu.VMEM),
+            pl.BlockSpec(memory_space=pltpu.VMEM),
+        ],
+        out_specs=(pl.BlockSpec(memory_space=pltpu.VMEM),) * 2,
+        compiler_params=pltpu.CompilerParams(vmem_limit_bytes=16 << 20),
+    )(codes, a_blocks, b_blocks)
+
+
+def product_body(a_slots, b_slots, place_ref, a_codes, b_codes, *refs):
+    a_refs, b_refs = refs[:4], refs[4:8]
+    keep_ref, send_ref, dense, total = refs[8:]
+    width = dense.shape[1] // CB
+    pieces, owners_a, owners_b = 2, 2, 4
+    is_middle, core, col, own_row, next_row = (place_ref[i] for i in range(5))
+    rows_of_group = 2
+
+    @pl.when(is_middle == 0)
+    def _():
+        keep_ref[...] = jnp.zeros_like(keep_ref)
+        send_ref[...] = jnp.zeros_like(send_ref)
+
+    @pl.when(is_middle == 1)
+    def _():
+        dense[...] = jnp.zeros_like(dense)
+        total[...] = jnp.zeros_like(total)
+        for source in range(4):
+            for slot in range(b_slots):
+                code = b_codes[source * b_slots + slot]
+
+                @pl.when(code >= 0)
+                def _():
+                    piece = lax.rem(slot // (b_slots // owners_b) + col, owners_b)
+                    inner = piece * KB + code // CB
+                    column = lax.rem(code, CB)
+                    dense[
+                        pl.ds(pl.multiple_of(inner * width, width), width),
+                        pl.ds(pl.multiple_of(column * width, width), width),
+                    ] = b_refs[source][pl.ds(slot * width, width), :]
+
+        for group in range(2):
+            row = (own_row, next_row)[group]
+            for source in (2 * group, 2 * group + 1):
+                for slot in range(a_slots):
+                    code = a_codes[source * a_slots + slot]
+                    live = (code >= 0).astype(jnp.int32)
+                    safe = jnp.maximum(code, 0)
+                    owner = slot // (a_slots // owners_a)
+                    piece = lax.rem(row + owner, owners_a) + owners_a * lax.rem(safe // KB, pieces)
+                    inner = piece * KB + lax.rem(safe, KB)
+                    block_row = safe // (pieces * KB)
+                    sent = lax.rem(block_row, rows_of_group) != core
+                    spot = sent.astype(jnp.int32) * 4 + group * 2 + block_row // rows_of_group
+                    spot = live * spot + (1 - live) * 8
+                    part = jnp.dot(
+                        a_refs[source][pl.ds(slot * width, width), :],
+                        dense[pl.ds(pl.multiple_of(inner * width, width), width), :],
+                        preferred_element_type=jnp.float32,
+                    )
+                    total[pl.ds(pl.multiple_of(spot * width, width), width), :] += part
+        keep_ref[...] = total[pl.ds(0, 4 * width), :]
+        send_ref[...] = total[pl.ds(4 * width, 4 * width), :]
+
+
+def product(place, a_codes, b_codes, a_packs, b_packs, a_slots, b_slots):
+    width = a_packs[0].shape[1]
+    smem, vmem = pl.BlockSpec(memory_space=pltpu.SMEM), pl.BlockSpec(memory_space=pltpu.VMEM)
+    half = jax.ShapeDtypeStruct((4 * width, CB * width), jnp.float32)
+    return pl.pallas_call(
+        functools.partial(product_body, a_slots, b_slots),
+        out_shape=(half, half),
+        in_specs=[smem] * 3 + [vmem] * 8,
+        out_specs=(vmem, vmem),
+        scratch_shapes=[
+            pltpu.VMEM((4 * KB * width, CB * width), jnp.bfloat16),
+            pltpu.VMEM((9 * width, CB * width), jnp.float32),
+        ],
+        compiler_params=pltpu.CompilerParams(vmem_limit_bytes=32 << 20),
+        cost_estimate=pl.CostEstimate(flops=6 << 30, bytes_accessed=8 << 20, transcendentals=0),
+    )(place, a_codes, b_codes, *a_packs, *b_packs)
+
+
+TO_MIDDLE = [(0, 1), (3, 2)]
+MIDDLE = [(1, 2), (2, 1)]
+
+
+def middle_shards(a_blocks, a_codes, b_blocks, b_codes):
+    a_slots, width, _ = a_blocks.shape
+    b_slots = b_blocks.shape[0]
+    row, col, layer = (lax.axis_index(name) for name in ("row", "col", "layer"))
+    chip, core = layer // 2, layer % 2
+    is_middle = ((row == 1) | (row == 2)).astype(jnp.int32)
+    next_row = jnp.where(row == 1, 0, 3)
+    place = jnp.stack([is_middle, core, col, row, next_row]).astype(jnp.int32)
+
+    a_pack, b_pack = pack(jnp.concatenate([a_codes, b_codes]), a_blocks, b_blocks)
+    b_across = lax.ppermute(b_pack, "row", MIDDLE)
+    b_end = lax.ppermute(b_pack, "row", TO_MIDDLE)
+    a_other = lax.ppermute(a_pack, "col", [(0, 1), (1, 0)])
+    a_end = lax.ppermute(a_pack, "row", TO_MIDDLE)
+    b_far = lax.ppermute(b_end, "row", MIDDLE)
+    rows_cols = [(r * 2 + c, r * 2 + 1 - c) for r in (1, 2) for c in (0, 1)]
+    a_end_other = lax.ppermute(a_end, ("row", "col"), rows_cols)
+
+    a_packs = (a_pack, a_other, a_end, a_end_other)
+    b_packs = (b_pack, b_across, b_end, b_far)
+
+    def codes_of(packs, slots):
+        first = slots * width
+        tails = [lax.slice(p, (first, 0), (first + slots, 1)) for p in packs]
+        return jnp.concatenate(tails)[:, 0].astype(jnp.int32)
+
+    keep, send = product(
+        place, codes_of(a_packs, a_slots), codes_of(b_packs, b_slots), a_packs, b_packs, a_slots, b_slots
+    )
+    cores = [(r * 4 + m, r * 4 + (m ^ 1)) for r in (1, 2) for m in range(4)]
+    summed = keep + lax.ppermute(send, ("row", "layer"), cores)
+    summed = summed.reshape(2, 2, width, CB * width)
+    near = lax.dynamic_index_in_dim(summed, chip, axis=1, keepdims=False)
+    far = lax.dynamic_index_in_dim(summed, 1 - chip, axis=1, keepdims=False)
+    ends = ((1, 0), (2, 3))
+    across = [(s * 4 + m, e * 4 + (m ^ 2)) for s, e in ends for m in range(4)]
+    along = [(s * 4 + m, e * 4 + m) for s, e in ends for m in range(4)]
+    chips = [(r * 4 + m, r * 4 + (m ^ 2)) for r in (1, 2) for m in range(4)]
+    out = near[0]
+    out = out + lax.ppermute(far[1], ("row", "layer"), across)
+    out = out + lax.ppermute(far[0], ("row", "layer"), chips)
+    out = out + lax.ppermute(near[1], ("row", "layer"), along)
+    return out.astype(jnp.bfloat16)
+
+
 def solution(mesh):
     placed = (
         P(("row", "col", "layer"), None, None),
@@ -100,6 +271,7 @@
         P(("row", "col", "layer"), None, None),
         P(("row", "col", "layer")),
     )
+    body = middle_shards if middle_plan(mesh.shape) else shards
     return jax.shard_map(
-        shards, mesh=mesh, in_specs=placed, out_specs=P(("row", "layer"), "col"), check_vma=False
-    )
+        body, mesh=mesh, in_specs=placed, out_specs=P(("row", "layer"), "col"), check_vma=False
+    )

time: 130 us -> 66.8 us (0.51)
  blocking collectives: 19.2 us -> 0 us
  between operations: 13.5 us -> 0.2 us
  waiting for transfers between devices: 53.2 us -> 40.3 us
  starting transfers between devices: 24.5 us -> 13.9 us
  matrix products: 7.73 us -> 0 us
  Pallas kernels: 0 us -> 2.28 us
  other arithmetic: 3.35 us -> 1.86 us
    reduce_scatter x1 -> x0, waiting for transfers between devices: 26.3 us -> none  [shards(): lax.psum_scatter(accumulated, 'layer', scatter_dimension=0, tiled=True)]
    ppermute x12 -> x10, waiting for transfers between devices: 15.4 us -> 40.3 us  [the longest x1 22.7 us: middle_shards(): out = out + lax.ppermute(far[1], ('row', 'layer'), across)]
    all_to_all x2 -> x0, blocking collectives: 19.2 us -> none  [the longest x1 10.6 us: shards(): lax.all_to_all(b_codes, 'row', split_axis=0, concat_axis=0, tiled=True)]
    all_to_all x2 -> x0, waiting for transfers between devices: 11.5 us -> none  [the longest x1 8.58 us: shards(): lax.all_to_all(b_blocks, 'row', split_axis=0, concat_axis=0, tiled=True)]
    dot_general x12 -> x0, matrix products: 7.73 us -> none  [the longest x4 4.81 us: multiply(): jnp.dot(left_tile, right_tile, preferred_element_type=jnp.float32)]
    all_to_all x2 -> x0, starting transfers between devices: 7.71 us -> none  [the longest x1 4.23 us: shards(): lax.all_to_all(a_codes, 'col', split_axis=0, concat_axis=0, tiled=True)]
    unnamed x2 -> x16, local copies, waits for them, and re-layouts: 0.52 us -> 6.96 us
    convert_element_type x5 -> x0, local copies, waits for them, and re-layouts: 4.03 us -> none  [the longest x4 2.14 us: dense_right(): dense_tile.astype(jnp.bfloat16).reshape(KB * block_width, CB * block_width)]
  transfers between devices with their start and end apart: 15 -> 10, of which waited for: 7 -> 5; matrix products, arithmetic and copies ran while one was open for 7% -> 1% of each run, Pallas kernels for 0% -> 0%
where the time goes in v1:
time: 66.8 us; the launch traced here: 66.3 us
  waiting for transfers between devices  40.3 us (60%)
  starting transfers between devices  13.9 us (21%)
  local copies, waits for them, and re-layouts  7.88 us (12%)
  Pallas kernels  2.28 us (3%)
  other arithmetic  1.86 us (3%)
    ppermute x1, waiting for transfers between devices, middle_shards(): out = out + lax.ppermute(far[1], ('row', 'layer'), across)  22.7 us
    ppermute x1, waiting for transfers between devices, middle_shards(): b_end = lax.ppermute(b_pack, 'row', TO_MIDDLE)  10.3 us
    unnamed x16, local copies, waits for them, and re-layouts  6.96 us
    ppermute x1, starting transfers between devices, middle_shards(): b_end = lax.ppermute(b_pack, 'row', TO_MIDDLE)  4.96 us
    ppermute x1, waiting for transfers between devices, middle_shards(): out = out + lax.ppermute(near[1], ('row', 'layer'), along)  4.09 us
    ppermute x1, waiting for transfers between devices, middle_shards(): a_end = lax.ppermute(a_pack, 'row', TO_MIDDLE)  2.28 us
    pallas_call x1, Pallas kernels, product(): pl.pallas_call(functools.partial(product_body, a_slots, b_slots), out_sha...  1.69 us
    ppermute x1, starting transfers between devices, middle_shards(): a_other = lax.ppermute(a_pack, 'col', [(0, 1), (1, 0)])  1.58 us
  transfers between devices with their start and end apart: 10, of which 5 were waited for; matrix products, arithmetic and copies ran while one was open for 1% of the time, Pallas kernels for 0%

profile of v1, /device:TPU:0, one launch (start us, length us, event | category | flops | bytes accessed | tf_op | source)
XLA Modules:
  0.0 66.3 jit_solution(11837628202293968696)
XLA Ops:
  0.0 0.7 %pad_add_fusion.codes_ref = s32[24]{0:T(128)S(1)} fusion(s32[16]{0:T(128)} %param.7, s32[8]{0:T(128)} %param.5), kind=kLoop, calls=%fused_computation.8 | loop fusion | flops 24 | bytes 192 | tf_op jit(solution)/shard_map/concatenate | solution.py:231
  0.7 1.0 %copy-done = bf16[16,128,128]{2,1,0:T(8,128)(2,1)S(1)} copy-done((bf16[16,128,128]{2,1,0:T(8,128)(2,1)S(1)}, bf16[16,128,128]{2,1,0:T(8,128)(2,1)}, u32[]{:S(2)}) %copy-start) | copy-done | bytes 524312
  1.8 0.9 %copy-done.1 = bf16[8,128,128]{2,1,0:T(8,128)(2,1)S(1)} copy-done((bf16[8,128,128]{2,1,0:T(8,128)(2,1)S(1)}, bf16[8,128,128]{2,1,0:T(8,128)(2,1)}, u32[]{:S(2)}) %copy-start.1) | copy-done | bytes 262168
  2.7 0.6 shard_map.46
  3.3 5.0 %collective-permute-start.4 = (bf16[2064,128]{1,0:T(8,128)(2,1)S(1)}, bf16[2064,128]{1,0:T(8,128)(2,1)S(1)}, u32[]{:S(2)}, u32[]{:S(2)}) collective-permute-start(bf16[2064,128]{1,0:T(8,128)(2,1)S(1)} %get-tuple-element.10.refs_4_), channel_id=1, source_target_pairs={{0,8},{24,16},{1,9},{25,17},{2,10},{26,18},{3,11},{27,19},{4,12},{... | collective-permute-start | bytes 1585160 | tf_op jit(solution)/shard_map/ppermute | solution.py:233
  8.3 1.3 %collective-permute-start.1 = (bf16[1040,128]{1,0:T(8,128)(2,1)S(1)}, bf16[1040,128]{1,0:T(8,128)(2,1)S(1)}, u32[]{:S(2)}, u32[]{:S(2)}) collective-permute-start(bf16[1040,128]{1,0:T(8,128)(2,1)S(1)} %get-tuple-element.9.refs_0_), channel_id=1, source_target_pairs={{0,8},{24,16},{1,9},{25,17},{2,10},{26,18},{3,11},{27,19},{4,12},{... | collective-permute-start | bytes 798728 | tf_op jit(solution)/shard_map/ppermute | solution.py:235
  9.6 0.7 %collective-permute-start.3 = (bf16[2064,128]{1,0:T(8,128)(2,1)S(1)}, bf16[2064,128]{1,0:T(8,128)(2,1)S(1)}, u32[]{:S(2)}, u32[]{:S(2)}) collective-permute-start(bf16[2064,128]{1,0:T(8,128)(2,1)S(1)} %get-tuple-element.10.refs_4_), channel_id=1, source_target_pairs={{8,16},{16,8},{9,17},{17,9},{10,18},{18,10},{11,19},{19,11},{12,20... | collective-permute-start | bytes 1585160 | tf_op jit(solution)/shard_map/ppermute | solution.py:232
  10.3 10.3 %collective-permute-done.4.refs_6_ = bf16[2064,128]{1,0:T(8,128)(2,1)S(1)} collective-permute-done((bf16[2064,128]{1,0:T(8,128)(2,1)S(1)}, bf16[2064,128]{1,0:T(8,128)(2,1)S(1)}, u32[]{:S(2)}, u32[]{:S(2)}) %collective-permute-start.4) | collective-permute-done | bytes 528416 | tf_op jit(solution)/shard_map/ppermute | solution.py:233
  20.7 0.7 %collective-permute-start.5 = (bf16[2064,128]{1,0:T(8,128)(2,1)S(1)}, bf16[2064,128]{1,0:T(8,128)(2,1)S(1)}, u32[]{:S(2)}, u32[]{:S(2)}) collective-permute-start(bf16[2064,128]{1,0:T(8,128)(2,1)S(1)} %collective-permute-done.4.refs_6_), channel_id=1, source_target_pairs={{8,16},{16,8},{9,17},{17,9},{10,18},{18,10},{11,19},{19,11},{12,20... | collective-permute-start | bytes 1585160 | tf_op jit(solution)/shard_map/ppermute | solution.py:236
  21.4 1.6 %collective-permute-start = (bf16[1040,128]{1,0:T(8,128)(2,1)S(1)}, bf16[1040,128]{1,0:T(8,128)(2,1)S(1)}, u32[]{:S(2)}, u32[]{:S(2)}) collective-permute-start(bf16[1040,128]{1,0:T(8,128)(2,1)S(1)} %get-tuple-element.9.refs_0_), channel_id=1, source_target_pairs={{0,4},{4,0},{1,5},{5,1},{2,6},{6,2},{3,7},{7,3},{8,12},{12,8},{9,1... | collective-permute-start | bytes 798728 | tf_op jit(solution)/shard_map/ppermute | solution.py:234
  23.0 2.3 %collective-permute-done.1.refs_2_ = bf16[1040,128]{1,0:T(8,128)(2,1)S(1)} collective-permute-done((bf16[1040,128]{1,0:T(8,128)(2,1)S(1)}, bf16[1040,128]{1,0:T(8,128)(2,1)S(1)}, u32[]{:S(2)}, u32[]{:S(2)}) %collective-permute-start.1) | collective-permute-done | bytes 266272 | tf_op jit(solution)/shard_map/ppermute | solution.py:235
  25.2 0.7 %collective-permute-start.2 = (bf16[1040,128]{1,0:T(8,128)(2,1)S(1)}, bf16[1040,128]{1,0:T(8,128)(2,1)S(1)}, u32[]{:S(2)}, u32[]{:S(2)}) collective-permute-start(bf16[1040,128]{1,0:T(8,128)(2,1)S(1)} %collective-permute-done.1.refs_2_), channel_id=1, source_target_pairs={{8,12},{12,8},{16,20},{20,16},{9,13},{13,9},{17,21},{21,17},{10,14... | collective-permute-start | bytes 798728 | tf_op jit(solution)/shard_map/ppermute | solution.py:238
  26.0 0.1 copy.5
  26.2 0.7 %copy-done.2 = bf16[1040,128]{1,0:T(8,128)(2,1)} copy-done((bf16[1040,128]{1,0:T(8,128)(2,1)}, bf16[1040,128]{1,0:T(8,128)(2,1)S(1)}, u32[]{:S(2)}) %copy-start.2) | copy-done | bytes 266264
  27.0 0.8 %collective-permute-done.refs_1_ = bf16[1040,128]{1,0:T(8,128)(2,1)S(1)} collective-permute-done((bf16[1040,128]{1,0:T(8,128)(2,1)S(1)}, bf16[1040,128]{1,0:T(8,128)(2,1)S(1)}, u32[]{:S(2)}, u32[]{:S(2)}) %collective-permute-start) | collective-permute-done | bytes 266272 | tf_op jit(solution)/shard_map/ppermute | solution.py:234
  27.9 0.7 %copy-done.4 = bf16[1040,128]{1,0:T(8,128)(2,1)} copy-done((bf16[1040,128]{1,0:T(8,128)(2,1)}, bf16[1040,128]{1,0:T(8,128)(2,1)S(1)}, u32[]{:S(2)}) %copy-start.4) | copy-done | bytes 266264
  28.6 0.1 copy.11
  28.8 0.1 copy.10
  28.9 0.7 %copy-done.6 = bf16[1040,128]{1,0:T(8,128)(2,1)} copy-done((bf16[1040,128]{1,0:T(8,128)(2,1)}, bf16[1040,128]{1,0:T(8,128)(2,1)S(1)}, u32[]{:S(2)}) %copy-start.6) | copy-done | bytes 266264
  29.7 0.1 copy.12
  29.9 1.0 %copy-done.3 = bf16[1040,128]{1,0:T(8,128)(2,1)S(1)} copy-done((bf16[1040,128]{1,0:T(8,128)(2,1)S(1)}, bf16[1040,128]{1,0:T(8,128)(2,1)}, u32[]{:S(2)}) %copy-start.3) | copy-done | bytes 266264
  30.9 0.9 %copy-done.5 = bf16[1040,128]{1,0:T(8,128)(2,1)S(1)} copy-done((bf16[1040,128]{1,0:T(8,128)(2,1)S(1)}, bf16[1040,128]{1,0:T(8,128)(2,1)}, u32[]{:S(2)}) %copy-start.5) | copy-done | bytes 266264
  31.8 0.9 %copy-done.7 = bf16[1040,128]{1,0:T(8,128)(2,1)S(1)} copy-done((bf16[1040,128]{1,0:T(8,128)(2,1)S(1)}, bf16[1040,128]{1,0:T(8,128)(2,1)}, u32[]{:S(2)}) %copy-start.7) | copy-done | bytes 266264
  32.8 1.7 %shard_map.47 = (f32[512,512]{1,0:T(8,128)S(1)}, f32[512,512]{1,0:T(8,128)}) custom-call(s32[5]{0:T(128)S(1)} %stack.27.place_ref, s32[32]{0:T(128)S(1)} %fusion.4.a_codes, s32[64]{0:T(128)S(1)} %fusion.5.b_codes, bf16[1040,128]{1,0:T(8,128)(2,1)S(1)} %get-tuple-element.9.refs_0_, bf16[1040,128]{1,0:T(8,128)(2,1)S(1)} %copy-done.5, ...), custom_call_target="tpu_custom_call" | custom-call | flops 6442450944 | bytes 8388608 | tf_op jit(solution)/shard_map/pallas_call | solution.py:204
  34.5 0.7 %collective-permute-start.6 = (f32[512,512]{1,0:T(8,128)}, f32[512,512]{1,0:T(8,128)S(1)}, u32[]{:S(2)}, u32[]{:S(2)}) collective-permute-start(f32[512,512]{1,0:T(8,128)} %get-tuple-element.12), channel_id=1, source_target_pairs={{8,9},{9,8},{10,11},{11,10},{16,17},{17,16},{18,19},{19,18},{12,13... | collective-permute-start | bytes 3145736 | tf_op jit(solution)/shard_map/ppermute | solution.py:252
  35.2 0.2 add.26
  35.5 1.3 %collective-permute-start.7 = (f32[128,512]{1,0:T(8,128)S(1)}, f32[128,512]{1,0:T(8,128)S(1)}, u32[]{:S(2)}, u32[]{:S(2)}) collective-permute-start(f32[128,512]{1,0:T(8,128)S(1)} %get-tuple-element.13), channel_id=1, source_target_pairs={{8,2},{9,3},{10,0},{11,1},{16,26},{17,27},{18,24},{19,25},{12,6},{... | collective-permute-start | bytes 786440 | tf_op jit(solution)/shard_map/ppermute | solution.py:261
  36.8 0.7 %collective-permute-start.8 = (f32[128,512]{1,0:T(8,128)S(1)}, f32[128,512]{1,0:T(8,128)S(1)}, u32[]{:S(2)}, u32[]{:S(2)}) collective-permute-start(f32[128,512]{1,0:T(8,128)S(1)} %get-tuple-element.14), channel_id=1, source_target_pairs={{8,10},{9,11},{10,8},{11,9},{16,18},{17,19},{18,16},{19,17},{12,14... | collective-permute-start | bytes 786440 | tf_op jit(solution)/shard_map/ppermute | solution.py:262
  37.5 1.3 %collective-permute-start.9 = (f32[128,512]{1,0:T(8,128)S(1)}, f32[128,512]{1,0:T(8,128)S(1)}, u32[]{:S(2)}, u32[]{:S(2)}) collective-permute-start(f32[128,512]{1,0:T(8,128)S(1)} %get-tuple-element.15), channel_id=1, source_target_pairs={{8,0},{9,1},{10,2},{11,3},{16,24},{17,25},{18,26},{19,27},{12,4},{... | collective-permute-start | bytes 786440 | tf_op jit(solution)/shard_map/ppermute | solution.py:263
  38.8 22.7 %collective-permute-done.7 = f32[128,512]{1,0:T(8,128)S(1)} collective-permute-done((f32[128,512]{1,0:T(8,128)S(1)}, f32[128,512]{1,0:T(8,128)S(1)}, u32[]{:S(2)}, u32[]{:S(2)}) %collective-permute-start.7) | collective-permute-done | bytes 262176 | tf_op jit(solution)/shard_map/ppermute | solution.py:261
  61.5 4.1 %collective-permute-done.9 = f32[128,512]{1,0:T(8,128)S(1)} collective-permute-done((f32[128,512]{1,0:T(8,128)S(1)}, f32[128,512]{1,0:T(8,128)S(1)}, u32[]{:S(2)}, u32[]{:S(2)}) %collective-permute-start.9) | collective-permute-done | bytes 262176 | tf_op jit(solution)/shard_map/ppermute | solution.py:263
  65.6 0.7 %fusion.3 = bf16[128,512]{1,0:T(8,128)(2,1)} fusion(f32[128,512]{1,0:T(8,128)S(1)} %collective-permute-done.9, f32[128,512]{1,0:T(8,128)S(1)} %collective-permute-done.8, f32[128,512]{1,0:T(8,128)S(1)} %collective-permute-done.7, f32[2,2,128,512]{3,2,1,0:T(8,128)S(1)} %bitcast.33, s32[]{:T(128)S(6)} %select_n.25), kind=kLoop, calls=%fused_computation.7 | loop fusion | flops 262144 | bytes 1179652 | tf_op jit(solution)/shard_map/convert_element_type | solution.py:264
  (29 shorter events, 0.7 us)
Async XLA Ops:
  0.7 1.0 %copy-start = (bf16[16,128,128]{2,1,0:T(8,128)(2,1)S(1)}, bf16[16,128,128]{2,1,0:T(8,128)(2,1)}, u32[]{:S(2)}) copy-start(bf16[16,128,128]{2,1,0:T(8,128)(2,1)} %b_ref.1) | copy-start | bytes 1572868
  1.8 0.9 %copy-start.1 = (bf16[8,128,128]{2,1,0:T(8,128)(2,1)S(1)}, bf16[8,128,128]{2,1,0:T(8,128)(2,1)}, u32[]{:S(2)}) copy-start(bf16[8,128,128]{2,1,0:T(8,128)(2,1)} %a_ref.1) | copy-start | bytes 786436
  3.3 17.3 %collective-permute-start.4 = (bf16[2064,128]{1,0:T(8,128)(2,1)S(1)}, bf16[2064,128]{1,0:T(8,128)(2,1)S(1)}, u32[]{:S(2)}, u32[]{:S(2)}) collective-permute-start(bf16[2064,128]{1,0:T(8,128)(2,1)S(1)} %get-tuple-element.10.refs_4_), channel_id=1, source_target_pairs={{0,8},{24,16},{1,9},{25,17},{2,10},{26,18},{3,11},{27,19},{4,12},{... | collective-permute-start | bytes 1585160 | tf_op jit(solution)/shard_map/ppermute | solution.py:233
  8.3 16.9 %collective-permute-start.1 = (bf16[1040,128]{1,0:T(8,128)(2,1)S(1)}, bf16[1040,128]{1,0:T(8,128)(2,1)S(1)}, u32[]{:S(2)}, u32[]{:S(2)}) collective-permute-start(bf16[1040,128]{1,0:T(8,128)(2,1)S(1)} %get-tuple-element.9.refs_0_), channel_id=1, source_target_pairs={{0,8},{24,16},{1,9},{25,17},{2,10},{26,18},{3,11},{27,19},{4,12},{... | collective-permute-start | bytes 798728 | tf_op jit(solution)/shard_map/ppermute | solution.py:235
  9.6 19.1 %collective-permute-start.3 = (bf16[2064,128]{1,0:T(8,128)(2,1)S(1)}, bf16[2064,128]{1,0:T(8,128)(2,1)S(1)}, u32[]{:S(2)}, u32[]{:S(2)}) collective-permute-start(bf16[2064,128]{1,0:T(8,128)(2,1)S(1)} %get-tuple-element.10.refs_4_), channel_id=1, source_target_pairs={{8,16},{16,8},{9,17},{17,9},{10,18},{18,10},{11,19},{19,11},{12,20... | collective-permute-start | bytes 1585160 | tf_op jit(solution)/shard_map/ppermute | solution.py:232
  20.7 9.1 %collective-permute-start.5 = (bf16[2064,128]{1,0:T(8,128)(2,1)S(1)}, bf16[2064,128]{1,0:T(8,128)(2,1)S(1)}, u32[]{:S(2)}, u32[]{:S(2)}) collective-permute-start(bf16[2064,128]{1,0:T(8,128)(2,1)S(1)} %collective-permute-done.4.refs_6_), channel_id=1, source_target_pairs={{8,16},{16,8},{9,17},{17,9},{10,18},{18,10},{11,19},{19,11},{12,20... | collective-permute-start | bytes 1585160 | tf_op jit(solution)/shard_map/ppermute | solution.py:236
  21.4 6.5 %collective-permute-start = (bf16[1040,128]{1,0:T(8,128)(2,1)S(1)}, bf16[1040,128]{1,0:T(8,128)(2,1)S(1)}, u32[]{:S(2)}, u32[]{:S(2)}) collective-permute-start(bf16[1040,128]{1,0:T(8,128)(2,1)S(1)} %get-tuple-element.9.refs_0_), channel_id=1, source_target_pairs={{0,4},{4,0},{1,5},{5,1},{2,6},{6,2},{3,7},{7,3},{8,12},{12,8},{9,1... | collective-permute-start | bytes 798728 | tf_op jit(solution)/shard_map/ppermute | solution.py:234
  25.2 3.6 %collective-permute-start.2 = (bf16[1040,128]{1,0:T(8,128)(2,1)S(1)}, bf16[1040,128]{1,0:T(8,128)(2,1)S(1)}, u32[]{:S(2)}, u32[]{:S(2)}) collective-permute-start(bf16[1040,128]{1,0:T(8,128)(2,1)S(1)} %collective-permute-done.1.refs_2_), channel_id=1, source_target_pairs={{8,12},{12,8},{16,20},{20,16},{9,13},{13,9},{17,21},{21,17},{10,14... | collective-permute-start | bytes 798728 | tf_op jit(solution)/shard_map/ppermute | solution.py:238
  26.2 0.7 %copy-start.2 = (bf16[1040,128]{1,0:T(8,128)(2,1)}, bf16[1040,128]{1,0:T(8,128)(2,1)S(1)}, u32[]{:S(2)}) copy-start(bf16[1040,128]{1,0:T(8,128)(2,1)S(1)} %collective-permute-done.1.refs_2_) | copy-start | bytes 798724
  27.9 0.7 %copy-start.4 = (bf16[1040,128]{1,0:T(8,128)(2,1)}, bf16[1040,128]{1,0:T(8,128)(2,1)S(1)}, u32[]{:S(2)}) copy-start(bf16[1040,128]{1,0:T(8,128)(2,1)S(1)} %collective-permute-done.refs_1_) | copy-start | bytes 798724
  28.9 0.7 %copy-start.6 = (bf16[1040,128]{1,0:T(8,128)(2,1)}, bf16[1040,128]{1,0:T(8,128)(2,1)S(1)}, u32[]{:S(2)}) copy-start(bf16[1040,128]{1,0:T(8,128)(2,1)S(1)} %collective-permute-done.2.refs_3_) | copy-start | bytes 798724
  29.9 1.0 %copy-start.3 = (bf16[1040,128]{1,0:T(8,128)(2,1)S(1)}, bf16[1040,128]{1,0:T(8,128)(2,1)}, u32[]{:S(2)}) copy-start(bf16[1040,128]{1,0:T(8,128)(2,1)} %copy-done.2) | copy-start | bytes 798724
  30.9 1.0 %copy-start.5 = (bf16[1040,128]{1,0:T(8,128)(2,1)S(1)}, bf16[1040,128]{1,0:T(8,128)(2,1)}, u32[]{:S(2)}) copy-start(bf16[1040,128]{1,0:T(8,128)(2,1)} %copy-done.4) | copy-start | bytes 798724
  31.8 1.0 %copy-start.7 = (bf16[1040,128]{1,0:T(8,128)(2,1)S(1)}, bf16[1040,128]{1,0:T(8,128)(2,1)}, u32[]{:S(2)}) copy-start(bf16[1040,128]{1,0:T(8,128)(2,1)} %copy-done.6) | copy-start | bytes 798724
  34.5 0.8 %collective-permute-start.6 = (f32[512,512]{1,0:T(8,128)}, f32[512,512]{1,0:T(8,128)S(1)}, u32[]{:S(2)}, u32[]{:S(2)}) collective-permute-start(f32[512,512]{1,0:T(8,128)} %get-tuple-element.12), channel_id=1, source_target_pairs={{8,9},{9,8},{10,11},{11,10},{16,17},{17,16},{18,19},{19,18},{12,13... | collective-permute-start | bytes 3145736 | tf_op jit(solution)/shard_map/ppermute | solution.py:252
  35.5 26.0 %collective-permute-start.7 = (f32[128,512]{1,0:T(8,128)S(1)}, f32[128,512]{1,0:T(8,128)S(1)}, u32[]{:S(2)}, u32[]{:S(2)}) collective-permute-start(f32[128,512]{1,0:T(8,128)S(1)} %get-tuple-element.13), channel_id=1, source_target_pairs={{8,2},{9,3},{10,0},{11,1},{16,26},{17,27},{18,24},{19,25},{12,6},{... | collective-permute-start | bytes 786440 | tf_op jit(solution)/shard_map/ppermute | solution.py:261
  36.8 24.7 %collective-permute-start.8 = (f32[128,512]{1,0:T(8,128)S(1)}, f32[128,512]{1,0:T(8,128)S(1)}, u32[]{:S(2)}, u32[]{:S(2)}) collective-permute-start(f32[128,512]{1,0:T(8,128)S(1)} %get-tuple-element.14), channel_id=1, source_target_pairs={{8,10},{9,11},{10,8},{11,9},{16,18},{17,19},{18,16},{19,17},{12,14... | collective-permute-start | bytes 786440 | tf_op jit(solution)/shard_map/ppermute | solution.py:262
  37.5 28.1 %collective-permute-start.9 = (f32[128,512]{1,0:T(8,128)S(1)}, f32[128,512]{1,0:T(8,128)S(1)}, u32[]{:S(2)}, u32[]{:S(2)}) collective-permute-start(f32[128,512]{1,0:T(8,128)S(1)} %get-tuple-element.15), channel_id=1, source_target_pairs={{8,0},{9,1},{10,2},{11,3},{16,24},{17,25},{18,26},{19,27},{12,4},{... | collective-permute-start | bytes 786440 | tf_op jit(solution)/shard_map/ppermute | solution.py:263

commit v2 on v0

--- a/solution.py
+++ b/solution.py
@@ -1,6 +1,10 @@
+import functools
+
 import jax
 import jax.numpy as jnp
 from jax import lax
+from jax.experimental import pallas as pl
+from jax.experimental.pallas import tpu as pltpu
 from jax.sharding import PartitionSpec as P
 
 RB = 4
@@ -93,6 +97,278 @@
     return reduced.astype(jnp.bfloat16)
 
 
+CODE_ROWS = 16
+
+
+def middle_plan(mesh_shape):
+    return (mesh_shape["row"], mesh_shape["col"], mesh_shape["layer"]) == (4, 2, 4)
+
+
+def spaces(*names):
+    kinds = {"s": pltpu.SMEM, "v": pltpu.VMEM, "h": pltpu.HBM}
+    return [pl.BlockSpec(memory_space=kinds[name]) for name in names]
+
+
+def pack_body(a_codes, b_codes, a_ref, b_ref, a_out, b_out, first_out, second_out, sems):
+    a_rows, b_rows = a_ref.shape[0], b_ref.shape[0]
+    width = a_ref.shape[1]
+    half = b_rows // 2
+    copies = [
+        pltpu.make_async_copy(b_ref.at[pl.ds(0, half)], first_out.at[pl.ds(0, half)], sems.at[0]),
+        pltpu.make_async_copy(b_ref, b_out.at[pl.ds(0, b_rows)], sems.at[1]),
+        pltpu.make_async_copy(b_ref.at[pl.ds(half, half)], second_out, sems.at[2]),
+        pltpu.make_async_copy(a_ref, a_out.at[pl.ds(0, a_rows)], sems.at[3]),
+    ]
+    for copy in copies:
+        copy.start()
+
+    def code_rows(codes_ref):
+        lanes = lax.broadcasted_iota(jnp.int32, (CODE_ROWS, width), 1)
+        values = jnp.full((CODE_ROWS, width), -1, jnp.int32)
+        for slot in range(codes_ref.shape[0]):
+            values = jnp.where(lanes == slot, codes_ref[slot], values)
+        return values.astype(jnp.float32).astype(jnp.bfloat16)
+
+    a_out[pl.ds(a_rows, CODE_ROWS), :] = code_rows(a_codes)
+    b_tail = code_rows(b_codes)
+    b_out[pl.ds(b_rows, CODE_ROWS), :] = b_tail
+    first_out[pl.ds(half, CODE_ROWS), :] = b_tail
+    for copy in copies:
+        copy.wait()
+
+
+def pack(a_codes, b_codes, a_blocks, b_blocks):
+    width = a_blocks.shape[1]
+    a_flat = a_blocks.reshape(-1, width)
+    b_flat = b_blocks.reshape(-1, width)
+    a_rows, b_rows = a_flat.shape[0], b_flat.shape[0]
+    sizes = (a_rows + CODE_ROWS, b_rows + CODE_ROWS, b_rows // 2 + CODE_ROWS, b_rows // 2)
+    return pl.pallas_call(
+        pack_body,
+        out_shape=tuple(jax.ShapeDtypeStruct((rows, width), jnp.bfloat16) for rows in sizes),
+        in_specs=spaces("s", "s", "h", "h"),
+        out_specs=tuple(spaces("v", "v", "v", "v")),
+        scratch_shapes=[pltpu.SemaphoreType.DMA((4,))],
+        compiler_params=pltpu.CompilerParams(vmem_limit_bytes=8 << 20),
+    )(*(pltpu.with_memory_space_constraint(x, pltpu.HBM) for x in (a_codes, b_codes, a_flat, b_flat)))
+
+
+def fetch_codes(packs, staged, codes, sem):
+    for index, pack_ref in enumerate(packs):
+        tail = pack_ref[pl.ds(pack_ref.shape[0] - CODE_ROWS, CODE_ROWS), :]
+        staged[pl.ds(index, 1), :] = tail.astype(jnp.float32).astype(jnp.int32)[:1]
+    return pltpu.make_async_copy(staged, codes, sem)
+
+
+def code_scratch():
+    return [
+        pltpu.VMEM((8, 128), jnp.int32),
+        pltpu.SMEM((8, 128), jnp.int32),
+        pltpu.SemaphoreType.DMA(()),
+    ]
+
+
+def in_middle():
+    row = lax.axis_index("row")
+    return jnp.logical_or(row == 1, row == 2)
+
+
+def put_blocks(dense, source, codes, line, first_slot, count, slots, col):
+    width = source.shape[1]
+    owners = 4
+    for index in range(count):
+        code = codes[line, first_slot + index]
+
+        @pl.when(code >= 0)
+        def _():
+            piece = lax.rem((first_slot + index) // (slots // owners) + col, owners)
+            inner = piece * KB + code // CB
+            column = lax.rem(code, CB)
+            dense[
+                pl.ds(pl.multiple_of(inner * width, width), width),
+                pl.ds(pl.multiple_of(column * width, width), width),
+            ] = source[pl.ds(index * width, width), :]
+
+
+def early_body(slots, own, across, first, second, far, other, dense, staged, codes, sem):
+    del other
+    half = slots // 2
+
+    @pl.when(in_middle())
+    def _():
+        col = lax.axis_index("col")
+        copy = fetch_codes((own, across, first, far), staged, codes, sem)
+        copy.start()
+        dense[...] = jnp.zeros_like(dense)
+        copy.wait()
+        put_blocks(dense, own, codes, 0, 0, slots, slots, col)
+        put_blocks(dense, across, codes, 1, 0, slots, slots, col)
+        put_blocks(dense, first, codes, 2, 0, half, slots, col)
+        put_blocks(dense, second, codes, 2, half, half, slots, col)
+        put_blocks(dense, far, codes, 3, 0, half, slots, col)
+
+
+def early(own, across, first, second, far, other, slots):
+    width = own.shape[1]
+    return pl.pallas_call(
+        functools.partial(early_body, slots),
+        out_shape=jax.ShapeDtypeStruct((4 * KB * width, CB * width), jnp.bfloat16),
+        in_specs=spaces("v", "v", "v", "v", "v", "h"),
+        out_specs=spaces("v")[0],
+        scratch_shapes=code_scratch(),
+        compiler_params=pltpu.CompilerParams(vmem_limit_bytes=12 << 20),
+    )(own, across, first, second, far, other)
+
+
+def multiply_group(dense, total, packs, codes, slots, row):
+    width = packs[0].shape[1]
+    pieces, owners = 2, 2
+    core = lax.rem(lax.axis_index("layer"), 2)
+    total[...] = jnp.zeros_like(total)
+    for source in range(2):
+        for slot in range(slots):
+            code = codes[source, slot]
+            live = (code >= 0).astype(jnp.int32)
+            safe = jnp.maximum(code, 0)
+            owner = slot // (slots // owners)
+            piece = lax.rem(row + owner, owners) + owners * lax.rem(safe // KB, pieces)
+            inner = piece * KB + lax.rem(safe, KB)
+            block_row = safe // (pieces * KB)
+            sent = (lax.rem(block_row, 2) != core).astype(jnp.int32)
+            spot = live * (sent * 2 + block_row // 2) + (1 - live) * 4
+            part = jnp.dot(
+                packs[source][pl.ds(slot * width, width), :],
+                dense[pl.ds(pl.multiple_of(inner * width, width), width), :],
+                preferred_element_type=jnp.float32,
+            )
+            total[pl.ds(pl.multiple_of(spot * width, width), width), :] += part
+
+
+def end_body(a_slots, slots, packs_0, packs_1, dense_in, first, second,
+             dense, keep, send, total, staged, codes, sem):
+    half = slots // 2
+    rows = keep.shape[0]
+    del dense_in
+
+    @pl.when(in_middle())
+    def _():
+        copy = fetch_codes((packs_0, packs_1, first), staged, codes, sem)
+        copy.start()
+        copy.wait()
+        put_blocks(dense, second, codes, 2, half, half, slots, lax.axis_index("col"))
+        row = jnp.where(lax.axis_index("row") == 1, 0, 3)
+        multiply_group(dense, total, (packs_0, packs_1), codes, a_slots, row)
+        keep[...] = total[pl.ds(0, rows), :]
+        send[...] = total[pl.ds(rows, rows), :]
+
+
+def own_body(a_slots, packs_0, packs_1, dense, keep, send, total, staged, codes, sem):
+    rows = keep.shape[0]
+
+    @pl.when(jnp.logical_not(in_middle()))
+    def _():
+        keep[...] = jnp.zeros_like(keep)
+
+    @pl.when(in_middle())
+    def _():
+        copy = fetch_codes((packs_0, packs_1), staged, codes, sem)
+        copy.start()
+        copy.wait()
+        multiply_group(dense, total, (packs_0, packs_1), codes, a_slots, lax.axis_index("row"))
+        keep[...] = total[pl.ds(0, rows), :]
+        send[...] = total[pl.ds(rows, rows), :]
+
+
+def end_product(packs, dense, first, second, a_slots, slots):
+    width = packs[0].shape[1]
+    half = jax.ShapeDtypeStruct((2 * width, CB * width), jnp.float32)
+    return pl.pallas_call(
+        functools.partial(end_body, a_slots, slots),
+        out_shape=(jax.ShapeDtypeStruct(dense.shape, dense.dtype), half, half),
+        in_specs=spaces("v", "v", "v", "v", "v"),
+        out_specs=tuple(spaces("v", "v", "v")),
+        scratch_shapes=[pltpu.VMEM((5 * width, CB * width), jnp.float32)] + code_scratch(),
+        input_output_aliases={2: 0},
+        compiler_params=pltpu.CompilerParams(vmem_limit_bytes=16 << 20),
+    )(*packs, dense, first, second)
+
+
+def own_product(packs, dense, a_slots):
+    width = packs[0].shape[1]
+    half = jax.ShapeDtypeStruct((2 * width, CB * width), jnp.float32)
+    return pl.pallas_call(
+        functools.partial(own_body, a_slots),
+        out_shape=(half, half),
+        in_specs=spaces("v", "v", "v"),
+        out_specs=tuple(spaces("v", "v")),
+        scratch_shapes=[pltpu.VMEM((5 * width, CB * width), jnp.float32)] + code_scratch(),
+        compiler_params=pltpu.CompilerParams(vmem_limit_bytes=16 << 20),
+    )(*packs, dense)
+
+
+def fold_body(keep, got, near, far):
+    rows = near.shape[0]
+    chip = lax.axis_index("layer") // 2
+    for out, index in ((near, chip), (far, 1 - chip)):
+        block = pl.ds(pl.multiple_of(index * rows, rows), rows)
+        out[...] = keep[block, :] + got[block, :]
+
+
+def fold(keep, got):
+    rows, width = keep.shape
+    half = jax.ShapeDtypeStruct((rows // 2, width), keep.dtype)
+    return pl.pallas_call(
+        fold_body,
+        out_shape=(half, half),
+        in_specs=spaces("v", "v"),
+        out_specs=tuple(spaces("v", "v")),
+        compiler_params=pltpu.CompilerParams(vmem_limit_bytes=4 << 20),
+    )(keep, got)
+
+
+BESIDE = [(0, 1), (3, 2)]
+BEYOND = [(0, 2), (3, 1)]
+MIDDLE = [(1, 2), (2, 1)]
+
+
+def middle_shards(a_blocks, a_codes, b_blocks, b_codes):
+    a_slots, slots = a_blocks.shape[0], b_blocks.shape[0]
+    a_pack, b_pack, b_first, b_second = pack(a_codes, b_codes, a_blocks, b_blocks)
+    b_across = lax.ppermute(b_pack, "row", MIDDLE)
+    end_first = lax.ppermute(b_first, "row", BESIDE)
+    a_other = lax.ppermute(a_pack, "col", [(0, 1), (1, 0)])
+    a_end = lax.ppermute(a_pack, "row", BESIDE)
+    end_second = lax.ppermute(b_second, "row", BESIDE)
+    far_first = lax.ppermute(end_first, "row", MIDDLE)
+    far_second = lax.ppermute(end_second, "row", MIDDLE)
+    rows_cols = [(r * 2 + c, r * 2 + 1 - c) for r in (1, 2) for c in (0, 1)]
+    a_end_other = lax.ppermute(a_end, ("row", "col"), rows_cols)
+
+    dense = early(b_pack, b_across, end_first, end_second, far_first, a_other, slots)
+    dense, end_keep, end_send = end_product(
+        (a_end, a_end_other), dense, far_first, far_second, a_slots, slots
+    )
+    own_keep, own_send = own_product((a_pack, a_other), dense, a_slots)
+
+    cores = [(r * 4 + m, r * 4 + (m ^ 1)) for r in (1, 2) for m in range(4)]
+    ends = ((1, 0), (2, 3))
+    across = [(s * 4 + m, e * 4 + (m ^ 2)) for s, e in ends for m in range(4)]
+    along = [(s * 4 + m, e * 4 + m) for s, e in ends for m in range(4)]
+    chips = [(r * 4 + m, r * 4 + (m ^ 2)) for r in (1, 2) for m in range(4)]
+
+    def over_cores(keep, send):
+        return fold(keep, lax.ppermute(send, ("row", "layer"), cores))
+
+    near, far = over_cores(end_keep, end_send)
+    out = lax.ppermute(near, ("row", "layer"), along)
+    out = out + lax.ppermute(far, ("row", "layer"), across)
+    own_send, _ = lax.optimization_barrier((own_send, near))
+    near, far = over_cores(own_keep, own_send)
+    out = out + near
+    out = out + lax.ppermute(far, ("row", "layer"), chips)
+    return out.astype(jnp.bfloat16)
+
+
 def solution(mesh):
     placed = (
         P(("row", "col", "layer"), None, None),
@@ -100,6 +376,7 @@
         P(("row", "col", "layer"), None, None),
         P(("row", "col", "layer")),
     )
+    body = middle_shards if middle_plan(mesh.shape) else shards
     return jax.shard_map(
-        shards, mesh=mesh, in_specs=placed, out_specs=P(("row", "layer"), "col"), check_vma=False
-    )
+        body, mesh=mesh, in_specs=placed, out_specs=P(("row", "layer"), "col"), check_vma=False
+    )

time: 130 us -> 58.8 us (0.45)
  blocking collectives: 19.2 us -> 0 us
  waiting for transfers between devices: 53.2 us -> 35.9 us
  between operations: 13.5 us -> 0.2 us
  matrix products: 7.73 us -> 0 us
  local copies, waits for them, and re-layouts: 7.49 us -> 0 us
  starting transfers between devices: 24.5 us -> 19.2 us
  other arithmetic: 3.35 us -> 0.75 us
  Pallas kernels: 0 us -> 2.28 us
    reduce_scatter x1 -> x0, waiting for transfers between devices: 26.3 us -> none  [shards(): lax.psum_scatter(accumulated, 'layer', scatter_dimension=0, tiled=True)]
    ppermute x12 -> x13, waiting for transfers between devices: 15.4 us -> 35.9 us  [the longest x1 28 us: middle_shards(): out = out + lax.ppermute(far, ('row', 'layer'), across)]
    all_to_all x2 -> x0, blocking collectives: 19.2 us -> none  [the longest x1 10.6 us: shards(): lax.all_to_all(b_codes, 'row', split_axis=0, concat_axis=0, tiled=True)]
    all_to_all x2 -> x0, waiting for transfers between devices: 11.5 us -> none  [the longest x1 8.58 us: shards(): lax.all_to_all(b_blocks, 'row', split_axis=0, concat_axis=0, tiled=True)]
    dot_general x12 -> x0, matrix products: 7.73 us -> none  [the longest x4 4.81 us: multiply(): jnp.dot(left_tile, right_tile, preferred_element_type=jnp.float32)]
    all_to_all x2 -> x0, starting transfers between devices: 7.71 us -> none  [the longest x1 4.23 us: shards(): lax.all_to_all(a_codes, 'col', split_axis=0, concat_axis=0, tiled=True)]
    convert_element_type x5 -> x0, local copies, waits for them, and re-layouts: 4.03 us -> none  [the longest x4 2.14 us: dense_right(): dense_tile.astype(jnp.bfloat16).reshape(KB * block_width, CB * block_width)]
    all_to_all x5 -> x0, local copies, waits for them, and re-layouts: 2.78 us -> none  [the longest x3 1.96 us: shards(): lax.all_to_all(a_codes, 'col', split_axis=0, concat_axis=0, tiled=True)]
  transfers between devices with their start and end apart: 15 -> 13, of which waited for: 7 -> 3; matrix products, arithmetic and copies ran while one was open for 7% -> 0% of each run, Pallas kernels for 0% -> 0%
where the time goes in v2:
time: 58.8 us; the launch traced here: 58.4 us
  waiting for transfers between devices  35.9 us (61%)
  starting transfers between devices  19.2 us (33%)
  Pallas kernels  2.28 us (4%)
  other arithmetic  0.75 us (1%)
    ppermute x1, waiting for transfers between devices, middle_shards(): out = out + lax.ppermute(far, ('row', 'layer'), across)  28 us
    ppermute x1, starting transfers between devices, middle_shards(): end_first = lax.ppermute(b_first, 'row', BESIDE)  4.94 us
    ppermute x1, waiting for transfers between devices, middle_shards(): a_end = lax.ppermute(a_pack, 'row', BESIDE)  4.11 us
    ppermute x1, starting transfers between devices, middle_shards(): end_second = lax.ppermute(b_second, 'row', BESIDE)  4.07 us
    ppermute x1, waiting for transfers between devices, middle_shards(): end_second = lax.ppermute(b_second, 'row', BESIDE)  3.8 us
    pallas_call x1, Pallas kernels, pack(): pl.pallas_call(pack_body, out_shape=tuple((jax.ShapeDtypeStruct((rows, wi...  2.01 us
    ppermute x1, starting transfers between devices, middle_shards(): a_other = lax.ppermute(a_pack, 'col', [(0, 1), (1, 0)])  1.58 us
    ppermute x2, starting transfers between devices, over_cores(): return fold(keep, lax.ppermute(send, ('row', 'layer'), cores))  1.39 us
  transfers between devices with their start and end apart: 13, of which 3 were waited for; matrix products, arithmetic and copies ran while one was open for 0% of the time, Pallas kernels for 0%

profile of v2, /device:TPU:0, one launch (start us, length us, event | category | flops | bytes accessed | tf_op | source)
XLA Modules:
  0.0 58.4 jit_solution(17070754233253743032)
XLA Ops:
  0.0 2.0 %shard_map.46 = (bf16[1040,128]{1,0:T(8,128)(2,1)S(1)}, bf16[2064,128]{1,0:T(8,128)(2,1)S(1)}, bf16[1040,128]{1,0:T(8,128)(2,1)S(1)}, bf16[1024,128]{1,0:T(8,128)(2,1)S(1)}) custom-call(s32[8]{0:T(128)} %a_codes.1, s32[16]{0:T(128)} %b_codes.1, bf16[1024,128]{1,0:T(8,128)(2,1)} %bitcast.3, bf16[2048,128]{1,0:T(8,128)(2,1)} %bitcast.2), custom_call_target="tpu_custom_call" | custom-call | tf_op jit(solution)/shard_map/pallas_call | solution.py:146
  2.0 4.9 %collective-permute-start.3 = (bf16[1040,128]{1,0:T(8,128)(2,1)S(1)}, bf16[1040,128]{1,0:T(8,128)(2,1)S(1)}, u32[]{:S(2)}, u32[]{:S(2)}) collective-permute-start(bf16[1040,128]{1,0:T(8,128)(2,1)S(1)} %get-tuple-element.21), channel_id=1, source_target_pairs={{0,8},{24,16},{1,9},{25,17},{2,10},{26,18},{3,11},{27,19},{4,12},{... | collective-permute-start | bytes 798728 | tf_op jit(solution)/shard_map/ppermute | solution.py:338
  7.0 1.3 %collective-permute-start = (bf16[1040,128]{1,0:T(8,128)(2,1)S(1)}, bf16[1040,128]{1,0:T(8,128)(2,1)S(1)}, u32[]{:S(2)}, u32[]{:S(2)}) collective-permute-start(bf16[1040,128]{1,0:T(8,128)(2,1)S(1)} %get-tuple-element.19.packs_0), channel_id=1, source_target_pairs={{0,8},{24,16},{1,9},{25,17},{2,10},{26,18},{3,11},{27,19},{4,12},{... | collective-permute-start | bytes 798728 | tf_op jit(solution)/shard_map/ppermute | solution.py:340
  8.3 0.7 %collective-permute-start.2 = (bf16[2064,128]{1,0:T(8,128)(2,1)S(1)}, bf16[2064,128]{1,0:T(8,128)(2,1)S(1)}, u32[]{:S(2)}, u32[]{:S(2)}) collective-permute-start(bf16[2064,128]{1,0:T(8,128)(2,1)S(1)} %get-tuple-element.20.own), channel_id=1, source_target_pairs={{8,16},{16,8},{9,17},{17,9},{10,18},{18,10},{11,19},{19,11},{12,20... | collective-permute-start | bytes 1585160 | tf_op jit(solution)/shard_map/ppermute | solution.py:337
  9.0 4.1 %collective-permute-start.4 = (bf16[1024,128]{1,0:T(8,128)(2,1)S(1)}, bf16[1024,128]{1,0:T(8,128)(2,1)S(1)}, u32[]{:S(2)}, u32[]{:S(2)}) collective-permute-start(bf16[1024,128]{1,0:T(8,128)(2,1)S(1)} %get-tuple-element.22), channel_id=1, source_target_pairs={{0,8},{24,16},{1,9},{25,17},{2,10},{26,18},{3,11},{27,19},{4,12},{... | collective-permute-start | bytes 786440 | tf_op jit(solution)/shard_map/ppermute | solution.py:341
  13.1 1.6 %collective-permute-start.6 = (bf16[1040,128]{1,0:T(8,128)(2,1)S(1)}, bf16[1040,128]{1,0:T(8,128)(2,1)S(1)}, u32[]{:S(2)}, u32[]{:S(2)}) collective-permute-start(bf16[1040,128]{1,0:T(8,128)(2,1)S(1)} %get-tuple-element.19.packs_0), channel_id=1, source_target_pairs={{0,4},{4,0},{1,5},{5,1},{2,6},{6,2},{3,7},{7,3},{8,12},{12,8},{9,1... | collective-permute-start | bytes 798728 | tf_op jit(solution)/shard_map/ppermute | solution.py:339
  14.6 0.0 collective-permute-done.3.first
  14.7 0.7 %collective-permute-start.5 = (bf16[1040,128]{1,0:T(8,128)(2,1)S(1)}, bf16[1040,128]{1,0:T(8,128)(2,1)S(1)}, u32[]{:S(2)}, u32[]{:S(2)}) collective-permute-start(bf16[1040,128]{1,0:T(8,128)(2,1)S(1)} %collective-permute-done.3.first), channel_id=1, source_target_pairs={{8,16},{16,8},{9,17},{17,9},{10,18},{18,10},{11,19},{19,11},{12,20... | collective-permute-start | bytes 798728 | tf_op jit(solution)/shard_map/ppermute | solution.py:342
  15.3 4.1 %collective-permute-done.packs_0 = bf16[1040,128]{1,0:T(8,128)(2,1)S(1)} collective-permute-done((bf16[1040,128]{1,0:T(8,128)(2,1)S(1)}, bf16[1040,128]{1,0:T(8,128)(2,1)S(1)}, u32[]{:S(2)}, u32[]{:S(2)}) %collective-permute-start) | collective-permute-done | bytes 266272 | tf_op jit(solution)/shard_map/ppermute | solution.py:340
  19.4 0.7 %collective-permute-start.1 = (bf16[1040,128]{1,0:T(8,128)(2,1)S(1)}, bf16[1040,128]{1,0:T(8,128)(2,1)S(1)}, u32[]{:S(2)}, u32[]{:S(2)}) collective-permute-start(bf16[1040,128]{1,0:T(8,128)(2,1)S(1)} %collective-permute-done.packs_0), channel_id=1, source_target_pairs={{8,12},{12,8},{16,20},{20,16},{9,13},{13,9},{17,21},{21,17},{10,14... | collective-permute-start | bytes 798728 | tf_op jit(solution)/shard_map/ppermute | solution.py:345
  20.1 3.8 %collective-permute-done.4.second = bf16[1024,128]{1,0:T(8,128)(2,1)S(1)} collective-permute-done((bf16[1024,128]{1,0:T(8,128)(2,1)S(1)}, bf16[1024,128]{1,0:T(8,128)(2,1)S(1)}, u32[]{:S(2)}, u32[]{:S(2)}) %collective-permute-start.4) | collective-permute-done | bytes 262176 | tf_op jit(solution)/shard_map/ppermute | solution.py:341
  23.9 0.7 %collective-permute-start.7 = (bf16[1024,128]{1,0:T(8,128)(2,1)S(1)}, bf16[1024,128]{1,0:T(8,128)(2,1)S(1)}, u32[]{:S(2)}, u32[]{:S(2)}) collective-permute-start(bf16[1024,128]{1,0:T(8,128)(2,1)S(1)} %collective-permute-done.4.second), channel_id=1, source_target_pairs={{8,16},{16,8},{9,17},{17,9},{10,18},{18,10},{11,19},{19,11},{12,20... | collective-permute-start | bytes 786440 | tf_op jit(solution)/shard_map/ppermute | solution.py:343
  24.6 0.0 collective-permute-done.6.other.packs_1
  24.6 0.0 collective-permute-done.2.across
  24.6 0.0 collective-permute-done.5.far.first
  24.7 0.0 collective-permute-done.7.second
  24.7 0.0 collective-permute-done.1.packs_1
  24.7 0.7 %collective-permute-start.8 = (f32[256,512]{1,0:T(8,128)S(1)}, f32[256,512]{1,0:T(8,128)S(1)}, u32[]{:S(2)}, u32[]{:S(2)}) collective-permute-start(f32[256,512]{1,0:T(8,128)S(1)} %get-tuple-element.24), channel_id=1, source_target_pairs={{8,9},{9,8},{10,11},{11,10},{16,17},{17,16},{18,19},{19,18},{12,13... | collective-permute-start | bytes 1572872 | tf_op jit(solution)/shard_map/ppermute | solution.py:360
  25.4 0.1 shard_map.50
  25.5 0.0 collective-permute-done.8.got
  25.5 0.1 shard_map.49
  25.6 0.7 %collective-permute-start.11 = (f32[256,512]{1,0:T(8,128)S(1)}, f32[256,512]{1,0:T(8,128)S(1)}, u32[]{:S(2)}, u32[]{:S(2)}) collective-permute-start(f32[256,512]{1,0:T(8,128)S(1)} %get-tuple-element.30), channel_id=1, source_target_pairs={{8,9},{9,8},{10,11},{11,10},{16,17},{17,16},{18,19},{19,18},{12,13... | collective-permute-start | bytes 1572872 | tf_op jit(solution)/shard_map/ppermute | solution.py:360
  26.3 1.3 %collective-permute-start.9 = (f32[128,512]{1,0:T(8,128)S(1)}, f32[128,512]{1,0:T(8,128)S(1)}, u32[]{:S(2)}, u32[]{:S(2)}) collective-permute-start(f32[128,512]{1,0:T(8,128)S(1)} %get-tuple-element.25), channel_id=1, source_target_pairs={{8,0},{9,1},{10,2},{11,3},{16,24},{17,25},{18,26},{19,27},{12,4},{... | collective-permute-start | bytes 786440 | tf_op jit(solution)/shard_map/ppermute | solution.py:363
  27.6 1.3 %collective-permute-start.10 = (f32[128,512]{1,0:T(8,128)S(1)}, f32[128,512]{1,0:T(8,128)S(1)}, u32[]{:S(2)}, u32[]{:S(2)}) collective-permute-start(f32[128,512]{1,0:T(8,128)S(1)} %get-tuple-element.26), channel_id=1, source_target_pairs={{8,2},{9,3},{10,0},{11,1},{16,26},{17,27},{18,24},{19,25},{12,6},{... | collective-permute-start | bytes 786440 | tf_op jit(solution)/shard_map/ppermute | solution.py:364
  28.9 0.0 collective-permute-done.11.got
  28.9 0.1 shard_map.51
  29.0 0.7 %collective-permute-start.12 = (f32[128,512]{1,0:T(8,128)S(1)}, f32[128,512]{1,0:T(8,128)S(1)}, u32[]{:S(2)}, u32[]{:S(2)}) collective-permute-start(f32[128,512]{1,0:T(8,128)S(1)} %get-tuple-element.32), channel_id=1, source_target_pairs={{8,10},{9,11},{10,8},{11,9},{16,18},{17,19},{18,16},{19,17},{12,14... | collective-permute-start | bytes 786440 | tf_op jit(solution)/shard_map/ppermute | solution.py:368
  29.7 28.0 %collective-permute-done.10 = f32[128,512]{1,0:T(8,128)S(1)} collective-permute-done((f32[128,512]{1,0:T(8,128)S(1)}, f32[128,512]{1,0:T(8,128)S(1)}, u32[]{:S(2)}, u32[]{:S(2)}) %collective-permute-start.10) | collective-permute-done | bytes 262176 | tf_op jit(solution)/shard_map/ppermute | solution.py:364
  57.7 0.0 collective-permute-done.9
  57.7 0.0 collective-permute-done.12
  57.7 0.8 %add_convert_fusion = bf16[128,512]{1,0:T(8,128)(2,1)} fusion(f32[128,512]{1,0:T(8,128)S(1)} %collective-permute-done.12, f32[128,512]{1,0:T(8,128)S(1)} %get-tuple-element.31, f32[128,512]{1,0:T(8,128)S(1)} %collective-permute-done.9, f32[128,512]{1,0:T(8,128)S(1)} %collective-permute-done.10), kind=kLoop, calls=%fused_computation | loop fusion | flops 262144 | bytes 1179648 | tf_op jit(solution)/shard_map/convert_element_type | solution.py:369
  (2 shorter events, 0.1 us)
Async XLA Ops:
  2.0 12.6 %collective-permute-start.3 = (bf16[1040,128]{1,0:T(8,128)(2,1)S(1)}, bf16[1040,128]{1,0:T(8,128)(2,1)S(1)}, u32[]{:S(2)}, u32[]{:S(2)}) collective-permute-start(bf16[1040,128]{1,0:T(8,128)(2,1)S(1)} %get-tuple-element.21), channel_id=1, source_target_pairs={{0,8},{24,16},{1,9},{25,17},{2,10},{26,18},{3,11},{27,19},{4,12},{... | collective-permute-start | bytes 798728 | tf_op jit(solution)/shard_map/ppermute | solution.py:338
  7.0 12.5 %collective-permute-start = (bf16[1040,128]{1,0:T(8,128)(2,1)S(1)}, bf16[1040,128]{1,0:T(8,128)(2,1)S(1)}, u32[]{:S(2)}, u32[]{:S(2)}) collective-permute-start(bf16[1040,128]{1,0:T(8,128)(2,1)S(1)} %get-tuple-element.19.packs_0), channel_id=1, source_target_pairs={{0,8},{24,16},{1,9},{25,17},{2,10},{26,18},{3,11},{27,19},{4,12},{... | collective-permute-start | bytes 798728 | tf_op jit(solution)/shard_map/ppermute | solution.py:340
  8.3 16.3 %collective-permute-start.2 = (bf16[2064,128]{1,0:T(8,128)(2,1)S(1)}, bf16[2064,128]{1,0:T(8,128)(2,1)S(1)}, u32[]{:S(2)}, u32[]{:S(2)}) collective-permute-start(bf16[2064,128]{1,0:T(8,128)(2,1)S(1)} %get-tuple-element.20.own), channel_id=1, source_target_pairs={{8,16},{16,8},{9,17},{17,9},{10,18},{18,10},{11,19},{19,11},{12,20... | collective-permute-start | bytes 1585160 | tf_op jit(solution)/shard_map/ppermute | solution.py:337
  9.0 14.9 %collective-permute-start.4 = (bf16[1024,128]{1,0:T(8,128)(2,1)S(1)}, bf16[1024,128]{1,0:T(8,128)(2,1)S(1)}, u32[]{:S(2)}, u32[]{:S(2)}) collective-permute-start(bf16[1024,128]{1,0:T(8,128)(2,1)S(1)} %get-tuple-element.22), channel_id=1, source_target_pairs={{0,8},{24,16},{1,9},{25,17},{2,10},{26,18},{3,11},{27,19},{4,12},{... | collective-permute-start | bytes 786440 | tf_op jit(solution)/shard_map/ppermute | solution.py:341
  13.1 11.5 %collective-permute-start.6 = (bf16[1040,128]{1,0:T(8,128)(2,1)S(1)}, bf16[1040,128]{1,0:T(8,128)(2,1)S(1)}, u32[]{:S(2)}, u32[]{:S(2)}) collective-permute-start(bf16[1040,128]{1,0:T(8,128)(2,1)S(1)} %get-tuple-element.19.packs_0), channel_id=1, source_target_pairs={{0,4},{4,0},{1,5},{5,1},{2,6},{6,2},{3,7},{7,3},{8,12},{12,8},{9,1... | collective-permute-start | bytes 798728 | tf_op jit(solution)/shard_map/ppermute | solution.py:339
  14.7 10.0 %collective-permute-start.5 = (bf16[1040,128]{1,0:T(8,128)(2,1)S(1)}, bf16[1040,128]{1,0:T(8,128)(2,1)S(1)}, u32[]{:S(2)}, u32[]{:S(2)}) collective-permute-start(bf16[1040,128]{1,0:T(8,128)(2,1)S(1)} %collective-permute-done.3.first), channel_id=1, source_target_pairs={{8,16},{16,8},{9,17},{17,9},{10,18},{18,10},{11,19},{19,11},{12,20... | collective-permute-start | bytes 798728 | tf_op jit(solution)/shard_map/ppermute | solution.py:342
  19.4 5.2 %collective-permute-start.1 = (bf16[1040,128]{1,0:T(8,128)(2,1)S(1)}, bf16[1040,128]{1,0:T(8,128)(2,1)S(1)}, u32[]{:S(2)}, u32[]{:S(2)}) collective-permute-start(bf16[1040,128]{1,0:T(8,128)(2,1)S(1)} %collective-permute-done.packs_0), channel_id=1, source_target_pairs={{8,12},{12,8},{16,20},{20,16},{9,13},{13,9},{17,21},{21,17},{10,14... | collective-permute-start | bytes 798728 | tf_op jit(solution)/shard_map/ppermute | solution.py:345
  23.9 0.7 %collective-permute-start.7 = (bf16[1024,128]{1,0:T(8,128)(2,1)S(1)}, bf16[1024,128]{1,0:T(8,128)(2,1)S(1)}, u32[]{:S(2)}, u32[]{:S(2)}) collective-permute-start(bf16[1024,128]{1,0:T(8,128)(2,1)S(1)} %collective-permute-done.4.second), channel_id=1, source_target_pairs={{8,16},{16,8},{9,17},{17,9},{10,18},{18,10},{11,19},{19,11},{12,20... | collective-permute-start | bytes 786440 | tf_op jit(solution)/shard_map/ppermute | solution.py:343
  24.7 0.8 %collective-permute-start.8 = (f32[256,512]{1,0:T(8,128)S(1)}, f32[256,512]{1,0:T(8,128)S(1)}, u32[]{:S(2)}, u32[]{:S(2)}) collective-permute-start(f32[256,512]{1,0:T(8,128)S(1)} %get-tuple-element.24), channel_id=1, source_target_pairs={{8,9},{9,8},{10,11},{11,10},{16,17},{17,16},{18,19},{19,18},{12,13... | collective-permute-start | bytes 1572872 | tf_op jit(solution)/shard_map/ppermute | solution.py:360
  25.6 3.3 %collective-permute-start.11 = (f32[256,512]{1,0:T(8,128)S(1)}, f32[256,512]{1,0:T(8,128)S(1)}, u32[]{:S(2)}, u32[]{:S(2)}) collective-permute-start(f32[256,512]{1,0:T(8,128)S(1)} %get-tuple-element.30), channel_id=1, source_target_pairs={{8,9},{9,8},{10,11},{11,10},{16,17},{17,16},{18,19},{19,18},{12,13... | collective-permute-start | bytes 1572872 | tf_op jit(solution)/shard_map/ppermute | solution.py:360
  26.3 31.4 %collective-permute-start.9 = (f32[128,512]{1,0:T(8,128)S(1)}, f32[128,512]{1,0:T(8,128)S(1)}, u32[]{:S(2)}, u32[]{:S(2)}) collective-permute-start(f32[128,512]{1,0:T(8,128)S(1)} %get-tuple-element.25), channel_id=1, source_target_pairs={{8,0},{9,1},{10,2},{11,3},{16,24},{17,25},{18,26},{19,27},{12,4},{... | collective-permute-start | bytes 786440 | tf_op jit(solution)/shard_map/ppermute | solution.py:363
  27.6 30.1 %collective-permute-start.10 = (f32[128,512]{1,0:T(8,128)S(1)}, f32[128,512]{1,0:T(8,128)S(1)}, u32[]{:S(2)}, u32[]{:S(2)}) collective-permute-start(f32[128,512]{1,0:T(8,128)S(1)} %get-tuple-element.26), channel_id=1, source_target_pairs={{8,2},{9,3},{10,0},{11,1},{16,26},{17,27},{18,24},{19,25},{12,6},{... | collective-permute-start | bytes 786440 | tf_op jit(solution)/shard_map/ppermute | solution.py:364
  29.0 28.7 %collective-permute-start.12 = (f32[128,512]{1,0:T(8,128)S(1)}, f32[128,512]{1,0:T(8,128)S(1)}, u32[]{:S(2)}, u32[]{:S(2)}) collective-permute-start(f32[128,512]{1,0:T(8,128)S(1)} %get-tuple-element.32), channel_id=1, source_target_pairs={{8,10},{9,11},{10,8},{11,9},{16,18},{17,19},{18,16},{19,17},{12,14... | collective-permute-start | bytes 786440 | tf_op jit(solution)/shard_map/ppermute | solution.py:368

commit v3 on v2

--- a/solution.py
+++ b/solution.py
@@ -98,6 +98,7 @@
 
 
 CODE_ROWS = 16
+FIRST = 8
 
 
 def middle_plan(mesh_shape):
@@ -109,15 +110,21 @@
     return [pl.BlockSpec(memory_space=kinds[name]) for name in names]
 
 
-def pack_body(a_codes, b_codes, a_ref, b_ref, a_out, b_out, first_out, second_out, sems):
+def first_slots(slots):
+    return slots * FIRST // 16
+
+
+def pack_body(a_codes, b_codes, a_ref, b_ref, a_out, b_out, mixed_out, second_out, sems):
     a_rows, b_rows = a_ref.shape[0], b_ref.shape[0]
     width = a_ref.shape[1]
-    half = b_rows // 2
+    second = second_out.shape[0] - CODE_ROWS
+    first = b_rows - second
     copies = [
-        pltpu.make_async_copy(b_ref.at[pl.ds(0, half)], first_out.at[pl.ds(0, half)], sems.at[0]),
-        pltpu.make_async_copy(b_ref, b_out.at[pl.ds(0, b_rows)], sems.at[1]),
-        pltpu.make_async_copy(b_ref.at[pl.ds(half, half)], second_out, sems.at[2]),
-        pltpu.make_async_copy(a_ref, a_out.at[pl.ds(0, a_rows)], sems.at[3]),
+        pltpu.make_async_copy(b_ref, b_out.at[pl.ds(0, b_rows)], sems.at[0]),
+        pltpu.make_async_copy(b_ref.at[pl.ds(0, first)], mixed_out.at[pl.ds(0, first)], sems.at[1]),
+        pltpu.make_async_copy(a_ref, mixed_out.at[pl.ds(first + CODE_ROWS, a_rows)], sems.at[2]),
+        pltpu.make_async_copy(b_ref.at[pl.ds(first, second)], second_out.at[pl.ds(0, second)], sems.at[3]),
+        pltpu.make_async_copy(a_ref, a_out.at[pl.ds(0, a_rows)], sems.at[4]),
     ]
     for copy in copies:
         copy.start()
@@ -129,10 +136,12 @@
             values = jnp.where(lanes == slot, codes_ref[slot], values)
         return values.astype(jnp.float32).astype(jnp.bfloat16)
 
-    a_out[pl.ds(a_rows, CODE_ROWS), :] = code_rows(a_codes)
-    b_tail = code_rows(b_codes)
+    a_tail, b_tail = code_rows(a_codes), code_rows(b_codes)
+    a_out[pl.ds(a_rows, CODE_ROWS), :] = a_tail
     b_out[pl.ds(b_rows, CODE_ROWS), :] = b_tail
-    first_out[pl.ds(half, CODE_ROWS), :] = b_tail
+    mixed_out[pl.ds(first, CODE_ROWS), :] = b_tail
+    mixed_out[pl.ds(first + CODE_ROWS + a_rows, CODE_ROWS), :] = a_tail
+    second_out[pl.ds(second, CODE_ROWS), :] = b_tail
     for copy in copies:
         copy.wait()
 
@@ -142,15 +151,38 @@
     a_flat = a_blocks.reshape(-1, width)
     b_flat = b_blocks.reshape(-1, width)
     a_rows, b_rows = a_flat.shape[0], b_flat.shape[0]
-    sizes = (a_rows + CODE_ROWS, b_rows + CODE_ROWS, b_rows // 2 + CODE_ROWS, b_rows // 2)
+    first = first_slots(b_blocks.shape[0]) * width
+    sizes = (
+        a_rows + CODE_ROWS,
+        b_rows + CODE_ROWS,
+        first + a_rows + 2 * CODE_ROWS,
+        b_rows - first + CODE_ROWS,
+    )
     return pl.pallas_call(
         pack_body,
         out_shape=tuple(jax.ShapeDtypeStruct((rows, width), jnp.bfloat16) for rows in sizes),
         in_specs=spaces("s", "s", "h", "h"),
         out_specs=tuple(spaces("v", "v", "v", "v")),
-        scratch_shapes=[pltpu.SemaphoreType.DMA((4,))],
+        scratch_shapes=[pltpu.SemaphoreType.DMA((5,))],
         compiler_params=pltpu.CompilerParams(vmem_limit_bytes=8 << 20),
     )(*(pltpu.with_memory_space_constraint(x, pltpu.HBM) for x in (a_codes, b_codes, a_flat, b_flat)))
+
+
+def part_body(mixed, first, second):
+    rows = first.shape[0]
+    first[...] = mixed[pl.ds(0, rows), :]
+    second[...] = mixed[pl.ds(rows, second.shape[0]), :]
+
+
+def part(mixed, rows):
+    sizes = (rows, mixed.shape[0] - rows)
+    return pl.pallas_call(
+        part_body,
+        out_shape=tuple(jax.ShapeDtypeStruct((n, mixed.shape[1]), mixed.dtype) for n in sizes),
+        in_specs=spaces("v"),
+        out_specs=tuple(spaces("v", "v")),
+        compiler_params=pltpu.CompilerParams(vmem_limit_bytes=4 << 20),
+    )(mixed)
 
 
 def fetch_codes(packs, staged, codes, sem):
@@ -192,7 +224,7 @@
 
 def early_body(slots, own, across, first, second, far, other, dense, staged, codes, sem):
     del other
-    half = slots // 2
+    cut = first_slots(slots)
 
     @pl.when(in_middle())
     def _():
@@ -203,9 +235,9 @@
         copy.wait()
         put_blocks(dense, own, codes, 0, 0, slots, slots, col)
         put_blocks(dense, across, codes, 1, 0, slots, slots, col)
-        put_blocks(dense, first, codes, 2, 0, half, slots, col)
-        put_blocks(dense, second, codes, 2, half, half, slots, col)
-        put_blocks(dense, far, codes, 3, 0, half, slots, col)
+        put_blocks(dense, first, codes, 2, 0, cut, slots, col)
+        put_blocks(dense, second, codes, 2, cut, slots - cut, slots, col)
+        put_blocks(dense, far, codes, 3, cut, slots - cut, slots, col)
 
 
 def early(own, across, first, second, far, other, slots):
@@ -244,60 +276,67 @@
             total[pl.ds(pl.multiple_of(spot * width, width), width), :] += part
 
 
-def end_body(a_slots, slots, packs_0, packs_1, dense_in, first, second,
+def own_body(a_slots, slots, packs_0, packs_1, dense_in, first,
              dense, keep, send, total, staged, codes, sem):
-    half = slots // 2
+    cut = first_slots(slots)
     rows = keep.shape[0]
     del dense_in
+
+    @pl.when(jnp.logical_not(in_middle()))
+    def _():
+        keep[...] = jnp.zeros_like(keep)
+        send[...] = jnp.zeros_like(send)
 
     @pl.when(in_middle())
     def _():
         copy = fetch_codes((packs_0, packs_1, first), staged, codes, sem)
         copy.start()
         copy.wait()
-        put_blocks(dense, second, codes, 2, half, half, slots, lax.axis_index("col"))
-        row = jnp.where(lax.axis_index("row") == 1, 0, 3)
-        multiply_group(dense, total, (packs_0, packs_1), codes, a_slots, row)
+        col = lax.axis_index("col")
+        put_blocks(dense, first, codes, 2, 0, cut, slots, col)
+        multiply_group(dense, total, (packs_0, packs_1), codes, a_slots, lax.axis_index("row"))
         keep[...] = total[pl.ds(0, rows), :]
         send[...] = total[pl.ds(rows, rows), :]
 
 
-def own_body(a_slots, packs_0, packs_1, dense, keep, send, total, staged, codes, sem):
+def end_body(a_slots, packs_0, packs_1, dense, keep, send, total, staged, codes, sem):
     rows = keep.shape[0]
 
     @pl.when(jnp.logical_not(in_middle()))
     def _():
         keep[...] = jnp.zeros_like(keep)
+        send[...] = jnp.zeros_like(send)
 
     @pl.when(in_middle())
     def _():
         copy = fetch_codes((packs_0, packs_1), staged, codes, sem)
         copy.start()
         copy.wait()
-        multiply_group(dense, total, (packs_0, packs_1), codes, a_slots, lax.axis_index("row"))
+        row = jnp.where(lax.axis_index("row") == 1, 0, 3)
+        multiply_group(dense, total, (packs_0, packs_1), codes, a_slots, row)
         keep[...] = total[pl.ds(0, rows), :]
         send[...] = total[pl.ds(rows, rows), :]
 
 
-def end_product(packs, dense, first, second, a_slots, slots):
+def own_product(packs, dense, first, a_slots, slots):
     width = packs[0].shape[1]
     half = jax.ShapeDtypeStruct((2 * width, CB * width), jnp.float32)
     return pl.pallas_call(
-        functools.partial(end_body, a_slots, slots),
+        functools.partial(own_body, a_slots, slots),
         out_shape=(jax.ShapeDtypeStruct(dense.shape, dense.dtype), half, half),
-        in_specs=spaces("v", "v", "v", "v", "v"),
+        in_specs=spaces("v", "v", "v", "v"),
         out_specs=tuple(spaces("v", "v", "v")),
         scratch_shapes=[pltpu.VMEM((5 * width, CB * width), jnp.float32)] + code_scratch(),
         input_output_aliases={2: 0},
         compiler_params=pltpu.CompilerParams(vmem_limit_bytes=16 << 20),
-    )(*packs, dense, first, second)
-
-
-def own_product(packs, dense, a_slots):
+    )(*packs, dense, first)
+
+
+def end_product(packs, dense, a_slots):
     width = packs[0].shape[1]
     half = jax.ShapeDtypeStruct((2 * width, CB * width), jnp.float32)
     return pl.pallas_call(
-        functools.partial(own_body, a_slots),
+        functools.partial(end_body, a_slots),
         out_shape=(half, half),
         in_specs=spaces("v", "v", "v"),
         out_specs=tuple(spaces("v", "v")),
@@ -326,46 +365,41 @@
     )(keep, got)
 
 
-BESIDE = [(0, 1), (3, 2)]
-BEYOND = [(0, 2), (3, 1)]
-MIDDLE = [(1, 2), (2, 1)]
+BESIDE = [(0, 1), (1, 0), (2, 3), (3, 2)]
+BEYOND = [(0, 2), (2, 3), (3, 1), (1, 0)]
+COLS = [(0, 1), (1, 0)]
+CORES = [(0, 1), (1, 0), (2, 3), (3, 2)]
+CHIPS = [(0, 2), (2, 0), (1, 3), (3, 1)]
+MIDDLE = [(r * 4 + m, (3 - r) * 4 + m if r in (1, 2) else r * 4 + (m ^ 1)) for r in range(4) for m in range(4)]
+ACROSS = [(r * 4 + m, (r ^ 1) * 4 + (m ^ 2)) for r in range(4) for m in range(4)]
 
 
 def middle_shards(a_blocks, a_codes, b_blocks, b_codes):
     a_slots, slots = a_blocks.shape[0], b_blocks.shape[0]
-    a_pack, b_pack, b_first, b_second = pack(a_codes, b_codes, a_blocks, b_blocks)
-    b_across = lax.ppermute(b_pack, "row", MIDDLE)
-    end_first = lax.ppermute(b_first, "row", BESIDE)
-    a_other = lax.ppermute(a_pack, "col", [(0, 1), (1, 0)])
-    a_end = lax.ppermute(a_pack, "row", BESIDE)
+    a_pack, b_pack, mixed, b_second = pack(a_codes, b_codes, a_blocks, b_blocks)
+    b_across = lax.ppermute(b_pack, ("row", "layer"), MIDDLE)
+    end_mixed = lax.ppermute(mixed, "row", BESIDE)
+    far_second = lax.ppermute(b_second, "row", BEYOND)
     end_second = lax.ppermute(b_second, "row", BESIDE)
-    far_first = lax.ppermute(end_first, "row", MIDDLE)
-    far_second = lax.ppermute(end_second, "row", MIDDLE)
-    rows_cols = [(r * 2 + c, r * 2 + 1 - c) for r in (1, 2) for c in (0, 1)]
-    a_end_other = lax.ppermute(a_end, ("row", "col"), rows_cols)
-
-    dense = early(b_pack, b_across, end_first, end_second, far_first, a_other, slots)
-    dense, end_keep, end_send = end_product(
-        (a_end, a_end_other), dense, far_first, far_second, a_slots, slots
-    )
-    own_keep, own_send = own_product((a_pack, a_other), dense, a_slots)
-
-    cores = [(r * 4 + m, r * 4 + (m ^ 1)) for r in (1, 2) for m in range(4)]
-    ends = ((1, 0), (2, 3))
-    across = [(s * 4 + m, e * 4 + (m ^ 2)) for s, e in ends for m in range(4)]
-    along = [(s * 4 + m, e * 4 + m) for s, e in ends for m in range(4)]
-    chips = [(r * 4 + m, r * 4 + (m ^ 2)) for r in (1, 2) for m in range(4)]
+    a_other = lax.ppermute(a_pack, "col", COLS)
+    end_first, a_end = part(end_mixed, end_mixed.shape[0] - a_pack.shape[0])
+    far_first = lax.ppermute(end_first, ("row", "layer"), MIDDLE)
+    a_end_other = lax.ppermute(a_end, "col", COLS)
+
+    dense = early(b_pack, b_across, end_first, end_second, far_second, a_other, slots)
+    dense, own_keep, own_send = own_product(
+        (a_pack, a_other), dense, far_first, a_slots, slots
+    )
+    end_keep, end_send = end_product((a_end, a_end_other), dense, a_slots)
 
     def over_cores(keep, send):
-        return fold(keep, lax.ppermute(send, ("row", "layer"), cores))
-
-    near, far = over_cores(end_keep, end_send)
-    out = lax.ppermute(near, ("row", "layer"), along)
-    out = out + lax.ppermute(far, ("row", "layer"), across)
-    own_send, _ = lax.optimization_barrier((own_send, near))
-    near, far = over_cores(own_keep, own_send)
-    out = out + near
-    out = out + lax.ppermute(far, ("row", "layer"), chips)
+        return fold(keep, lax.ppermute(send, "layer", CORES))
+
+    own_near, own_far = over_cores(own_keep, own_send)
+    end_near, end_far = over_cores(end_keep, end_send)
+    out = own_near + lax.ppermute(end_near, "row", BESIDE)
+    out = out + lax.ppermute(end_far, ("row", "layer"), ACROSS)
+    out = out + lax.ppermute(own_far, "layer", CHIPS)
     return out.astype(jnp.bfloat16)
 
 

time: 58.8 us -> 52.6 us (0.89)
  waiting for transfers between devices: 35.9 us -> 29.5 us
    ppermute x12 -> x11, waiting for transfers between devices: 32.1 us -> 26 us  [the longest x1 8.25 us: middle_shards(): end_mixed = lax.ppermute(mixed, 'row', BESIDE)]
    ppermute x12 -> x11, starting transfers between devices: 15.2 us -> 16.6 us  [the longest x1 8.54 us: middle_shards(): out = out + lax.ppermute(end_far, ('row', 'layer'), ACROSS)]
    ppermute x1, starting transfers between devices: 4.07 us -> 3.15 us  [middle_shards(): end_second = lax.ppermute(b_second, 'row', BESIDE)]
  transfers between devices with their start and end apart: 13 -> 12, of which waited for: 3 -> 7; matrix products, arithmetic and copies ran while one was open for 0% -> 0% of each run, Pallas kernels for 0% -> 1%
where the time goes in v3:
time: 52.6 us; the launch traced here: 52.5 us
  waiting for transfers between devices  29.5 us (56%)
  starting transfers between devices  19.7 us (37%)
  Pallas kernels  2.48 us (5%)
  other arithmetic  0.73 us (1%)
    ppermute x1, starting transfers between devices, middle_shards(): out = out + lax.ppermute(end_far, ('row', 'layer'), ACROSS)  8.54 us
    ppermute x1, waiting for transfers between devices, middle_shards(): end_mixed = lax.ppermute(mixed, 'row', BESIDE)  8.25 us
    ppermute x1, waiting for transfers between devices, middle_shards(): out = out + lax.ppermute(end_far, ('row', 'layer'), ACROSS)  6.34 us
    ppermute x1, waiting for transfers between devices, middle_shards(): far_second = lax.ppermute(b_second, 'row', BEYOND)  4.88 us
    ppermute x1, waiting for transfers between devices, middle_shards(): out = own_near + lax.ppermute(end_near, 'row', BESIDE)  4.39 us
    ppermute x1, waiting for transfers between devices, middle_shards(): end_second = lax.ppermute(b_second, 'row', BESIDE)  3.51 us
    ppermute x1, starting transfers between devices, middle_shards(): end_second = lax.ppermute(b_second, 'row', BESIDE)  3.15 us
    ppermute x1, starting transfers between devices, middle_shards(): end_mixed = lax.ppermute(mixed, 'row', BESIDE)  3.09 us
  transfers between devices with their start and end apart: 12, of which 7 were waited for; matrix products, arithmetic and copies ran while one was open for 0% of the time, Pallas kernels for 1%

profile of v3, /device:TPU:0, one launch (start us, length us, event | category | flops | bytes accessed | tf_op | source)
XLA Modules:
  0.0 52.5 jit_solution(9524259468632573994)
XLA Ops:
  0.0 2.1 %shard_map.46 = (bf16[1040,128]{1,0:T(8,128)(2,1)S(1)}, bf16[2064,128]{1,0:T(8,128)(2,1)S(1)}, bf16[2080,128]{1,0:T(8,128)(2,1)S(1)}, bf16[1040,128]{1,0:T(8,128)(2,1)S(1)}) custom-call(s32[8]{0:T(128)} %a_codes.1, s32[16]{0:T(128)} %b_codes.1, bf16[1024,128]{1,0:T(8,128)(2,1)} %bitcast.3, bf16[2048,128]{1,0:T(8,128)(2,1)} %bitcast.2), custom_call_target="tpu_custom_call" | custom-call | tf_op jit(solution)/shard_map/pallas_call | solution.py:161
  2.1 3.1 %collective-permute-start.2 = (bf16[2080,128]{1,0:T(8,128)(2,1)S(1)}, bf16[2080,128]{1,0:T(8,128)(2,1)S(1)}, u32[]{:S(2)}, u32[]{:S(2)}) collective-permute-start(bf16[2080,128]{1,0:T(8,128)(2,1)S(1)} %get-tuple-element.22), channel_id=1, source_target_pairs={{0,8},{8,0},{16,24},{24,16},{1,9},{9,1},{17,25},{25,17},{2,10},{10... | collective-permute-start | bytes 1597448 | tf_op jit(solution)/shard_map/ppermute | solution.py:381
  5.2 1.5 %collective-permute-start = (bf16[1040,128]{1,0:T(8,128)(2,1)S(1)}, bf16[1040,128]{1,0:T(8,128)(2,1)S(1)}, u32[]{:S(2)}, u32[]{:S(2)}) collective-permute-start(bf16[1040,128]{1,0:T(8,128)(2,1)S(1)} %get-tuple-element.20.packs_0), channel_id=1, source_target_pairs={{0,4},{4,0},{1,5},{5,1},{2,6},{6,2},{3,7},{7,3},{8,12},{12,8},{9,1... | collective-permute-start | bytes 798728 | tf_op jit(solution)/shard_map/ppermute | solution.py:384
  6.7 0.0 collective-permute-start.1
  6.7 3.1 %collective-permute-start.3 = (bf16[1040,128]{1,0:T(8,128)(2,1)S(1)}, bf16[1040,128]{1,0:T(8,128)(2,1)S(1)}, u32[]{:S(2)}, u32[]{:S(2)}) collective-permute-start(bf16[1040,128]{1,0:T(8,128)(2,1)S(1)} %get-tuple-element.24), channel_id=1, source_target_pairs={{0,8},{8,0},{16,24},{24,16},{1,9},{9,1},{17,25},{25,17},{2,10},{10... | collective-permute-start | bytes 798728 | tf_op jit(solution)/shard_map/ppermute | solution.py:383
  9.9 0.0 collective-permute-start.4
  9.9 8.2 %collective-permute-done.2.mixed = bf16[2080,128]{1,0:T(8,128)(2,1)S(1)} collective-permute-done((bf16[2080,128]{1,0:T(8,128)(2,1)S(1)}, bf16[2080,128]{1,0:T(8,128)(2,1)S(1)}, u32[]{:S(2)}, u32[]{:S(2)}) %collective-permute-start.2) | collective-permute-done | bytes 532512 | tf_op jit(solution)/shard_map/ppermute | solution.py:381
  18.2 0.1 collective-permute-start.5
  18.2 0.0 collective-permute-done.other.packs_1
  18.3 2.1 %collective-permute-start.7 = (bf16[1040,128]{1,0:T(8,128)(2,1)S(1)}, bf16[1040,128]{1,0:T(8,128)(2,1)S(1)}, u32[]{:S(2)}, u32[]{:S(2)}) collective-permute-start(bf16[1040,128]{1,0:T(8,128)(2,1)S(1)} %get-tuple-element.28.packs_0), channel_id=1, source_target_pairs={{0,4},{4,0},{1,5},{5,1},{2,6},{6,2},{3,7},{7,3},{8,12},{12,8},{9,1... | collective-permute-start | bytes 798728 | tf_op jit(solution)/shard_map/ppermute | solution.py:387
  20.3 3.5 %collective-permute-done.3.second = bf16[1040,128]{1,0:T(8,128)(2,1)S(1)} collective-permute-done((bf16[1040,128]{1,0:T(8,128)(2,1)S(1)}, bf16[1040,128]{1,0:T(8,128)(2,1)S(1)}, u32[]{:S(2)}, u32[]{:S(2)}) %collective-permute-start.3) | collective-permute-done | bytes 266272 | tf_op jit(solution)/shard_map/ppermute | solution.py:383
  23.8 4.9 %collective-permute-done.4.far = bf16[1040,128]{1,0:T(8,128)(2,1)S(1)} collective-permute-done((bf16[1040,128]{1,0:T(8,128)(2,1)S(1)}, bf16[1040,128]{1,0:T(8,128)(2,1)S(1)}, u32[]{:S(2)}, u32[]{:S(2)}) %collective-permute-start.4) | collective-permute-done | bytes 266272 | tf_op jit(solution)/shard_map/ppermute | solution.py:382
  28.7 0.0 collective-permute-done.1.across
  28.7 0.0 collective-permute-done.5.first
  28.7 0.1 shard_map.49
  28.8 0.0 collective-permute-done.7.packs_1
  28.9 0.1 shard_map.51
  29.0 0.1 collective-permute-start.8
  29.0 0.5 collective-permute-start.6
  29.5 1.4 %collective-permute-done.8.got = f32[256,512]{1,0:T(8,128)S(1)} collective-permute-done((f32[256,512]{1,0:T(8,128)S(1)}, f32[256,512]{1,0:T(8,128)S(1)}, u32[]{:S(2)}, u32[]{:S(2)}) %collective-permute-start.8) | collective-permute-done | bytes 524320 | tf_op jit(solution)/shard_map/ppermute | solution.py:396
  30.9 0.1 shard_map.52
  31.0 8.5 %collective-permute-start.10 = (f32[128,512]{1,0:T(8,128)S(1)}, f32[128,512]{1,0:T(8,128)S(1)}, u32[]{:S(2)}, u32[]{:S(2)}) collective-permute-start(f32[128,512]{1,0:T(8,128)S(1)} %get-tuple-element.33), channel_id=1, source_target_pairs={{0,10},{1,11},{2,8},{3,9},{8,2},{9,3},{10,0},{11,1},{16,26},{17,27... | collective-permute-start | bytes 786440 | tf_op jit(solution)/shard_map/ppermute | solution.py:401
  39.5 0.0 collective-permute-start.9
  39.6 0.0 collective-permute-done.6.got
  39.6 0.1 shard_map.50
  39.6 0.7 %collective-permute-start.11 = (f32[128,512]{1,0:T(8,128)S(1)}, f32[128,512]{1,0:T(8,128)S(1)}, u32[]{:S(2)}, u32[]{:S(2)}) collective-permute-start(f32[128,512]{1,0:T(8,128)S(1)} %get-tuple-element.34), channel_id=1, source_target_pairs={{0,2},{2,0},{1,3},{3,1},{4,6},{6,4},{5,7},{7,5},{8,10},{10,8},{9,1... | collective-permute-start | bytes 786440 | tf_op jit(solution)/shard_map/ppermute | solution.py:402
  40.3 6.3 %collective-permute-done.10 = f32[128,512]{1,0:T(8,128)S(1)} collective-permute-done((f32[128,512]{1,0:T(8,128)S(1)}, f32[128,512]{1,0:T(8,128)S(1)}, u32[]{:S(2)}, u32[]{:S(2)}) %collective-permute-start.10) | collective-permute-done | bytes 262176 | tf_op jit(solution)/shard_map/ppermute | solution.py:401
  46.7 4.4 %collective-permute-done.9 = f32[128,512]{1,0:T(8,128)S(1)} collective-permute-done((f32[128,512]{1,0:T(8,128)S(1)}, f32[128,512]{1,0:T(8,128)S(1)}, u32[]{:S(2)}, u32[]{:S(2)}) %collective-permute-start.9) | collective-permute-done | bytes 262176 | tf_op jit(solution)/shard_map/ppermute | solution.py:400
  51.1 0.7 %collective-permute-done.11 = f32[128,512]{1,0:T(8,128)S(1)} collective-permute-done((f32[128,512]{1,0:T(8,128)S(1)}, f32[128,512]{1,0:T(8,128)S(1)}, u32[]{:S(2)}, u32[]{:S(2)}) %collective-permute-start.11) | collective-permute-done | bytes 262176 | tf_op jit(solution)/shard_map/ppermute | solution.py:402
  51.8 0.7 %add_convert_fusion = bf16[128,512]{1,0:T(8,128)(2,1)} fusion(f32[128,512]{1,0:T(8,128)S(1)} %collective-permute-done.11, f32[128,512]{1,0:T(8,128)S(1)} %collective-permute-done.10, f32[128,512]{1,0:T(8,128)S(1)} %get-tuple-element.27, f32[128,512]{1,0:T(8,128)S(1)} %collective-permute-done.9), kind=kLoop, calls=%fused_computation | loop fusion | flops 262144 | bytes 1179648 | tf_op jit(solution)/shard_map/convert_element_type | solution.py:403
  (2 shorter events, 0.0 us)
Async XLA Ops:
  2.1 16.0 %collective-permute-start.2 = (bf16[2080,128]{1,0:T(8,128)(2,1)S(1)}, bf16[2080,128]{1,0:T(8,128)(2,1)S(1)}, u32[]{:S(2)}, u32[]{:S(2)}) collective-permute-start(bf16[2080,128]{1,0:T(8,128)(2,1)S(1)} %get-tuple-element.22), channel_id=1, source_target_pairs={{0,8},{8,0},{16,24},{24,16},{1,9},{9,1},{17,25},{25,17},{2,10},{10... | collective-permute-start | bytes 1597448 | tf_op jit(solution)/shard_map/ppermute | solution.py:381
  5.2 13.0 %collective-permute-start = (bf16[1040,128]{1,0:T(8,128)(2,1)S(1)}, bf16[1040,128]{1,0:T(8,128)(2,1)S(1)}, u32[]{:S(2)}, u32[]{:S(2)}) collective-permute-start(bf16[1040,128]{1,0:T(8,128)(2,1)S(1)} %get-tuple-element.20.packs_0), channel_id=1, source_target_pairs={{0,4},{4,0},{1,5},{5,1},{2,6},{6,2},{3,7},{7,3},{8,12},{12,8},{9,1... | collective-permute-start | bytes 798728 | tf_op jit(solution)/shard_map/ppermute | solution.py:384
  6.7 22.0 %collective-permute-start.1 = (bf16[2064,128]{1,0:T(8,128)(2,1)S(1)}, bf16[2064,128]{1,0:T(8,128)(2,1)S(1)}, u32[]{:S(2)}, u32[]{:S(2)}) collective-permute-start(bf16[2064,128]{1,0:T(8,128)(2,1)S(1)} %get-tuple-element.21.own), channel_id=1, source_target_pairs={{0,1},{1,0},{2,3},{3,2},{8,16},{9,17},{10,18},{11,19},{16,8},{17,9... | collective-permute-start | bytes 1585160 | tf_op jit(solution)/shard_map/ppermute | solution.py:380
  6.7 17.1 %collective-permute-start.3 = (bf16[1040,128]{1,0:T(8,128)(2,1)S(1)}, bf16[1040,128]{1,0:T(8,128)(2,1)S(1)}, u32[]{:S(2)}, u32[]{:S(2)}) collective-permute-start(bf16[1040,128]{1,0:T(8,128)(2,1)S(1)} %get-tuple-element.24), channel_id=1, source_target_pairs={{0,8},{8,0},{16,24},{24,16},{1,9},{9,1},{17,25},{25,17},{2,10},{10... | collective-permute-start | bytes 798728 | tf_op jit(solution)/shard_map/ppermute | solution.py:383
  9.9 18.8 %collective-permute-start.4 = (bf16[1040,128]{1,0:T(8,128)(2,1)S(1)}, bf16[1040,128]{1,0:T(8,128)(2,1)S(1)}, u32[]{:S(2)}, u32[]{:S(2)}) collective-permute-start(bf16[1040,128]{1,0:T(8,128)(2,1)S(1)} %get-tuple-element.24), channel_id=1, source_target_pairs={{0,16},{16,24},{24,8},{8,0},{1,17},{17,25},{25,9},{9,1},{2,18},{18... | collective-permute-start | bytes 798728 | tf_op jit(solution)/shard_map/ppermute | solution.py:382
  18.2 10.6 %collective-permute-start.5 = (bf16[1040,128]{1,0:T(8,128)(2,1)S(1)}, bf16[1040,128]{1,0:T(8,128)(2,1)S(1)}, u32[]{:S(2)}, u32[]{:S(2)}) collective-permute-start(bf16[1040,128]{1,0:T(8,128)(2,1)S(1)} %get-tuple-element.23.first), channel_id=1, source_target_pairs={{0,1},{1,0},{2,3},{3,2},{8,16},{9,17},{10,18},{11,19},{16,8},{17,9... | collective-permute-start | bytes 798728 | tf_op jit(solution)/shard_map/ppermute | solution.py:386
  18.3 10.6 %collective-permute-start.7 = (bf16[1040,128]{1,0:T(8,128)(2,1)S(1)}, bf16[1040,128]{1,0:T(8,128)(2,1)S(1)}, u32[]{:S(2)}, u32[]{:S(2)}) collective-permute-start(bf16[1040,128]{1,0:T(8,128)(2,1)S(1)} %get-tuple-element.28.packs_0), channel_id=1, source_target_pairs={{0,4},{4,0},{1,5},{5,1},{2,6},{6,2},{3,7},{7,3},{8,12},{12,8},{9,1... | collective-permute-start | bytes 798728 | tf_op jit(solution)/shard_map/ppermute | solution.py:387
  29.0 2.0 %collective-permute-start.8 = (f32[256,512]{1,0:T(8,128)S(1)}, f32[256,512]{1,0:T(8,128)S(1)}, u32[]{:S(2)}, u32[]{:S(2)}) collective-permute-start(f32[256,512]{1,0:T(8,128)S(1)} %get-tuple-element.31), channel_id=1, source_target_pairs={{0,1},{1,0},{2,3},{3,2},{4,5},{5,4},{6,7},{7,6},{8,9},{9,8},{10,11... | collective-permute-start | bytes 1572872 | tf_op jit(solution)/shard_map/ppermute | solution.py:396
  29.0 10.5 %collective-permute-start.6 = (f32[256,512]{1,0:T(8,128)S(1)}, f32[256,512]{1,0:T(8,128)S(1)}, u32[]{:S(2)}, u32[]{:S(2)}) collective-permute-start(f32[256,512]{1,0:T(8,128)S(1)} %get-tuple-element.26), channel_id=1, source_target_pairs={{0,1},{1,0},{2,3},{3,2},{4,5},{5,4},{6,7},{7,6},{8,9},{9,8},{10,11... | collective-permute-start | bytes 1572872 | tf_op jit(solution)/shard_map/ppermute | solution.py:396
  31.0 15.7 %collective-permute-start.10 = (f32[128,512]{1,0:T(8,128)S(1)}, f32[128,512]{1,0:T(8,128)S(1)}, u32[]{:S(2)}, u32[]{:S(2)}) collective-permute-start(f32[128,512]{1,0:T(8,128)S(1)} %get-tuple-element.33), channel_id=1, source_target_pairs={{0,10},{1,11},{2,8},{3,9},{8,2},{9,3},{10,0},{11,1},{16,26},{17,27... | collective-permute-start | bytes 786440 | tf_op jit(solution)/shard_map/ppermute | solution.py:401
  39.5 11.5 %collective-permute-start.9 = (f32[128,512]{1,0:T(8,128)S(1)}, f32[128,512]{1,0:T(8,128)S(1)}, u32[]{:S(2)}, u32[]{:S(2)}) collective-permute-start(f32[128,512]{1,0:T(8,128)S(1)} %get-tuple-element.32), channel_id=1, source_target_pairs={{0,8},{8,0},{16,24},{24,16},{1,9},{9,1},{17,25},{25,17},{2,10},{10... | collective-permute-start | bytes 786440 | tf_op jit(solution)/shard_map/ppermute | solution.py:400
  39.6 12.1 %collective-permute-start.11 = (f32[128,512]{1,0:T(8,128)S(1)}, f32[128,512]{1,0:T(8,128)S(1)}, u32[]{:S(2)}, u32[]{:S(2)}) collective-permute-start(f32[128,512]{1,0:T(8,128)S(1)} %get-tuple-element.34), channel_id=1, source_target_pairs={{0,2},{2,0},{1,3},{3,1},{4,6},{6,4},{5,7},{7,5},{8,10},{10,8},{9,1... | collective-permute-start | bytes 786440 | tf_op jit(solution)/shard_map/ppermute | solution.py:402

commit v4 on v3

--- a/solution.py
+++ b/solution.py
@@ -121,10 +121,7 @@
     first = b_rows - second
     copies = [
         pltpu.make_async_copy(b_ref, b_out.at[pl.ds(0, b_rows)], sems.at[0]),
-        pltpu.make_async_copy(b_ref.at[pl.ds(0, first)], mixed_out.at[pl.ds(0, first)], sems.at[1]),
-        pltpu.make_async_copy(a_ref, mixed_out.at[pl.ds(first + CODE_ROWS, a_rows)], sems.at[2]),
-        pltpu.make_async_copy(b_ref.at[pl.ds(first, second)], second_out.at[pl.ds(0, second)], sems.at[3]),
-        pltpu.make_async_copy(a_ref, a_out.at[pl.ds(0, a_rows)], sems.at[4]),
+        pltpu.make_async_copy(a_ref, a_out.at[pl.ds(0, a_rows)], sems.at[1]),
     ]
     for copy in copies:
         copy.start()
@@ -142,8 +139,11 @@
     mixed_out[pl.ds(first, CODE_ROWS), :] = b_tail
     mixed_out[pl.ds(first + CODE_ROWS + a_rows, CODE_ROWS), :] = a_tail
     second_out[pl.ds(second, CODE_ROWS), :] = b_tail
-    for copy in copies:
-        copy.wait()
+    copies[0].wait()
+    mixed_out[pl.ds(0, first), :] = b_out[pl.ds(0, first), :]
+    second_out[pl.ds(0, second), :] = b_out[pl.ds(first, second), :]
+    copies[1].wait()
+    mixed_out[pl.ds(first + CODE_ROWS, a_rows), :] = a_out[pl.ds(0, a_rows), :]
 
 
 def pack(a_codes, b_codes, a_blocks, b_blocks):
@@ -163,7 +163,7 @@
         out_shape=tuple(jax.ShapeDtypeStruct((rows, width), jnp.bfloat16) for rows in sizes),
         in_specs=spaces("s", "s", "h", "h"),
         out_specs=tuple(spaces("v", "v", "v", "v")),
-        scratch_shapes=[pltpu.SemaphoreType.DMA((5,))],
+        scratch_shapes=[pltpu.SemaphoreType.DMA((2,))],
         compiler_params=pltpu.CompilerParams(vmem_limit_bytes=8 << 20),
     )(*(pltpu.with_memory_space_constraint(x, pltpu.HBM) for x in (a_codes, b_codes, a_flat, b_flat)))
 
@@ -222,14 +222,13 @@
             ] = source[pl.ds(index * width, width), :]
 
 
-def early_body(slots, own, across, first, second, far, other, dense, staged, codes, sem):
-    del other
+def early_body(slots, own, across, first, second, dense, staged, codes, sem):
     cut = first_slots(slots)
 
     @pl.when(in_middle())
     def _():
         col = lax.axis_index("col")
-        copy = fetch_codes((own, across, first, far), staged, codes, sem)
+        copy = fetch_codes((own, across, first), staged, codes, sem)
         copy.start()
         dense[...] = jnp.zeros_like(dense)
         copy.wait()
@@ -237,19 +236,18 @@
         put_blocks(dense, across, codes, 1, 0, slots, slots, col)
         put_blocks(dense, first, codes, 2, 0, cut, slots, col)
         put_blocks(dense, second, codes, 2, cut, slots - cut, slots, col)
-        put_blocks(dense, far, codes, 3, cut, slots - cut, slots, col)
-
-
-def early(own, across, first, second, far, other, slots):
+
+
+def early(own, across, first, second, slots):
     width = own.shape[1]
     return pl.pallas_call(
         functools.partial(early_body, slots),
         out_shape=jax.ShapeDtypeStruct((4 * KB * width, CB * width), jnp.bfloat16),
-        in_specs=spaces("v", "v", "v", "v", "v", "h"),
+        in_specs=spaces("v", "v", "v", "v"),
         out_specs=spaces("v")[0],
         scratch_shapes=code_scratch(),
         compiler_params=pltpu.CompilerParams(vmem_limit_bytes=12 << 20),
-    )(own, across, first, second, far, other)
+    )(own, across, first, second)
 
 
 def multiply_group(dense, total, packs, codes, slots, row):
@@ -276,7 +274,7 @@
             total[pl.ds(pl.multiple_of(spot * width, width), width), :] += part
 
 
-def own_body(a_slots, slots, packs_0, packs_1, dense_in, first,
+def end_body(a_slots, slots, packs_0, packs_1, dense_in, first, second,
              dense, keep, send, total, staged, codes, sem):
     cut = first_slots(slots)
     rows = keep.shape[0]
@@ -294,12 +292,14 @@
         copy.wait()
         col = lax.axis_index("col")
         put_blocks(dense, first, codes, 2, 0, cut, slots, col)
-        multiply_group(dense, total, (packs_0, packs_1), codes, a_slots, lax.axis_index("row"))
+        put_blocks(dense, second, codes, 2, cut, slots - cut, slots, col)
+        row = jnp.where(lax.axis_index("row") == 1, 0, 3)
+        multiply_group(dense, total, (packs_0, packs_1), codes, a_slots, row)
         keep[...] = total[pl.ds(0, rows), :]
         send[...] = total[pl.ds(rows, rows), :]
 
 
-def end_body(a_slots, packs_0, packs_1, dense, keep, send, total, staged, codes, sem):
+def own_body(a_slots, packs_0, packs_1, dense, keep, send, total, staged, codes, sem):
     rows = keep.shape[0]
 
     @pl.when(jnp.logical_not(in_middle()))
@@ -312,31 +312,30 @@
         copy = fetch_codes((packs_0, packs_1), staged, codes, sem)
         copy.start()
         copy.wait()
-        row = jnp.where(lax.axis_index("row") == 1, 0, 3)
-        multiply_group(dense, total, (packs_0, packs_1), codes, a_slots, row)
+        multiply_group(dense, total, (packs_0, packs_1), codes, a_slots, lax.axis_index("row"))
         keep[...] = total[pl.ds(0, rows), :]
         send[...] = total[pl.ds(rows, rows), :]
 
 
-def own_product(packs, dense, first, a_slots, slots):
+def end_product(packs, dense, first, second, a_slots, slots):
     width = packs[0].shape[1]
     half = jax.ShapeDtypeStruct((2 * width, CB * width), jnp.float32)
     return pl.pallas_call(
-        functools.partial(own_body, a_slots, slots),
+        functools.partial(end_body, a_slots, slots),
         out_shape=(jax.ShapeDtypeStruct(dense.shape, dense.dtype), half, half),
-        in_specs=spaces("v", "v", "v", "v"),
+        in_specs=spaces("v", "v", "v", "v", "v"),
         out_specs=tuple(spaces("v", "v", "v")),
         scratch_shapes=[pltpu.VMEM((5 * width, CB * width), jnp.float32)] + code_scratch(),
         input_output_aliases={2: 0},
         compiler_params=pltpu.CompilerParams(vmem_limit_bytes=16 << 20),
-    )(*packs, dense, first)
-
-
-def end_product(packs, dense, a_slots):
+    )(*packs, dense, first, second)
+
+
+def own_product(packs, dense, a_slots):
     width = packs[0].shape[1]
     half = jax.ShapeDtypeStruct((2 * width, CB * width), jnp.float32)
     return pl.pallas_call(
-        functools.partial(end_body, a_slots),
+        functools.partial(own_body, a_slots),
         out_shape=(half, half),
         in_specs=spaces("v", "v", "v"),
         out_specs=tuple(spaces("v", "v")),
@@ -369,9 +368,10 @@
 BEYOND = [(0, 2), (2, 3), (3, 1), (1, 0)]
 COLS = [(0, 1), (1, 0)]
 CORES = [(0, 1), (1, 0), (2, 3), (3, 2)]
-CHIPS = [(0, 2), (2, 0), (1, 3), (3, 1)]
-MIDDLE = [(r * 4 + m, (3 - r) * 4 + m if r in (1, 2) else r * 4 + (m ^ 1)) for r in range(4) for m in range(4)]
-ACROSS = [(r * 4 + m, (r ^ 1) * 4 + (m ^ 2)) for r in range(4) for m in range(4)]
+EVERY = [(r, m) for r in range(4) for m in range(4)]
+MIDDLE = [(r * 4 + m, (3 - r) * 4 + m if r in (1, 2) else r * 4 + (m ^ 1)) for r, m in EVERY]
+CHIPS = [(r * 4 + m, r * 4 + (m ^ 2 if r in (1, 2) else m ^ 1)) for r, m in EVERY]
+ACROSS = [(r * 4 + m, (r ^ 1) * 4 + (m ^ 2 if r in (1, 2) else m)) for r, m in EVERY]
 
 
 def middle_shards(a_blocks, a_codes, b_blocks, b_codes):
@@ -384,22 +384,24 @@
     a_other = lax.ppermute(a_pack, "col", COLS)
     end_first, a_end = part(end_mixed, end_mixed.shape[0] - a_pack.shape[0])
     far_first = lax.ppermute(end_first, ("row", "layer"), MIDDLE)
+    a_end, a_other = lax.optimization_barrier((a_end, a_other))
     a_end_other = lax.ppermute(a_end, "col", COLS)
 
-    dense = early(b_pack, b_across, end_first, end_second, far_second, a_other, slots)
-    dense, own_keep, own_send = own_product(
-        (a_pack, a_other), dense, far_first, a_slots, slots
-    )
-    end_keep, end_send = end_product((a_end, a_end_other), dense, a_slots)
+    dense = early(b_pack, b_across, end_first, end_second, slots)
+    dense, end_keep, end_send = end_product(
+        (a_end, a_end_other), dense, far_first, far_second, a_slots, slots
+    )
+    own_keep, own_send = own_product((a_pack, a_other), dense, a_slots)
 
     def over_cores(keep, send):
         return fold(keep, lax.ppermute(send, "layer", CORES))
 
+    end_near, end_far = over_cores(end_keep, end_send)
+    own_send, _ = lax.optimization_barrier((own_send, end_near))
     own_near, own_far = over_cores(own_keep, own_send)
-    end_near, end_far = over_cores(end_keep, end_send)
     out = own_near + lax.ppermute(end_near, "row", BESIDE)
     out = out + lax.ppermute(end_far, ("row", "layer"), ACROSS)
-    out = out + lax.ppermute(own_far, "layer", CHIPS)
+    out = out + lax.ppermute(own_far, ("row", "layer"), CHIPS)
     return out.astype(jnp.bfloat16)
 
 

time: 52.6 us -> 50.7 us (0.964)
  starting transfers between devices: 19.7 us -> 15.8 us
  waiting for transfers between devices: 29.5 us -> 31.6 us
    ppermute x1, starting transfers between devices: 8.54 us -> 0.02 us  [middle_shards(): out = out + lax.ppermute(end_far, ('row', 'layer'), ACROSS)]
    ppermute x1, waiting for transfers between devices: 6.34 us -> 13.1 us  [middle_shards(): out = out + lax.ppermute(end_far, ('row', 'layer'), ACROSS)]
    ppermute x1, starting transfers between devices: 0.01 us -> 5.57 us  [middle_shards(): out = own_near + lax.ppermute(end_near, 'row', BESIDE)]
    ppermute x1, waiting for transfers between devices: 3.51 us -> 8.46 us  [middle_shards(): end_second = lax.ppermute(b_second, 'row', BESIDE)]
    ppermute x1, waiting for transfers between devices: 4.88 us -> 0.01 us  [middle_shards(): far_second = lax.ppermute(b_second, 'row', BEYOND)]
    ppermute x1, waiting for transfers between devices: 4.39 us -> 0.01 us  [middle_shards(): out = own_near + lax.ppermute(end_near, 'row', BESIDE)]
    ppermute x1, starting transfers between devices: 3.15 us -> 0.56 us  [middle_shards(): end_second = lax.ppermute(b_second, 'row', BESIDE)]
    ppermute x1, starting transfers between devices: 0.01 us -> 2.59 us  [middle_shards(): far_second = lax.ppermute(b_second, 'row', BEYOND)]
  transfers between devices with their start and end apart: 12 -> 12, of which waited for: 7 -> 4; matrix products, arithmetic and copies ran while one was open for 0% -> 0% of each run, Pallas kernels for 1% -> 0%
where the time goes in v4:
time: 50.7 us; the launch traced here: 50.5 us
  waiting for transfers between devices  31.6 us (62%)
  starting transfers between devices  15.8 us (31%)
  Pallas kernels  2.2 us (4%)
  other arithmetic  0.73 us (1%)
    ppermute x1, waiting for transfers between devices, middle_shards(): out = out + lax.ppermute(end_far, ('row', 'layer'), ACROSS)  13.1 us
    ppermute x1, waiting for transfers between devices, middle_shards(): end_second = lax.ppermute(b_second, 'row', BESIDE)  8.46 us
    ppermute x1, waiting for transfers between devices, middle_shards(): end_mixed = lax.ppermute(mixed, 'row', BESIDE)  8.25 us
    ppermute x1, starting transfers between devices, middle_shards(): out = own_near + lax.ppermute(end_near, 'row', BESIDE)  5.57 us
    ppermute x1, starting transfers between devices, middle_shards(): end_mixed = lax.ppermute(mixed, 'row', BESIDE)  3.09 us
    ppermute x1, starting transfers between devices, middle_shards(): far_second = lax.ppermute(b_second, 'row', BEYOND)  2.59 us
    ppermute x1, starting transfers between devices, middle_shards(): a_end_other = lax.ppermute(a_end, 'col', COLS)  2.07 us
    pallas_call x1, Pallas kernels, pack(): pl.pallas_call(pack_body, out_shape=tuple((jax.ShapeDtypeStruct((rows, wi...  1.81 us
  transfers between devices with their start and end apart: 12, of which 4 were waited for; matrix products, arithmetic and copies ran while one was open for 0% of the time, Pallas kernels for 0%

profile of v4, /device:TPU:0, one launch (start us, length us, event | category | flops | bytes accessed | tf_op | source)
XLA Modules:
  0.0 50.5 jit_solution(13892355361758607466)
XLA Ops:
  0.0 1.8 %shard_map.46 = (bf16[1040,128]{1,0:T(8,128)(2,1)S(1)}, bf16[2064,128]{1,0:T(8,128)(2,1)S(1)}, bf16[2080,128]{1,0:T(8,128)(2,1)S(1)}, bf16[1040,128]{1,0:T(8,128)(2,1)S(1)}) custom-call(s32[8]{0:T(128)} %a_codes.1, s32[16]{0:T(128)} %b_codes.1, bf16[1024,128]{1,0:T(8,128)(2,1)} %bitcast.3, bf16[2048,128]{1,0:T(8,128)(2,1)} %bitcast.2), custom_call_target="tpu_custom_call" | custom-call | tf_op jit(solution)/shard_map/pallas_call | solution.py:161
  1.8 3.1 %collective-permute-start = (bf16[2080,128]{1,0:T(8,128)(2,1)S(1)}, bf16[2080,128]{1,0:T(8,128)(2,1)S(1)}, u32[]{:S(2)}, u32[]{:S(2)}) collective-permute-start(bf16[2080,128]{1,0:T(8,128)(2,1)S(1)} %get-tuple-element.24), channel_id=1, source_target_pairs={{0,8},{8,0},{16,24},{24,16},{1,9},{9,1},{17,25},{25,17},{2,10},{10... | collective-permute-start | bytes 1597448 | tf_op jit(solution)/shard_map/ppermute | solution.py:381
  4.9 1.5 %collective-permute-start.1 = (bf16[1040,128]{1,0:T(8,128)(2,1)S(1)}, bf16[1040,128]{1,0:T(8,128)(2,1)S(1)}, u32[]{:S(2)}, u32[]{:S(2)}) collective-permute-start(bf16[1040,128]{1,0:T(8,128)(2,1)S(1)} %get-tuple-element.23.packs_0), channel_id=1, source_target_pairs={{0,4},{4,0},{1,5},{5,1},{2,6},{6,2},{3,7},{7,3},{8,12},{12,8},{9,1... | collective-permute-start | bytes 798728 | tf_op jit(solution)/shard_map/ppermute | solution.py:384
  6.4 0.0 collective-permute-start.3
  6.4 2.6 %collective-permute-start.6 = (bf16[1040,128]{1,0:T(8,128)(2,1)S(1)}, bf16[1040,128]{1,0:T(8,128)(2,1)S(1)}, u32[]{:S(2)}, u32[]{:S(2)}) collective-permute-start(bf16[1040,128]{1,0:T(8,128)(2,1)S(1)} %get-tuple-element.30), channel_id=1, source_target_pairs={{0,16},{16,24},{24,8},{8,0},{1,17},{17,25},{25,9},{9,1},{2,18},{18... | collective-permute-start | bytes 798728 | tf_op jit(solution)/shard_map/ppermute | solution.py:382
  9.0 0.6 %collective-permute-start.4 = (bf16[1040,128]{1,0:T(8,128)(2,1)S(1)}, bf16[1040,128]{1,0:T(8,128)(2,1)S(1)}, u32[]{:S(2)}, u32[]{:S(2)}) collective-permute-start(bf16[1040,128]{1,0:T(8,128)(2,1)S(1)} %get-tuple-element.30), channel_id=1, source_target_pairs={{0,8},{8,0},{16,24},{24,16},{1,9},{9,1},{17,25},{25,17},{2,10},{10... | collective-permute-start | bytes 798728 | tf_op jit(solution)/shard_map/ppermute | solution.py:383
  9.6 8.2 %collective-permute-done.mixed = bf16[2080,128]{1,0:T(8,128)(2,1)S(1)} collective-permute-done((bf16[2080,128]{1,0:T(8,128)(2,1)S(1)}, bf16[2080,128]{1,0:T(8,128)(2,1)S(1)}, u32[]{:S(2)}, u32[]{:S(2)}) %collective-permute-start) | collective-permute-done | bytes 532512 | tf_op jit(solution)/shard_map/ppermute | solution.py:381
  17.9 0.0 collective-permute-done.1.packs_1
  17.9 2.1 %collective-permute-start.2 = (bf16[1040,128]{1,0:T(8,128)(2,1)S(1)}, bf16[1040,128]{1,0:T(8,128)(2,1)S(1)}, u32[]{:S(2)}, u32[]{:S(2)}) collective-permute-start(bf16[1040,128]{1,0:T(8,128)(2,1)S(1)} %get-tuple-element.27.packs_0), channel_id=1, source_target_pairs={{0,4},{4,0},{1,5},{5,1},{2,6},{6,2},{3,7},{7,3},{8,12},{12,8},{9,1... | collective-permute-start | bytes 798728 | tf_op jit(solution)/shard_map/ppermute | solution.py:388
  20.0 0.0 collective-permute-start.5
  20.0 8.5 %collective-permute-done.4.second = bf16[1040,128]{1,0:T(8,128)(2,1)S(1)} collective-permute-done((bf16[1040,128]{1,0:T(8,128)(2,1)S(1)}, bf16[1040,128]{1,0:T(8,128)(2,1)S(1)}, u32[]{:S(2)}, u32[]{:S(2)}) %collective-permute-start.4) | collective-permute-done | bytes 266272 | tf_op jit(solution)/shard_map/ppermute | solution.py:383
  28.4 0.0 collective-permute-done.3.across
  28.4 0.0 collective-permute-done.6.second
  28.5 0.0 collective-permute-done.2.packs_1
  28.5 0.0 collective-permute-done.5.first
  28.5 0.1 shard_map.49
  28.6 0.1 collective-permute-start.7
  28.7 0.1 shard_map.50
  28.8 1.8 %collective-permute-done.7.got = f32[256,512]{1,0:T(8,128)S(1)} collective-permute-done((f32[256,512]{1,0:T(8,128)S(1)}, f32[256,512]{1,0:T(8,128)S(1)}, u32[]{:S(2)}, u32[]{:S(2)}) %collective-permute-start.7) | collective-permute-done | bytes 524320 | tf_op jit(solution)/shard_map/ppermute | solution.py:397
  30.6 0.1 shard_map.51
  30.6 0.2 collective-permute-start.8
  30.8 5.6 %collective-permute-start.9 = (f32[128,512]{1,0:T(8,128)S(1)}, f32[128,512]{1,0:T(8,128)S(1)}, u32[]{:S(2)}, u32[]{:S(2)}) collective-permute-start(f32[128,512]{1,0:T(8,128)S(1)} %get-tuple-element.36), channel_id=1, source_target_pairs={{0,8},{8,0},{16,24},{24,16},{1,9},{9,1},{17,25},{25,17},{2,10},{10... | collective-permute-start | bytes 786440 | tf_op jit(solution)/shard_map/ppermute | solution.py:402
  36.4 0.0 collective-permute-start.10
  36.4 0.0 collective-permute-done.8.got
  36.4 0.1 shard_map.52
  36.5 0.1 collective-permute-start.11
  36.6 13.1 %collective-permute-done.10 = f32[128,512]{1,0:T(8,128)S(1)} collective-permute-done((f32[128,512]{1,0:T(8,128)S(1)}, f32[128,512]{1,0:T(8,128)S(1)}, u32[]{:S(2)}, u32[]{:S(2)}) %collective-permute-start.10) | collective-permute-done | bytes 262176 | tf_op jit(solution)/shard_map/ppermute | solution.py:403
  49.8 0.0 collective-permute-done.9
  49.8 0.0 collective-permute-done.11
  49.8 0.7 %add_convert_fusion = bf16[128,512]{1,0:T(8,128)(2,1)} fusion(f32[128,512]{1,0:T(8,128)S(1)} %collective-permute-done.11, f32[128,512]{1,0:T(8,128)S(1)} %collective-permute-done.10, f32[128,512]{1,0:T(8,128)S(1)} %get-tuple-element.38, f32[128,512]{1,0:T(8,128)S(1)} %collective-permute-done.9), kind=kLoop, calls=%fused_computation | loop fusion | flops 262144 | bytes 1179648 | tf_op jit(solution)/shard_map/convert_element_type | solution.py:405
  (2 shorter events, 0.0 us)
Async XLA Ops:
  1.8 16.0 %collective-permute-start = (bf16[2080,128]{1,0:T(8,128)(2,1)S(1)}, bf16[2080,128]{1,0:T(8,128)(2,1)S(1)}, u32[]{:S(2)}, u32[]{:S(2)}) collective-permute-start(bf16[2080,128]{1,0:T(8,128)(2,1)S(1)} %get-tuple-element.24), channel_id=1, source_target_pairs={{0,8},{8,0},{16,24},{24,16},{1,9},{9,1},{17,25},{25,17},{2,10},{10... | collective-permute-start | bytes 1597448 | tf_op jit(solution)/shard_map/ppermute | solution.py:381
  4.9 13.0 %collective-permute-start.1 = (bf16[1040,128]{1,0:T(8,128)(2,1)S(1)}, bf16[1040,128]{1,0:T(8,128)(2,1)S(1)}, u32[]{:S(2)}, u32[]{:S(2)}) collective-permute-start(bf16[1040,128]{1,0:T(8,128)(2,1)S(1)} %get-tuple-element.23.packs_0), channel_id=1, source_target_pairs={{0,4},{4,0},{1,5},{5,1},{2,6},{6,2},{3,7},{7,3},{8,12},{12,8},{9,1... | collective-permute-start | bytes 798728 | tf_op jit(solution)/shard_map/ppermute | solution.py:384
  6.4 22.0 %collective-permute-start.3 = (bf16[2064,128]{1,0:T(8,128)(2,1)S(1)}, bf16[2064,128]{1,0:T(8,128)(2,1)S(1)}, u32[]{:S(2)}, u32[]{:S(2)}) collective-permute-start(bf16[2064,128]{1,0:T(8,128)(2,1)S(1)} %get-tuple-element.28.own), channel_id=1, source_target_pairs={{0,1},{1,0},{2,3},{3,2},{8,16},{9,17},{10,18},{11,19},{16,8},{17,9... | collective-permute-start | bytes 1585160 | tf_op jit(solution)/shard_map/ppermute | solution.py:380
  6.4 22.0 %collective-permute-start.6 = (bf16[1040,128]{1,0:T(8,128)(2,1)S(1)}, bf16[1040,128]{1,0:T(8,128)(2,1)S(1)}, u32[]{:S(2)}, u32[]{:S(2)}) collective-permute-start(bf16[1040,128]{1,0:T(8,128)(2,1)S(1)} %get-tuple-element.30), channel_id=1, source_target_pairs={{0,16},{16,24},{24,8},{8,0},{1,17},{17,25},{25,9},{9,1},{2,18},{18... | collective-permute-start | bytes 798728 | tf_op jit(solution)/shard_map/ppermute | solution.py:382
  9.0 19.4 %collective-permute-start.4 = (bf16[1040,128]{1,0:T(8,128)(2,1)S(1)}, bf16[1040,128]{1,0:T(8,128)(2,1)S(1)}, u32[]{:S(2)}, u32[]{:S(2)}) collective-permute-start(bf16[1040,128]{1,0:T(8,128)(2,1)S(1)} %get-tuple-element.30), channel_id=1, source_target_pairs={{0,8},{8,0},{16,24},{24,16},{1,9},{9,1},{17,25},{25,17},{2,10},{10... | collective-permute-start | bytes 798728 | tf_op jit(solution)/shard_map/ppermute | solution.py:383
  17.9 10.6 %collective-permute-start.2 = (bf16[1040,128]{1,0:T(8,128)(2,1)S(1)}, bf16[1040,128]{1,0:T(8,128)(2,1)S(1)}, u32[]{:S(2)}, u32[]{:S(2)}) collective-permute-start(bf16[1040,128]{1,0:T(8,128)(2,1)S(1)} %get-tuple-element.27.packs_0), channel_id=1, source_target_pairs={{0,4},{4,0},{1,5},{5,1},{2,6},{6,2},{3,7},{7,3},{8,12},{12,8},{9,1... | collective-permute-start | bytes 798728 | tf_op jit(solution)/shard_map/ppermute | solution.py:388
  20.0 8.5 %collective-permute-start.5 = (bf16[1040,128]{1,0:T(8,128)(2,1)S(1)}, bf16[1040,128]{1,0:T(8,128)(2,1)S(1)}, u32[]{:S(2)}, u32[]{:S(2)}) collective-permute-start(bf16[1040,128]{1,0:T(8,128)(2,1)S(1)} %get-tuple-element.29.first), channel_id=1, source_target_pairs={{0,1},{1,0},{2,3},{3,2},{8,16},{9,17},{10,18},{11,19},{16,8},{17,9... | collective-permute-start | bytes 798728 | tf_op jit(solution)/shard_map/ppermute | solution.py:386
  28.6 2.0 %collective-permute-start.7 = (f32[256,512]{1,0:T(8,128)S(1)}, f32[256,512]{1,0:T(8,128)S(1)}, u32[]{:S(2)}, u32[]{:S(2)}) collective-permute-start(f32[256,512]{1,0:T(8,128)S(1)} %get-tuple-element.35), channel_id=1, source_target_pairs={{0,1},{1,0},{2,3},{3,2},{4,5},{5,4},{6,7},{7,6},{8,9},{9,8},{10,11... | collective-permute-start | bytes 1572872 | tf_op jit(solution)/shard_map/ppermute | solution.py:397
  30.6 5.8 %collective-permute-start.8 = (f32[256,512]{1,0:T(8,128)S(1)}, f32[256,512]{1,0:T(8,128)S(1)}, u32[]{:S(2)}, u32[]{:S(2)}) collective-permute-start(f32[256,512]{1,0:T(8,128)S(1)} %get-tuple-element.37), channel_id=1, source_target_pairs={{0,1},{1,0},{2,3},{3,2},{4,5},{5,4},{6,7},{7,6},{8,9},{9,8},{10,11... | collective-permute-start | bytes 1572872 | tf_op jit(solution)/shard_map/ppermute | solution.py:397
  30.8 18.9 %collective-permute-start.9 = (f32[128,512]{1,0:T(8,128)S(1)}, f32[128,512]{1,0:T(8,128)S(1)}, u32[]{:S(2)}, u32[]{:S(2)}) collective-permute-start(f32[128,512]{1,0:T(8,128)S(1)} %get-tuple-element.36), channel_id=1, source_target_pairs={{0,8},{8,0},{16,24},{24,16},{1,9},{9,1},{17,25},{25,17},{2,10},{10... | collective-permute-start | bytes 786440 | tf_op jit(solution)/shard_map/ppermute | solution.py:402
  36.4 13.3 %collective-permute-start.10 = (f32[128,512]{1,0:T(8,128)S(1)}, f32[128,512]{1,0:T(8,128)S(1)}, u32[]{:S(2)}, u32[]{:S(2)}) collective-permute-start(f32[128,512]{1,0:T(8,128)S(1)} %get-tuple-element.39), channel_id=1, source_target_pairs={{0,8},{1,9},{2,10},{3,11},{8,2},{9,3},{10,0},{11,1},{16,26},{17,27... | collective-permute-start | bytes 786440 | tf_op jit(solution)/shard_map/ppermute | solution.py:403
  36.5 13.3 %collective-permute-start.11 = (f32[128,512]{1,0:T(8,128)S(1)}, f32[128,512]{1,0:T(8,128)S(1)}, u32[]{:S(2)}, u32[]{:S(2)}) collective-permute-start(f32[128,512]{1,0:T(8,128)S(1)} %get-tuple-element.40), channel_id=1, source_target_pairs={{0,1},{1,0},{2,3},{3,2},{8,10},{9,11},{10,8},{11,9},{16,18},{17,19... | collective-permute-start | bytes 786440 | tf_op jit(solution)/shard_map/ppermute | solution.py:404

commit v5 on v4

--- a/solution.py
+++ b/solution.py
@@ -99,6 +99,7 @@
 
 CODE_ROWS = 16
 FIRST = 8
+CUT = 2
 
 
 def middle_plan(mesh_shape):
@@ -250,14 +251,13 @@
     )(own, across, first, second)
 
 
-def multiply_group(dense, total, packs, codes, slots, row):
+def multiply_group(dense, total, packs, codes, line, slots, row):
     width = packs[0].shape[1]
     pieces, owners = 2, 2
     core = lax.rem(lax.axis_index("layer"), 2)
-    total[...] = jnp.zeros_like(total)
     for source in range(2):
         for slot in range(slots):
-            code = codes[source, slot]
+            code = codes[line + source, slot]
             live = (code >= 0).astype(jnp.int32)
             safe = jnp.maximum(code, 0)
             owner = slot // (slots // owners)
@@ -274,10 +274,11 @@
             total[pl.ds(pl.multiple_of(spot * width, width), width), :] += part
 
 
-def end_body(a_slots, slots, packs_0, packs_1, dense_in, first, second,
-             dense, keep, send, total, staged, codes, sem):
+def product_body(a_slots, slots, first_column, own_0, own_1, end_0, end_1, dense_in, first, second,
+                 dense, keep, send, total, staged, codes, sem):
     cut = first_slots(slots)
-    rows = keep.shape[0]
+    rows, columns = keep.shape[0] // 2, keep.shape[1]
+    place = first_column > 0
     del dense_in
 
     @pl.when(jnp.logical_not(in_middle()))
@@ -287,81 +288,87 @@
 
     @pl.when(in_middle())
     def _():
-        copy = fetch_codes((packs_0, packs_1, first), staged, codes, sem)
+        copy = fetch_codes((end_0, end_1, own_0, own_1, first), staged, codes, sem)
         copy.start()
+        total[...] = jnp.zeros_like(total)
         copy.wait()
-        col = lax.axis_index("col")
-        put_blocks(dense, first, codes, 2, 0, cut, slots, col)
-        put_blocks(dense, second, codes, 2, cut, slots - cut, slots, col)
-        row = jnp.where(lax.axis_index("row") == 1, 0, 3)
-        multiply_group(dense, total, (packs_0, packs_1), codes, a_slots, row)
-        keep[...] = total[pl.ds(0, rows), :]
-        send[...] = total[pl.ds(rows, rows), :]
-
-
-def own_body(a_slots, packs_0, packs_1, dense, keep, send, total, staged, codes, sem):
-    rows = keep.shape[0]
-
-    @pl.when(jnp.logical_not(in_middle()))
-    def _():
-        keep[...] = jnp.zeros_like(keep)
-        send[...] = jnp.zeros_like(send)
-
-    @pl.when(in_middle())
-    def _():
-        copy = fetch_codes((packs_0, packs_1), staged, codes, sem)
-        copy.start()
-        copy.wait()
-        multiply_group(dense, total, (packs_0, packs_1), codes, a_slots, lax.axis_index("row"))
-        keep[...] = total[pl.ds(0, rows), :]
-        send[...] = total[pl.ds(rows, rows), :]
-
-
-def end_product(packs, dense, first, second, a_slots, slots):
-    width = packs[0].shape[1]
-    half = jax.ShapeDtypeStruct((2 * width, CB * width), jnp.float32)
-    return pl.pallas_call(
-        functools.partial(end_body, a_slots, slots),
+        col, row = lax.axis_index("col"), lax.axis_index("row")
+        if place:
+            put_blocks(dense, first, codes, 4, 0, cut, slots, col)
+            put_blocks(dense, second, codes, 4, cut, slots - cut, slots, col)
+        next_row = jnp.where(row == 1, 0, 3)
+        part = dense.at[:, pl.ds(first_column, columns)]
+        multiply_group(part, total.at[0], (end_0, end_1), codes, 0, a_slots, next_row)
+        multiply_group(part, total.at[1], (own_0, own_1), codes, 2, a_slots, row)
+        for group in range(2):
+            keep[pl.ds(group * rows, rows), :] = total[group, pl.ds(0, rows), :]
+            send[pl.ds(group * rows, rows), :] = total[group, pl.ds(rows, rows), :]
+
+
+def product(own, end, dense, first, second, first_column, columns, a_slots, slots):
+    width = own[0].shape[1]
+    half = jax.ShapeDtypeStruct((4 * width, columns), jnp.float32)
+    return pl.pallas_call(
+        functools.partial(product_body, a_slots, slots, first_column),
         out_shape=(jax.ShapeDtypeStruct(dense.shape, dense.dtype), half, half),
-        in_specs=spaces("v", "v", "v", "v", "v"),
-        out_specs=tuple(spaces("v", "v", "v")),
-        scratch_shapes=[pltpu.VMEM((5 * width, CB * width), jnp.float32)] + code_scratch(),
-        input_output_aliases={2: 0},
-        compiler_params=pltpu.CompilerParams(vmem_limit_bytes=16 << 20),
-    )(*packs, dense, first, second)
-
-
-def own_product(packs, dense, a_slots):
-    width = packs[0].shape[1]
-    half = jax.ShapeDtypeStruct((2 * width, CB * width), jnp.float32)
-    return pl.pallas_call(
-        functools.partial(own_body, a_slots),
-        out_shape=(half, half),
-        in_specs=spaces("v", "v", "v"),
-        out_specs=tuple(spaces("v", "v")),
-        scratch_shapes=[pltpu.VMEM((5 * width, CB * width), jnp.float32)] + code_scratch(),
-        compiler_params=pltpu.CompilerParams(vmem_limit_bytes=16 << 20),
-    )(*packs, dense)
-
-
-def fold_body(keep, got, near, far):
-    rows = near.shape[0]
+        in_specs=spaces(*"vvvvvvv"),
+        out_specs=tuple(spaces(*"vvv")),
+        scratch_shapes=[pltpu.VMEM((2, 5 * width, columns), jnp.float32)] + code_scratch(),
+        input_output_aliases={4: 0},
+        compiler_params=pltpu.CompilerParams(vmem_limit_bytes=20 << 20),
+    )(*own, *end, dense, first, second)
+
+
+def fold_body(keep, got, end_near, end_far, own_near, own_far):
+    rows = end_near.shape[0]
     chip = lax.axis_index("layer") // 2
-    for out, index in ((near, chip), (far, 1 - chip)):
-        block = pl.ds(pl.multiple_of(index * rows, rows), rows)
-        out[...] = keep[block, :] + got[block, :]
+    for first, near, far in ((0, end_near, end_far), (2 * rows, own_near, own_far)):
+        for out, index in ((near, chip), (far, 1 - chip)):
+            block = pl.ds(pl.multiple_of(first + index * rows, rows), rows)
+            out[...] = keep[block, :] + got[block, :]
 
 
 def fold(keep, got):
-    rows, width = keep.shape
-    half = jax.ShapeDtypeStruct((rows // 2, width), keep.dtype)
+    part = jax.ShapeDtypeStruct((keep.shape[0] // 4, keep.shape[1]), jnp.float32)
     return pl.pallas_call(
         fold_body,
-        out_shape=(half, half),
+        out_shape=(part,) * 4,
+        in_specs=spaces(*"vv"),
+        out_specs=tuple(spaces(*"vvvv")),
+        compiler_params=pltpu.CompilerParams(vmem_limit_bytes=8 << 20),
+    )(keep, got)
+
+
+def settle_body(near, got, out):
+    out[...] = (near[...] + got[...]).astype(out.dtype)
+
+
+def settle(near, got):
+    return pl.pallas_call(
+        settle_body,
+        out_shape=jax.ShapeDtypeStruct(near.shape, jnp.bfloat16),
         in_specs=spaces("v", "v"),
-        out_specs=tuple(spaces("v", "v")),
+        out_specs=spaces("v")[0],
         compiler_params=pltpu.CompilerParams(vmem_limit_bytes=4 << 20),
-    )(keep, got)
+    )(near, got)
+
+
+def finish_body(left, left_got, right, right_got, near, far, settled, out):
+    cut = left.shape[1]
+    out[:, pl.ds(0, cut)] = ((left[...] + left_got[...]) + (near[...] + far[...])).astype(out.dtype)
+    rest = (right[...] + right_got[...]) + settled[...].astype(jnp.float32)
+    out[:, pl.ds(cut, rest.shape[1])] = rest.astype(out.dtype)
+
+
+def finish(*parts):
+    shape = (parts[0].shape[0], parts[0].shape[1] + parts[2].shape[1])
+    return pl.pallas_call(
+        finish_body,
+        out_shape=jax.ShapeDtypeStruct(shape, jnp.bfloat16),
+        in_specs=spaces(*"vvvvvvv"),
+        out_specs=spaces("v")[0],
+        compiler_params=pltpu.CompilerParams(vmem_limit_bytes=4 << 20),
+    )(*parts)
 
 
 BESIDE = [(0, 1), (1, 0), (2, 3), (3, 2)]
@@ -380,29 +387,31 @@
     b_across = lax.ppermute(b_pack, ("row", "layer"), MIDDLE)
     end_mixed = lax.ppermute(mixed, "row", BESIDE)
     far_second = lax.ppermute(b_second, "row", BEYOND)
-    end_second = lax.ppermute(b_second, "row", BESIDE)
     a_other = lax.ppermute(a_pack, "col", COLS)
+    b_late, a_other = lax.optimization_barrier((b_second, a_other))
+    end_second = lax.ppermute(b_late, "row", BESIDE)
     end_first, a_end = part(end_mixed, end_mixed.shape[0] - a_pack.shape[0])
     far_first = lax.ppermute(end_first, ("row", "layer"), MIDDLE)
     a_end, a_other = lax.optimization_barrier((a_end, a_other))
     a_end_other = lax.ppermute(a_end, "col", COLS)
 
     dense = early(b_pack, b_across, end_first, end_second, slots)
-    dense, end_keep, end_send = end_product(
-        (a_end, a_end_other), dense, far_first, far_second, a_slots, slots
-    )
-    own_keep, own_send = own_product((a_pack, a_other), dense, a_slots)
-
-    def over_cores(keep, send):
-        return fold(keep, lax.ppermute(send, "layer", CORES))
-
-    end_near, end_far = over_cores(end_keep, end_send)
-    own_send, _ = lax.optimization_barrier((own_send, end_near))
-    own_near, own_far = over_cores(own_keep, own_send)
-    out = own_near + lax.ppermute(end_near, "row", BESIDE)
-    out = out + lax.ppermute(end_far, ("row", "layer"), ACROSS)
-    out = out + lax.ppermute(own_far, ("row", "layer"), CHIPS)
-    return out.astype(jnp.bfloat16)
+    columns = CB * a_blocks.shape[1]
+    cut = columns * CUT // 4
+    own, end = (a_pack, a_other), (a_end, a_end_other)
+    dense, keep, send = product(own, end, dense, far_first, far_second, cut, columns - cut, a_slots, slots)
+    got = lax.ppermute(send, "layer", CORES)
+    _, left_keep, left_send = product(own, end, dense, far_first, far_second, 0, cut, a_slots, slots)
+    left_got = lax.ppermute(left_send, "layer", CORES)
+    rest_near, rest_far, right, right_far = fold(keep, got)
+    rest_got = lax.ppermute(rest_far, ("row", "layer"), CHIPS)
+    settled = lax.ppermute(settle(rest_near, rest_got), "row", BESIDE)
+    right_got = lax.ppermute(right_far, ("row", "layer"), CHIPS)
+    near, far, left, left_far = fold(left_keep, left_got)
+    got_near = lax.ppermute(near, "row", BESIDE)
+    got_far = lax.ppermute(far, ("row", "layer"), ACROSS)
+    left_got = lax.ppermute(left_far, ("row", "layer"), CHIPS)
+    return finish(left, left_got, right, right_got, got_near, got_far, settled)
 
 
 def solution(mesh):

time: 50.7 us -> 47.6 us (0.939)
  waiting for transfers between devices: 31.6 us -> 21.9 us
  starting transfers between devices: 15.8 us -> 22.6 us
  other arithmetic: 0.73 us -> 0 us
  Pallas kernels: 2.2 us -> 2.89 us
    ppermute x6 -> x9, waiting for transfers between devices: 23.4 us -> 13.4 us  [the longest x1 8.47 us: middle_shards(): end_second = lax.ppermute(b_late, 'row', BESIDE)]
    ppermute x6 -> x9, starting transfers between devices: 6.57 us -> 13.4 us  [the longest x1 7.57 us: middle_shards(): got_near = lax.ppermute(near, 'row', BESIDE)]
    ppermute x1, waiting for transfers between devices: 0.01 us -> 3.74 us  [middle_shards(): a_other = lax.ppermute(a_pack, 'col', COLS)]
    ppermute x1, waiting for transfers between devices: 8.25 us -> 4.71 us  [middle_shards(): end_mixed = lax.ppermute(mixed, 'row', BESIDE)]
    convert_element_type x1 -> x0, other arithmetic: 0.73 us -> none  [middle_shards(): return out.astype(jnp.bfloat16)]
    pallas_call x4 -> x6, Pallas kernels: 0.34 us -> 1.03 us  [the longest x1 0.7 us: finish(): pl.pallas_call(finish_body, out_shape=jax.ShapeDtypeStruct(shape, jnp.bfl...]
  transfers between devices with their start and end apart: 12 -> 15, of which waited for: 4 -> 6; matrix products, arithmetic and copies ran while one was open for 0% -> 0% of each run, Pallas kernels for 0% -> 1%
where the time goes in v5:
time: 47.6 us; the launch traced here: 47.5 us
  starting transfers between devices  22.6 us (47%)
  waiting for transfers between devices  21.9 us (46%)
  Pallas kernels  2.89 us (6%)
    ppermute x1, waiting for transfers between devices, middle_shards(): end_second = lax.ppermute(b_late, 'row', BESIDE)  8.47 us
    ppermute x1, starting transfers between devices, middle_shards(): got_near = lax.ppermute(near, 'row', BESIDE)  7.57 us
    ppermute x1, waiting for transfers between devices, middle_shards(): end_mixed = lax.ppermute(mixed, 'row', BESIDE)  4.71 us
    ppermute x1, starting transfers between devices, middle_shards(): settled = lax.ppermute(settle(rest_near, rest_got), 'row', BESIDE)  4.18 us
    ppermute x1, waiting for transfers between devices, middle_shards(): a_other = lax.ppermute(a_pack, 'col', COLS)  3.74 us
    ppermute x1, waiting for transfers between devices, middle_shards(): got_far = lax.ppermute(far, ('row', 'layer'), ACROSS)  3.55 us
    ppermute x1, starting transfers between devices, middle_shards(): end_mixed = lax.ppermute(mixed, 'row', BESIDE)  3.09 us
    ppermute x1, starting transfers between devices, middle_shards(): far_second = lax.ppermute(b_second, 'row', BEYOND)  2.59 us
  transfers between devices with their start and end apart: 15, of which 6 were waited for; matrix products, arithmetic and copies ran while one was open for 0% of the time, Pallas kernels for 1%

profile of v5, /device:TPU:0, one launch (start us, length us, event | category | flops | bytes accessed | tf_op | source)
XLA Modules:
  0.0 47.5 jit_solution(15111071602538223505)
XLA Ops:
  0.0 1.8 %shard_map.46 = (bf16[1040,128]{1,0:T(8,128)(2,1)S(1)}, bf16[2064,128]{1,0:T(8,128)(2,1)S(1)}, bf16[2080,128]{1,0:T(8,128)(2,1)S(1)}, bf16[1040,128]{1,0:T(8,128)(2,1)S(1)}) custom-call(s32[8]{0:T(128)} %a_codes.1, s32[16]{0:T(128)} %b_codes.1, bf16[1024,128]{1,0:T(8,128)(2,1)} %bitcast.3, bf16[2048,128]{1,0:T(8,128)(2,1)} %bitcast.2), custom_call_target="tpu_custom_call" | custom-call | tf_op jit(solution)/shard_map/pallas_call | solution.py:162
  1.8 3.1 %collective-permute-start = (bf16[2080,128]{1,0:T(8,128)(2,1)S(1)}, bf16[2080,128]{1,0:T(8,128)(2,1)S(1)}, u32[]{:S(2)}, u32[]{:S(2)}) collective-permute-start(bf16[2080,128]{1,0:T(8,128)(2,1)S(1)} %get-tuple-element.29), channel_id=1, source_target_pairs={{0,8},{8,0},{16,24},{24,16},{1,9},{9,1},{17,25},{25,17},{2,10},{10... | collective-permute-start | bytes 1597448 | tf_op jit(solution)/shard_map/ppermute | solution.py:388
  4.9 1.5 %collective-permute-start.1 = (bf16[1040,128]{1,0:T(8,128)(2,1)S(1)}, bf16[1040,128]{1,0:T(8,128)(2,1)S(1)}, u32[]{:S(2)}, u32[]{:S(2)}) collective-permute-start(bf16[1040,128]{1,0:T(8,128)(2,1)S(1)} %get-tuple-element.28.own_0), channel_id=1, source_target_pairs={{0,4},{4,0},{1,5},{5,1},{2,6},{6,2},{3,7},{7,3},{8,12},{12,8},{9,1... | collective-permute-start | bytes 798728 | tf_op jit(solution)/shard_map/ppermute | solution.py:390
  6.4 0.0 collective-permute-start.3
  6.4 2.6 %collective-permute-start.6 = (bf16[1040,128]{1,0:T(8,128)(2,1)S(1)}, bf16[1040,128]{1,0:T(8,128)(2,1)S(1)}, u32[]{:S(2)}, u32[]{:S(2)}) collective-permute-start(bf16[1040,128]{1,0:T(8,128)(2,1)S(1)} %get-tuple-element.37), channel_id=1, source_target_pairs={{0,16},{16,24},{24,8},{8,0},{1,17},{17,25},{25,9},{9,1},{2,18},{18... | collective-permute-start | bytes 798728 | tf_op jit(solution)/shard_map/ppermute | solution.py:389
  9.0 3.7 %collective-permute-done.1.own_1 = bf16[1040,128]{1,0:T(8,128)(2,1)S(1)} collective-permute-done((bf16[1040,128]{1,0:T(8,128)(2,1)S(1)}, bf16[1040,128]{1,0:T(8,128)(2,1)S(1)}, u32[]{:S(2)}, u32[]{:S(2)}) %collective-permute-start.1) | collective-permute-done | bytes 266272 | tf_op jit(solution)/shard_map/ppermute | solution.py:390
  12.8 0.4 collective-permute-start.4
  13.1 4.7 %collective-permute-done.mixed = bf16[2080,128]{1,0:T(8,128)(2,1)S(1)} collective-permute-done((bf16[2080,128]{1,0:T(8,128)(2,1)S(1)}, bf16[2080,128]{1,0:T(8,128)(2,1)S(1)}, u32[]{:S(2)}, u32[]{:S(2)}) %collective-permute-start) | collective-permute-done | bytes 532512 | tf_op jit(solution)/shard_map/ppermute | solution.py:388
  17.9 2.1 %collective-permute-start.2 = (bf16[1040,128]{1,0:T(8,128)(2,1)S(1)}, bf16[1040,128]{1,0:T(8,128)(2,1)S(1)}, u32[]{:S(2)}, u32[]{:S(2)}) collective-permute-start(bf16[1040,128]{1,0:T(8,128)(2,1)S(1)} %get-tuple-element.34.end_0), channel_id=1, source_target_pairs={{0,4},{4,0},{1,5},{5,1},{2,6},{6,2},{3,7},{7,3},{8,12},{12,8},{9,1... | collective-permute-start | bytes 798728 | tf_op jit(solution)/shard_map/ppermute | solution.py:396
  19.9 0.0 collective-permute-start.5
  19.9 0.0 collective-permute-done.3.across
  19.9 8.5 %collective-permute-done.4.second = bf16[1040,128]{1,0:T(8,128)(2,1)S(1)} collective-permute-done((bf16[1040,128]{1,0:T(8,128)(2,1)S(1)}, bf16[1040,128]{1,0:T(8,128)(2,1)S(1)}, u32[]{:S(2)}, u32[]{:S(2)}) %collective-permute-start.4) | collective-permute-done | bytes 266272 | tf_op jit(solution)/shard_map/ppermute | solution.py:392
  28.4 0.0 collective-permute-done.6.second
  28.5 0.0 collective-permute-done.5.first
  28.5 0.1 shard_map.49
  28.6 0.1 collective-permute-start.9
  28.7 0.1 shard_map.50
  28.8 0.5 %collective-permute-start.7 = (f32[512,256]{1,0:T(8,128)S(1)}, f32[512,256]{1,0:T(8,128)S(1)}, u32[]{:S(2)}, u32[]{:S(2)}) collective-permute-start(f32[512,256]{1,0:T(8,128)S(1)} %get-tuple-element.40), channel_id=1, source_target_pairs={{0,1},{1,0},{2,3},{3,2},{4,5},{5,4},{6,7},{7,6},{8,9},{9,8},{10,11... | collective-permute-start | bytes 1572872 | tf_op jit(solution)/shard_map/ppermute | solution.py:405
  29.3 1.2 %collective-permute-done.9.got = f32[512,256]{1,0:T(8,128)S(1)} collective-permute-done((f32[512,256]{1,0:T(8,128)S(1)}, f32[512,256]{1,0:T(8,128)S(1)}, u32[]{:S(2)}, u32[]{:S(2)}) %collective-permute-start.9) | collective-permute-done | bytes 524320 | tf_op jit(solution)/shard_map/ppermute | solution.py:403
  30.6 0.1 shard_map.52
  30.6 0.2 collective-permute-start.13
  30.8 0.4 collective-permute-start.10
  31.2 0.1 collective-permute-done.7.got
  31.3 0.1 shard_map.51
  31.4 7.6 %collective-permute-start.11 = (f32[128,256]{1,0:T(8,128)S(1)}, f32[128,256]{1,0:T(8,128)S(1)}, u32[]{:S(2)}, u32[]{:S(2)}) collective-permute-start(f32[128,256]{1,0:T(8,128)S(1)} %get-tuple-element.47), channel_id=1, source_target_pairs={{0,8},{8,0},{16,24},{24,16},{1,9},{9,1},{17,25},{25,17},{2,10},{10... | collective-permute-start | bytes 393224 | tf_op jit(solution)/shard_map/ppermute | solution.py:411
  38.9 0.1 collective-permute-start.12
  39.0 4.2 %collective-permute-start.14 = (bf16[128,256]{1,0:T(8,128)(2,1)S(1)}, bf16[128,256]{1,0:T(8,128)(2,1)S(1)}, u32[]{:S(2)}, u32[]{:S(2)}) collective-permute-start(bf16[128,256]{1,0:T(8,128)(2,1)S(1)} %shard_map.53), channel_id=1, source_target_pairs={{0,8},{8,0},{16,24},{24,16},{1,9},{9,1},{17,25},{25,17},{2,10},{10... | collective-permute-start | bytes 196616 | tf_op jit(solution)/shard_map/ppermute | solution.py:408
  43.2 0.0 collective-permute-done.10.right_got
  43.2 0.0 collective-permute-done.11.near
  43.2 3.5 %collective-permute-done.12.far = f32[128,256]{1,0:T(8,128)S(1)} collective-permute-done((f32[128,256]{1,0:T(8,128)S(1)}, f32[128,256]{1,0:T(8,128)S(1)}, u32[]{:S(2)}, u32[]{:S(2)}) %collective-permute-start.12) | collective-permute-done | bytes 131104 | tf_op jit(solution)/shard_map/ppermute | solution.py:412
  46.8 0.0 collective-permute-done.8.left_got
  46.8 0.7 %shard_map.54 = bf16[128,512]{1,0:T(8,128)(2,1)} custom-call(f32[128,256]{1,0:T(8,128)S(1)} %get-tuple-element.41.left, f32[128,256]{1,0:T(8,128)S(1)} %collective-permute-done.8.left_got, f32[128,256]{1,0:T(8,128)S(1)} %get-tuple-element.45.right, f32[128,256]{1,0:T(8,128)S(1)} %collective-permute-done.10.right_got, ...), custom_call_target="tpu_custom_call" | custom-call | tf_op jit(solution)/shard_map/pallas_call | solution.py:365
  (7 shorter events, 0.1 us)
Async XLA Ops:
  1.8 16.0 %collective-permute-start = (bf16[2080,128]{1,0:T(8,128)(2,1)S(1)}, bf16[2080,128]{1,0:T(8,128)(2,1)S(1)}, u32[]{:S(2)}, u32[]{:S(2)}) collective-permute-start(bf16[2080,128]{1,0:T(8,128)(2,1)S(1)} %get-tuple-element.29), channel_id=1, source_target_pairs={{0,8},{8,0},{16,24},{24,16},{1,9},{9,1},{17,25},{25,17},{2,10},{10... | collective-permute-start | bytes 1597448 | tf_op jit(solution)/shard_map/ppermute | solution.py:388
  4.9 7.9 %collective-permute-start.1 = (bf16[1040,128]{1,0:T(8,128)(2,1)S(1)}, bf16[1040,128]{1,0:T(8,128)(2,1)S(1)}, u32[]{:S(2)}, u32[]{:S(2)}) collective-permute-start(bf16[1040,128]{1,0:T(8,128)(2,1)S(1)} %get-tuple-element.28.own_0), channel_id=1, source_target_pairs={{0,4},{4,0},{1,5},{5,1},{2,6},{6,2},{3,7},{7,3},{8,12},{12,8},{9,1... | collective-permute-start | bytes 798728 | tf_op jit(solution)/shard_map/ppermute | solution.py:390
  6.4 13.5 %collective-permute-start.3 = (bf16[2064,128]{1,0:T(8,128)(2,1)S(1)}, bf16[2064,128]{1,0:T(8,128)(2,1)S(1)}, u32[]{:S(2)}, u32[]{:S(2)}) collective-permute-start(bf16[2064,128]{1,0:T(8,128)(2,1)S(1)} %get-tuple-element.35.own), channel_id=1, source_target_pairs={{0,1},{1,0},{2,3},{3,2},{8,16},{9,17},{10,18},{11,19},{16,8},{17,9... | collective-permute-start | bytes 1585160 | tf_op jit(solution)/shard_map/ppermute | solution.py:387
  6.4 22.0 %collective-permute-start.6 = (bf16[1040,128]{1,0:T(8,128)(2,1)S(1)}, bf16[1040,128]{1,0:T(8,128)(2,1)S(1)}, u32[]{:S(2)}, u32[]{:S(2)}) collective-permute-start(bf16[1040,128]{1,0:T(8,128)(2,1)S(1)} %get-tuple-element.37), channel_id=1, source_target_pairs={{0,16},{16,24},{24,8},{8,0},{1,17},{17,25},{25,9},{9,1},{2,18},{18... | collective-permute-start | bytes 798728 | tf_op jit(solution)/shard_map/ppermute | solution.py:389
  12.8 15.7 %collective-permute-start.4 = (bf16[1040,128]{1,0:T(8,128)(2,1)S(1)}, bf16[1040,128]{1,0:T(8,128)(2,1)S(1)}, u32[]{:S(2)}, u32[]{:S(2)}) collective-permute-start(bf16[1040,128]{1,0:T(8,128)(2,1)S(1)} %get-tuple-element.37), channel_id=1, source_target_pairs={{0,8},{8,0},{16,24},{24,16},{1,9},{9,1},{17,25},{25,17},{2,10},{10... | collective-permute-start | bytes 798728 | tf_op jit(solution)/shard_map/ppermute | solution.py:392
  17.9 10.6 %collective-permute-start.2 = (bf16[1040,128]{1,0:T(8,128)(2,1)S(1)}, bf16[1040,128]{1,0:T(8,128)(2,1)S(1)}, u32[]{:S(2)}, u32[]{:S(2)}) collective-permute-start(bf16[1040,128]{1,0:T(8,128)(2,1)S(1)} %get-tuple-element.34.end_0), channel_id=1, source_target_pairs={{0,4},{4,0},{1,5},{5,1},{2,6},{6,2},{3,7},{7,3},{8,12},{12,8},{9,1... | collective-permute-start | bytes 798728 | tf_op jit(solution)/shard_map/ppermute | solution.py:396
  19.9 8.5 %collective-permute-start.5 = (bf16[1040,128]{1,0:T(8,128)(2,1)S(1)}, bf16[1040,128]{1,0:T(8,128)(2,1)S(1)}, u32[]{:S(2)}, u32[]{:S(2)}) collective-permute-start(bf16[1040,128]{1,0:T(8,128)(2,1)S(1)} %get-tuple-element.36.first), channel_id=1, source_target_pairs={{0,1},{1,0},{2,3},{3,2},{8,16},{9,17},{10,18},{11,19},{16,8},{17,9... | collective-permute-start | bytes 798728 | tf_op jit(solution)/shard_map/ppermute | solution.py:394
  28.6 2.0 %collective-permute-start.9 = (f32[512,256]{1,0:T(8,128)S(1)}, f32[512,256]{1,0:T(8,128)S(1)}, u32[]{:S(2)}, u32[]{:S(2)}) collective-permute-start(f32[512,256]{1,0:T(8,128)S(1)} %get-tuple-element.44), channel_id=1, source_target_pairs={{0,1},{1,0},{2,3},{3,2},{4,5},{5,4},{6,7},{7,6},{8,9},{9,8},{10,11... | collective-permute-start | bytes 1572872 | tf_op jit(solution)/shard_map/ppermute | solution.py:403
  28.8 2.5 %collective-permute-start.7 = (f32[512,256]{1,0:T(8,128)S(1)}, f32[512,256]{1,0:T(8,128)S(1)}, u32[]{:S(2)}, u32[]{:S(2)}) collective-permute-start(f32[512,256]{1,0:T(8,128)S(1)} %get-tuple-element.40), channel_id=1, source_target_pairs={{0,1},{1,0},{2,3},{3,2},{4,5},{5,4},{6,7},{7,6},{8,9},{9,8},{10,11... | collective-permute-start | bytes 1572872 | tf_op jit(solution)/shard_map/ppermute | solution.py:405
  30.6 8.4 %collective-permute-start.13 = (f32[128,256]{1,0:T(8,128)S(1)}, f32[128,256]{1,0:T(8,128)S(1)}, u32[]{:S(2)}, u32[]{:S(2)}) collective-permute-start(f32[128,256]{1,0:T(8,128)S(1)} %get-tuple-element.50), channel_id=1, source_target_pairs={{0,1},{1,0},{2,3},{3,2},{8,10},{9,11},{10,8},{11,9},{16,18},{17,19... | collective-permute-start | bytes 393224 | tf_op jit(solution)/shard_map/ppermute | solution.py:407
  30.8 12.4 %collective-permute-start.10 = (f32[128,256]{1,0:T(8,128)S(1)}, f32[128,256]{1,0:T(8,128)S(1)}, u32[]{:S(2)}, u32[]{:S(2)}) collective-permute-start(f32[128,256]{1,0:T(8,128)S(1)} %get-tuple-element.46), channel_id=1, source_target_pairs={{0,1},{1,0},{2,3},{3,2},{8,10},{9,11},{10,8},{11,9},{16,18},{17,19... | collective-permute-start | bytes 393224 | tf_op jit(solution)/shard_map/ppermute | solution.py:409
  31.4 11.9 %collective-permute-start.11 = (f32[128,256]{1,0:T(8,128)S(1)}, f32[128,256]{1,0:T(8,128)S(1)}, u32[]{:S(2)}, u32[]{:S(2)}) collective-permute-start(f32[128,256]{1,0:T(8,128)S(1)} %get-tuple-element.47), channel_id=1, source_target_pairs={{0,8},{8,0},{16,24},{24,16},{1,9},{9,1},{17,25},{25,17},{2,10},{10... | collective-permute-start | bytes 393224 | tf_op jit(solution)/shard_map/ppermute | solution.py:411
  38.9 7.8 %collective-permute-start.12 = (f32[128,256]{1,0:T(8,128)S(1)}, f32[128,256]{1,0:T(8,128)S(1)}, u32[]{:S(2)}, u32[]{:S(2)}) collective-permute-start(f32[128,256]{1,0:T(8,128)S(1)} %get-tuple-element.48), channel_id=1, source_target_pairs={{0,8},{1,9},{2,10},{3,11},{8,2},{9,3},{10,0},{11,1},{16,26},{17,27... | collective-permute-start | bytes 393224 | tf_op jit(solution)/shard_map/ppermute | solution.py:412
  39.0 7.8 %collective-permute-start.8 = (f32[128,256]{1,0:T(8,128)S(1)}, f32[128,256]{1,0:T(8,128)S(1)}, u32[]{:S(2)}, u32[]{:S(2)}) collective-permute-start(f32[128,256]{1,0:T(8,128)S(1)} %get-tuple-element.42), channel_id=1, source_target_pairs={{0,1},{1,0},{2,3},{3,2},{8,10},{9,11},{10,8},{11,9},{16,18},{17,19... | collective-permute-start | bytes 393224 | tf_op jit(solution)/shard_map/ppermute | solution.py:413
  39.0 7.7 %collective-permute-start.14 = (bf16[128,256]{1,0:T(8,128)(2,1)S(1)}, bf16[128,256]{1,0:T(8,128)(2,1)S(1)}, u32[]{:S(2)}, u32[]{:S(2)}) collective-permute-start(bf16[128,256]{1,0:T(8,128)(2,1)S(1)} %shard_map.53), channel_id=1, source_target_pairs={{0,8},{8,0},{16,24},{24,16},{1,9},{9,1},{17,25},{25,17},{2,10},{10... | collective-permute-start | bytes 196616 | tf_op jit(solution)/shard_map/ppermute | solution.py:408

commit v6 on v5

--- a/solution.py
+++ b/solution.py
@@ -136,7 +136,8 @@
 
     a_tail, b_tail = code_rows(a_codes), code_rows(b_codes)
     a_out[pl.ds(a_rows, CODE_ROWS), :] = a_tail
-    b_out[pl.ds(b_rows, CODE_ROWS), :] = b_tail
+    for index in range(3):
+        b_out[pl.ds(b_rows + index * CODE_ROWS, CODE_ROWS), :] = b_tail
     mixed_out[pl.ds(first, CODE_ROWS), :] = b_tail
     mixed_out[pl.ds(first + CODE_ROWS + a_rows, CODE_ROWS), :] = a_tail
     second_out[pl.ds(second, CODE_ROWS), :] = b_tail
@@ -155,7 +156,7 @@
     first = first_slots(b_blocks.shape[0]) * width
     sizes = (
         a_rows + CODE_ROWS,
-        b_rows + CODE_ROWS,
+        b_rows + 3 * CODE_ROWS,
         first + a_rows + 2 * CODE_ROWS,
         b_rows - first + CODE_ROWS,
     )
@@ -223,7 +224,7 @@
             ] = source[pl.ds(index * width, width), :]
 
 
-def early_body(slots, own, across, first, second, dense, staged, codes, sem):
+def early_body(slots, own, across, first, dense, staged, codes, sem):
     cut = first_slots(slots)
 
     @pl.when(in_middle())
@@ -236,19 +237,18 @@
         put_blocks(dense, own, codes, 0, 0, slots, slots, col)
         put_blocks(dense, across, codes, 1, 0, slots, slots, col)
         put_blocks(dense, first, codes, 2, 0, cut, slots, col)
-        put_blocks(dense, second, codes, 2, cut, slots - cut, slots, col)
-
-
-def early(own, across, first, second, slots):
+
+
+def early(own, across, first, slots):
     width = own.shape[1]
     return pl.pallas_call(
         functools.partial(early_body, slots),
         out_shape=jax.ShapeDtypeStruct((4 * KB * width, CB * width), jnp.bfloat16),
-        in_specs=spaces("v", "v", "v", "v"),
+        in_specs=spaces("v", "v", "v"),
         out_specs=spaces("v")[0],
         scratch_shapes=code_scratch(),
         compiler_params=pltpu.CompilerParams(vmem_limit_bytes=12 << 20),
-    )(own, across, first, second)
+    )(own, across, first)
 
 
 def multiply_group(dense, total, packs, codes, line, slots, row):
@@ -274,7 +274,7 @@
             total[pl.ds(pl.multiple_of(spot * width, width), width), :] += part
 
 
-def product_body(a_slots, slots, first_column, own_0, own_1, end_0, end_1, dense_in, first, second,
+def product_body(a_slots, slots, first_column, own_0, own_1, end_0, end_1, dense_in, first, second, beside,
                  dense, keep, send, total, staged, codes, sem):
     cut = first_slots(slots)
     rows, columns = keep.shape[0] // 2, keep.shape[1]
@@ -288,7 +288,7 @@
 
     @pl.when(in_middle())
     def _():
-        copy = fetch_codes((end_0, end_1, own_0, own_1, first), staged, codes, sem)
+        copy = fetch_codes((end_0, end_1, own_0, own_1, first, beside), staged, codes, sem)
         copy.start()
         total[...] = jnp.zeros_like(total)
         copy.wait()
@@ -296,6 +296,7 @@
         if place:
             put_blocks(dense, first, codes, 4, 0, cut, slots, col)
             put_blocks(dense, second, codes, 4, cut, slots - cut, slots, col)
+            put_blocks(dense, beside, codes, 5, cut, slots - cut, slots, col)
         next_row = jnp.where(row == 1, 0, 3)
         part = dense.at[:, pl.ds(first_column, columns)]
         multiply_group(part, total.at[0], (end_0, end_1), codes, 0, a_slots, next_row)
@@ -305,34 +306,38 @@
             send[pl.ds(group * rows, rows), :] = total[group, pl.ds(rows, rows), :]
 
 
-def product(own, end, dense, first, second, first_column, columns, a_slots, slots):
+def product(own, end, dense, late, first_column, columns, a_slots, slots):
     width = own[0].shape[1]
     half = jax.ShapeDtypeStruct((4 * width, columns), jnp.float32)
     return pl.pallas_call(
         functools.partial(product_body, a_slots, slots, first_column),
         out_shape=(jax.ShapeDtypeStruct(dense.shape, dense.dtype), half, half),
-        in_specs=spaces(*"vvvvvvv"),
+        in_specs=spaces(*"vvvvvvvv"),
         out_specs=tuple(spaces(*"vvv")),
         scratch_shapes=[pltpu.VMEM((2, 5 * width, columns), jnp.float32)] + code_scratch(),
         input_output_aliases={4: 0},
         compiler_params=pltpu.CompilerParams(vmem_limit_bytes=20 << 20),
-    )(*own, *end, dense, first, second)
+    )(*own, *end, dense, *late)
 
 
 def fold_body(keep, got, end_near, end_far, own_near, own_far):
     rows = end_near.shape[0]
     chip = lax.axis_index("layer") // 2
+    extra = end_far.shape[0] - rows
+    if extra:
+        end_far[pl.ds(rows, extra), :] = jnp.zeros((extra, end_far.shape[1]), end_far.dtype)
     for first, near, far in ((0, end_near, end_far), (2 * rows, own_near, own_far)):
         for out, index in ((near, chip), (far, 1 - chip)):
             block = pl.ds(pl.multiple_of(first + index * rows, rows), rows)
-            out[...] = keep[block, :] + got[block, :]
-
-
-def fold(keep, got):
-    part = jax.ShapeDtypeStruct((keep.shape[0] // 4, keep.shape[1]), jnp.float32)
+            out[pl.ds(0, rows), :] = keep[block, :] + got[block, :]
+
+
+def fold(keep, got, extra):
+    rows, columns = keep.shape[0] // 4, keep.shape[1]
+    part, longer = (jax.ShapeDtypeStruct((n, columns), jnp.float32) for n in (rows, rows + extra))
     return pl.pallas_call(
         fold_body,
-        out_shape=(part,) * 4,
+        out_shape=(part, longer, part, part),
         in_specs=spaces(*"vv"),
         out_specs=tuple(spaces(*"vvvv")),
         compiler_params=pltpu.CompilerParams(vmem_limit_bytes=8 << 20),
@@ -355,7 +360,7 @@
 
 def finish_body(left, left_got, right, right_got, near, far, settled, out):
     cut = left.shape[1]
-    out[:, pl.ds(0, cut)] = ((left[...] + left_got[...]) + (near[...] + far[...])).astype(out.dtype)
+    out[:, pl.ds(0, cut)] = ((left[...] + left_got[...]) + (near[...] + far[pl.ds(0, near.shape[0]), :])).astype(out.dtype)
     rest = (right[...] + right_got[...]) + settled[...].astype(jnp.float32)
     out[:, pl.ds(cut, rest.shape[1])] = rest.astype(out.dtype)
 
@@ -395,19 +400,20 @@
     a_end, a_other = lax.optimization_barrier((a_end, a_other))
     a_end_other = lax.ppermute(a_end, "col", COLS)
 
-    dense = early(b_pack, b_across, end_first, end_second, slots)
+    dense = early(b_pack, b_across, end_first, slots)
     columns = CB * a_blocks.shape[1]
     cut = columns * CUT // 4
     own, end = (a_pack, a_other), (a_end, a_end_other)
-    dense, keep, send = product(own, end, dense, far_first, far_second, cut, columns - cut, a_slots, slots)
+    late = (far_first, far_second, end_second)
+    dense, keep, send = product(own, end, dense, late, cut, columns - cut, a_slots, slots)
     got = lax.ppermute(send, "layer", CORES)
-    _, left_keep, left_send = product(own, end, dense, far_first, far_second, 0, cut, a_slots, slots)
+    _, left_keep, left_send = product(own, end, dense, late, 0, cut, a_slots, slots)
     left_got = lax.ppermute(left_send, "layer", CORES)
-    rest_near, rest_far, right, right_far = fold(keep, got)
+    rest_near, rest_far, right, right_far = fold(keep, got, 0)
     rest_got = lax.ppermute(rest_far, ("row", "layer"), CHIPS)
     settled = lax.ppermute(settle(rest_near, rest_got), "row", BESIDE)
     right_got = lax.ppermute(right_far, ("row", "layer"), CHIPS)
-    near, far, left, left_far = fold(left_keep, left_got)
+    near, far, left, left_far = fold(left_keep, left_got, 8)
     got_near = lax.ppermute(near, "row", BESIDE)
     got_far = lax.ppermute(far, ("row", "layer"), ACROSS)
     left_got = lax.ppermute(left_far, ("row", "layer"), CHIPS)

time: 47.6 us -> 46.7 us (0.981)
  waiting for transfers between devices: 21.9 us -> 20.7 us
    ppermute x1, starting transfers between devices: 0.07 us -> 6.2 us  [middle_shards(): got_far = lax.ppermute(far, ('row', 'layer'), ACROSS)]
    ppermute x1, starting transfers between devices: 7.57 us -> 1.5 us  [middle_shards(): got_near = lax.ppermute(near, 'row', BESIDE)]
    ppermute x1, waiting for transfers between devices: 8.47 us -> 4.88 us  [middle_shards(): end_second = lax.ppermute(b_late, 'row', BESIDE)]
    ppermute x1, waiting for transfers between devices: 0.01 us -> 3.57 us  [middle_shards(): far_second = lax.ppermute(b_second, 'row', BEYOND)]
    ppermute x1, waiting for transfers between devices: 3.55 us -> 0.01 us  [middle_shards(): got_far = lax.ppermute(far, ('row', 'layer'), ACROSS)]
    ppermute x1, waiting for transfers between devices: 0.01 us -> 2.56 us  [middle_shards(): got_near = lax.ppermute(near, 'row', BESIDE)]
    ppermute x1, waiting for transfers between devices: 4.71 us -> 2.2 us  [middle_shards(): end_mixed = lax.ppermute(mixed, 'row', BESIDE)]
    ppermute x1, starting transfers between devices: 0.36 us -> 1.92 us  [middle_shards(): end_second = lax.ppermute(b_late, 'row', BESIDE)]
  transfers between devices with their start and end apart: 15 -> 15, of which waited for: 6 -> 8; matrix products, arithmetic and copies ran while one was open for 0% -> 0% of each run, Pallas kernels for 1% -> 1%
where the time goes in v6:
time: 46.7 us; the launch traced here: 46.5 us
  starting transfers between devices  22.9 us (49%)
  waiting for transfers between devices  20.7 us (44%)
  Pallas kernels  2.9 us (6%)
    ppermute x1, starting transfers between devices, middle_shards(): got_far = lax.ppermute(far, ('row', 'layer'), ACROSS)  6.2 us
    ppermute x1, waiting for transfers between devices, middle_shards(): end_second = lax.ppermute(b_late, 'row', BESIDE)  4.88 us
    ppermute x1, waiting for transfers between devices, middle_shards(): a_other = lax.ppermute(a_pack, 'col', COLS)  4.7 us
    ppermute x1, waiting for transfers between devices, middle_shards(): far_second = lax.ppermute(b_second, 'row', BEYOND)  3.57 us
    ppermute x1, starting transfers between devices, middle_shards(): settled = lax.ppermute(settle(rest_near, rest_got), 'row', BESIDE)  3.16 us
    ppermute x1, starting transfers between devices, middle_shards(): end_mixed = lax.ppermute(mixed, 'row', BESIDE)  3.09 us
    ppermute x1, starting transfers between devices, middle_shards(): far_second = lax.ppermute(b_second, 'row', BEYOND)  2.59 us
    ppermute x1, waiting for transfers between devices, middle_shards(): got_near = lax.ppermute(near, 'row', BESIDE)  2.56 us
  transfers between devices with their start and end apart: 15, of which 8 were waited for; matrix products, arithmetic and copies ran while one was open for 0% of the time, Pallas kernels for 1%

profile of v6, /device:TPU:0, one launch (start us, length us, event | category | flops | bytes accessed | tf_op | source)
XLA Modules:
  0.0 46.5 jit_solution(13627702829307921913)
XLA Ops:
  0.0 1.8 %shard_map.46 = (bf16[1040,128]{1,0:T(8,128)(2,1)S(1)}, bf16[2096,128]{1,0:T(8,128)(2,1)S(1)}, bf16[2080,128]{1,0:T(8,128)(2,1)S(1)}, bf16[1040,128]{1,0:T(8,128)(2,1)S(1)}) custom-call(s32[8]{0:T(128)} %a_codes.1, s32[16]{0:T(128)} %b_codes.1, bf16[1024,128]{1,0:T(8,128)(2,1)} %bitcast.3, bf16[2048,128]{1,0:T(8,128)(2,1)} %bitcast.2), custom_call_target="tpu_custom_call" | custom-call | tf_op jit(solution)/shard_map/pallas_call | solution.py:163
  1.8 3.1 %collective-permute-start = (bf16[2080,128]{1,0:T(8,128)(2,1)S(1)}, bf16[2080,128]{1,0:T(8,128)(2,1)S(1)}, u32[]{:S(2)}, u32[]{:S(2)}) collective-permute-start(bf16[2080,128]{1,0:T(8,128)(2,1)S(1)} %get-tuple-element.29), channel_id=1, source_target_pairs={{0,8},{8,0},{16,24},{24,16},{1,9},{9,1},{17,25},{25,17},{2,10},{10... | collective-permute-start | bytes 1597448 | tf_op jit(solution)/shard_map/ppermute | solution.py:393
  4.9 0.0 collective-permute-start.3
  4.9 1.5 %collective-permute-start.1 = (bf16[1040,128]{1,0:T(8,128)(2,1)S(1)}, bf16[1040,128]{1,0:T(8,128)(2,1)S(1)}, u32[]{:S(2)}, u32[]{:S(2)}) collective-permute-start(bf16[1040,128]{1,0:T(8,128)(2,1)S(1)} %get-tuple-element.28.own_0), channel_id=1, source_target_pairs={{0,4},{4,0},{1,5},{5,1},{2,6},{6,2},{3,7},{7,3},{8,12},{12,8},{9,1... | collective-permute-start | bytes 798728 | tf_op jit(solution)/shard_map/ppermute | solution.py:395
  6.4 2.6 %collective-permute-start.5 = (bf16[1040,128]{1,0:T(8,128)(2,1)S(1)}, bf16[1040,128]{1,0:T(8,128)(2,1)S(1)}, u32[]{:S(2)}, u32[]{:S(2)}) collective-permute-start(bf16[1040,128]{1,0:T(8,128)(2,1)S(1)} %get-tuple-element.37), channel_id=1, source_target_pairs={{0,16},{16,24},{24,8},{8,0},{1,17},{17,25},{25,9},{9,1},{2,18},{18... | collective-permute-start | bytes 798728 | tf_op jit(solution)/shard_map/ppermute | solution.py:394
  9.0 4.7 %collective-permute-done.1.own_1 = bf16[1040,128]{1,0:T(8,128)(2,1)S(1)} collective-permute-done((bf16[1040,128]{1,0:T(8,128)(2,1)S(1)}, bf16[1040,128]{1,0:T(8,128)(2,1)S(1)}, u32[]{:S(2)}, u32[]{:S(2)}) %collective-permute-start.1) | collective-permute-done | bytes 266272 | tf_op jit(solution)/shard_map/ppermute | solution.py:395
  13.7 1.9 %collective-permute-start.6 = (bf16[1040,128]{1,0:T(8,128)(2,1)S(1)}, bf16[1040,128]{1,0:T(8,128)(2,1)S(1)}, u32[]{:S(2)}, u32[]{:S(2)}) collective-permute-start(bf16[1040,128]{1,0:T(8,128)(2,1)S(1)} %get-tuple-element.37), channel_id=1, source_target_pairs={{0,8},{8,0},{16,24},{24,16},{1,9},{9,1},{17,25},{25,17},{2,10},{10... | collective-permute-start | bytes 798728 | tf_op jit(solution)/shard_map/ppermute | solution.py:397
  15.6 2.2 %collective-permute-done.mixed = bf16[2080,128]{1,0:T(8,128)(2,1)S(1)} collective-permute-done((bf16[2080,128]{1,0:T(8,128)(2,1)S(1)}, bf16[2080,128]{1,0:T(8,128)(2,1)S(1)}, u32[]{:S(2)}, u32[]{:S(2)}) %collective-permute-start) | collective-permute-done | bytes 532512 | tf_op jit(solution)/shard_map/ppermute | solution.py:393
  17.9 2.1 %collective-permute-start.2 = (bf16[1040,128]{1,0:T(8,128)(2,1)S(1)}, bf16[1040,128]{1,0:T(8,128)(2,1)S(1)}, u32[]{:S(2)}, u32[]{:S(2)}) collective-permute-start(bf16[1040,128]{1,0:T(8,128)(2,1)S(1)} %get-tuple-element.34.end_0), channel_id=1, source_target_pairs={{0,4},{4,0},{1,5},{5,1},{2,6},{6,2},{3,7},{7,3},{8,12},{12,8},{9,1... | collective-permute-start | bytes 798728 | tf_op jit(solution)/shard_map/ppermute | solution.py:401
  19.9 0.0 collective-permute-start.4
  19.9 0.0 collective-permute-done.3.across
  20.0 3.6 %collective-permute-done.5.second = bf16[1040,128]{1,0:T(8,128)(2,1)S(1)} collective-permute-done((bf16[1040,128]{1,0:T(8,128)(2,1)S(1)}, bf16[1040,128]{1,0:T(8,128)(2,1)S(1)}, u32[]{:S(2)}, u32[]{:S(2)}) %collective-permute-start.5) | collective-permute-done | bytes 266272 | tf_op jit(solution)/shard_map/ppermute | solution.py:394
  23.5 4.9 %collective-permute-done.6.beside = bf16[1040,128]{1,0:T(8,128)(2,1)S(1)} collective-permute-done((bf16[1040,128]{1,0:T(8,128)(2,1)S(1)}, bf16[1040,128]{1,0:T(8,128)(2,1)S(1)}, u32[]{:S(2)}, u32[]{:S(2)}) %collective-permute-start.6) | collective-permute-done | bytes 266272 | tf_op jit(solution)/shard_map/ppermute | solution.py:397
  28.4 0.1 shard_map.49
  28.5 0.1 collective-permute-start.9
  28.6 0.1 shard_map.50
  28.7 0.5 %collective-permute-start.7 = (f32[512,256]{1,0:T(8,128)S(1)}, f32[512,256]{1,0:T(8,128)S(1)}, u32[]{:S(2)}, u32[]{:S(2)}) collective-permute-start(f32[512,256]{1,0:T(8,128)S(1)} %get-tuple-element.40), channel_id=1, source_target_pairs={{0,1},{1,0},{2,3},{3,2},{4,5},{5,4},{6,7},{7,6},{8,9},{9,8},{10,11... | collective-permute-start | bytes 1572872 | tf_op jit(solution)/shard_map/ppermute | solution.py:411
  29.2 1.2 %collective-permute-done.9.got = f32[512,256]{1,0:T(8,128)S(1)} collective-permute-done((f32[512,256]{1,0:T(8,128)S(1)}, f32[512,256]{1,0:T(8,128)S(1)}, u32[]{:S(2)}, u32[]{:S(2)}) %collective-permute-start.9) | collective-permute-done | bytes 524320 | tf_op jit(solution)/shard_map/ppermute | solution.py:409
  30.5 0.1 shard_map.52
  30.5 0.2 collective-permute-start.13
  30.8 0.5 %collective-permute-done.7.got = f32[512,256]{1,0:T(8,128)S(1)} collective-permute-done((f32[512,256]{1,0:T(8,128)S(1)}, f32[512,256]{1,0:T(8,128)S(1)}, u32[]{:S(2)}, u32[]{:S(2)}) %collective-permute-start.7) | collective-permute-done | bytes 524320 | tf_op jit(solution)/shard_map/ppermute | solution.py:411
  31.2 0.1 shard_map.51
  31.3 6.2 %collective-permute-start.12 = (f32[136,256]{1,0:T(8,128)S(1)}, f32[136,256]{1,0:T(8,128)S(1)}, u32[]{:S(2)}, u32[]{:S(2)}) collective-permute-start(f32[136,256]{1,0:T(8,128)S(1)} %get-tuple-element.48), channel_id=1, source_target_pairs={{0,8},{1,9},{2,10},{3,11},{8,2},{9,3},{10,0},{11,1},{16,26},{17,27... | collective-permute-start | bytes 417800 | tf_op jit(solution)/shard_map/ppermute | solution.py:418
  37.5 0.0 collective-permute-start.10
  37.5 1.5 %collective-permute-start.11 = (f32[128,256]{1,0:T(8,128)S(1)}, f32[128,256]{1,0:T(8,128)S(1)}, u32[]{:S(2)}, u32[]{:S(2)}) collective-permute-start(f32[128,256]{1,0:T(8,128)S(1)} %get-tuple-element.47), channel_id=1, source_target_pairs={{0,8},{8,0},{16,24},{24,16},{1,9},{9,1},{17,25},{25,17},{2,10},{10... | collective-permute-start | bytes 393224 | tf_op jit(solution)/shard_map/ppermute | solution.py:417
  39.0 0.0 collective-permute-start.8
  39.0 0.0 collective-permute-done.13.got
  39.0 3.2 %collective-permute-start.14 = (bf16[128,256]{1,0:T(8,128)(2,1)S(1)}, bf16[128,256]{1,0:T(8,128)(2,1)S(1)}, u32[]{:S(2)}, u32[]{:S(2)}) collective-permute-start(bf16[128,256]{1,0:T(8,128)(2,1)S(1)} %shard_map.53), channel_id=1, source_target_pairs={{0,8},{8,0},{16,24},{24,16},{1,9},{9,1},{17,25},{25,17},{2,10},{10... | collective-permute-start | bytes 196616 | tf_op jit(solution)/shard_map/ppermute | solution.py:414
  42.2 0.0 collective-permute-done.10.right_got
  42.2 2.6 %collective-permute-done.11.near = f32[128,256]{1,0:T(8,128)S(1)} collective-permute-done((f32[128,256]{1,0:T(8,128)S(1)}, f32[128,256]{1,0:T(8,128)S(1)}, u32[]{:S(2)}, u32[]{:S(2)}) %collective-permute-start.11) | collective-permute-done | bytes 131104 | tf_op jit(solution)/shard_map/ppermute | solution.py:417
  44.8 1.0 %collective-permute-done.14.settled = bf16[128,256]{1,0:T(8,128)(2,1)S(1)} collective-permute-done((bf16[128,256]{1,0:T(8,128)(2,1)S(1)}, bf16[128,256]{1,0:T(8,128)(2,1)S(1)}, u32[]{:S(2)}, u32[]{:S(2)}) %collective-permute-start.14) | collective-permute-done | bytes 65568 | tf_op jit(solution)/shard_map/ppermute | solution.py:414
  45.8 0.7 %shard_map.54 = bf16[128,512]{1,0:T(8,128)(2,1)} custom-call(f32[128,256]{1,0:T(8,128)S(1)} %get-tuple-element.41.left, f32[128,256]{1,0:T(8,128)S(1)} %collective-permute-done.8.left_got, f32[128,256]{1,0:T(8,128)S(1)} %get-tuple-element.45.right, f32[128,256]{1,0:T(8,128)S(1)} %collective-permute-done.10.right_got, ...), custom_call_target="tpu_custom_call" | custom-call | tf_op jit(solution)/shard_map/pallas_call | solution.py:370
  (7 shorter events, 0.1 us)
Async XLA Ops:
  1.8 16.0 %collective-permute-start = (bf16[2080,128]{1,0:T(8,128)(2,1)S(1)}, bf16[2080,128]{1,0:T(8,128)(2,1)S(1)}, u32[]{:S(2)}, u32[]{:S(2)}) collective-permute-start(bf16[2080,128]{1,0:T(8,128)(2,1)S(1)} %get-tuple-element.29), channel_id=1, source_target_pairs={{0,8},{8,0},{16,24},{24,16},{1,9},{9,1},{17,25},{25,17},{2,10},{10... | collective-permute-start | bytes 1597448 | tf_op jit(solution)/shard_map/ppermute | solution.py:393
  4.9 15.0 %collective-permute-start.3 = (bf16[2096,128]{1,0:T(8,128)(2,1)S(1)}, bf16[2096,128]{1,0:T(8,128)(2,1)S(1)}, u32[]{:S(2)}, u32[]{:S(2)}) collective-permute-start(bf16[2096,128]{1,0:T(8,128)(2,1)S(1)} %get-tuple-element.35.own), channel_id=1, source_target_pairs={{0,1},{1,0},{2,3},{3,2},{8,16},{9,17},{10,18},{11,19},{16,8},{17,9... | collective-permute-start | bytes 1609736 | tf_op jit(solution)/shard_map/ppermute | solution.py:392
  4.9 8.8 %collective-permute-start.1 = (bf16[1040,128]{1,0:T(8,128)(2,1)S(1)}, bf16[1040,128]{1,0:T(8,128)(2,1)S(1)}, u32[]{:S(2)}, u32[]{:S(2)}) collective-permute-start(bf16[1040,128]{1,0:T(8,128)(2,1)S(1)} %get-tuple-element.28.own_0), channel_id=1, source_target_pairs={{0,4},{4,0},{1,5},{5,1},{2,6},{6,2},{3,7},{7,3},{8,12},{12,8},{9,1... | collective-permute-start | bytes 798728 | tf_op jit(solution)/shard_map/ppermute | solution.py:395
  6.4 17.1 %collective-permute-start.5 = (bf16[1040,128]{1,0:T(8,128)(2,1)S(1)}, bf16[1040,128]{1,0:T(8,128)(2,1)S(1)}, u32[]{:S(2)}, u32[]{:S(2)}) collective-permute-start(bf16[1040,128]{1,0:T(8,128)(2,1)S(1)} %get-tuple-element.37), channel_id=1, source_target_pairs={{0,16},{16,24},{24,8},{8,0},{1,17},{17,25},{25,9},{9,1},{2,18},{18... | collective-permute-start | bytes 798728 | tf_op jit(solution)/shard_map/ppermute | solution.py:394
  13.7 14.7 %collective-permute-start.6 = (bf16[1040,128]{1,0:T(8,128)(2,1)S(1)}, bf16[1040,128]{1,0:T(8,128)(2,1)S(1)}, u32[]{:S(2)}, u32[]{:S(2)}) collective-permute-start(bf16[1040,128]{1,0:T(8,128)(2,1)S(1)} %get-tuple-element.37), channel_id=1, source_target_pairs={{0,8},{8,0},{16,24},{24,16},{1,9},{9,1},{17,25},{25,17},{2,10},{10... | collective-permute-start | bytes 798728 | tf_op jit(solution)/shard_map/ppermute | solution.py:397
  17.9 10.5 %collective-permute-start.2 = (bf16[1040,128]{1,0:T(8,128)(2,1)S(1)}, bf16[1040,128]{1,0:T(8,128)(2,1)S(1)}, u32[]{:S(2)}, u32[]{:S(2)}) collective-permute-start(bf16[1040,128]{1,0:T(8,128)(2,1)S(1)} %get-tuple-element.34.end_0), channel_id=1, source_target_pairs={{0,4},{4,0},{1,5},{5,1},{2,6},{6,2},{3,7},{7,3},{8,12},{12,8},{9,1... | collective-permute-start | bytes 798728 | tf_op jit(solution)/shard_map/ppermute | solution.py:401
  19.9 8.5 %collective-permute-start.4 = (bf16[1040,128]{1,0:T(8,128)(2,1)S(1)}, bf16[1040,128]{1,0:T(8,128)(2,1)S(1)}, u32[]{:S(2)}, u32[]{:S(2)}) collective-permute-start(bf16[1040,128]{1,0:T(8,128)(2,1)S(1)} %get-tuple-element.36.first), channel_id=1, source_target_pairs={{0,1},{1,0},{2,3},{3,2},{8,16},{9,17},{10,18},{11,19},{16,8},{17,9... | collective-permute-start | bytes 798728 | tf_op jit(solution)/shard_map/ppermute | solution.py:399
  28.5 2.0 %collective-permute-start.9 = (f32[512,256]{1,0:T(8,128)S(1)}, f32[512,256]{1,0:T(8,128)S(1)}, u32[]{:S(2)}, u32[]{:S(2)}) collective-permute-start(f32[512,256]{1,0:T(8,128)S(1)} %get-tuple-element.44), channel_id=1, source_target_pairs={{0,1},{1,0},{2,3},{3,2},{4,5},{5,4},{6,7},{7,6},{8,9},{9,8},{10,11... | collective-permute-start | bytes 1572872 | tf_op jit(solution)/shard_map/ppermute | solution.py:409
  28.7 2.5 %collective-permute-start.7 = (f32[512,256]{1,0:T(8,128)S(1)}, f32[512,256]{1,0:T(8,128)S(1)}, u32[]{:S(2)}, u32[]{:S(2)}) collective-permute-start(f32[512,256]{1,0:T(8,128)S(1)} %get-tuple-element.40), channel_id=1, source_target_pairs={{0,1},{1,0},{2,3},{3,2},{4,5},{5,4},{6,7},{7,6},{8,9},{9,8},{10,11... | collective-permute-start | bytes 1572872 | tf_op jit(solution)/shard_map/ppermute | solution.py:411
  30.5 8.5 %collective-permute-start.13 = (f32[128,256]{1,0:T(8,128)S(1)}, f32[128,256]{1,0:T(8,128)S(1)}, u32[]{:S(2)}, u32[]{:S(2)}) collective-permute-start(f32[128,256]{1,0:T(8,128)S(1)} %get-tuple-element.50), channel_id=1, source_target_pairs={{0,1},{1,0},{2,3},{3,2},{8,10},{9,11},{10,8},{11,9},{16,18},{17,19... | collective-permute-start | bytes 393224 | tf_op jit(solution)/shard_map/ppermute | solution.py:413
  31.3 13.5 %collective-permute-start.12 = (f32[136,256]{1,0:T(8,128)S(1)}, f32[136,256]{1,0:T(8,128)S(1)}, u32[]{:S(2)}, u32[]{:S(2)}) collective-permute-start(f32[136,256]{1,0:T(8,128)S(1)} %get-tuple-element.48), channel_id=1, source_target_pairs={{0,8},{1,9},{2,10},{3,11},{8,2},{9,3},{10,0},{11,1},{16,26},{17,27... | collective-permute-start | bytes 417800 | tf_op jit(solution)/shard_map/ppermute | solution.py:418
  37.5 4.7 %collective-permute-start.10 = (f32[128,256]{1,0:T(8,128)S(1)}, f32[128,256]{1,0:T(8,128)S(1)}, u32[]{:S(2)}, u32[]{:S(2)}) collective-permute-start(f32[128,256]{1,0:T(8,128)S(1)} %get-tuple-element.46), channel_id=1, source_target_pairs={{0,1},{1,0},{2,3},{3,2},{8,10},{9,11},{10,8},{11,9},{16,18},{17,19... | collective-permute-start | bytes 393224 | tf_op jit(solution)/shard_map/ppermute | solution.py:415
  37.5 7.3 %collective-permute-start.11 = (f32[128,256]{1,0:T(8,128)S(1)}, f32[128,256]{1,0:T(8,128)S(1)}, u32[]{:S(2)}, u32[]{:S(2)}) collective-permute-start(f32[128,256]{1,0:T(8,128)S(1)} %get-tuple-element.47), channel_id=1, source_target_pairs={{0,8},{8,0},{16,24},{24,16},{1,9},{9,1},{17,25},{25,17},{2,10},{10... | collective-permute-start | bytes 393224 | tf_op jit(solution)/shard_map/ppermute | solution.py:417
  39.0 5.8 %collective-permute-start.8 = (f32[128,256]{1,0:T(8,128)S(1)}, f32[128,256]{1,0:T(8,128)S(1)}, u32[]{:S(2)}, u32[]{:S(2)}) collective-permute-start(f32[128,256]{1,0:T(8,128)S(1)} %get-tuple-element.42), channel_id=1, source_target_pairs={{0,1},{1,0},{2,3},{3,2},{8,10},{9,11},{10,8},{11,9},{16,18},{17,19... | collective-permute-start | bytes 393224 | tf_op jit(solution)/shard_map/ppermute | solution.py:419
  39.0 6.7 %collective-permute-start.14 = (bf16[128,256]{1,0:T(8,128)(2,1)S(1)}, bf16[128,256]{1,0:T(8,128)(2,1)S(1)}, u32[]{:S(2)}, u32[]{:S(2)}) collective-permute-start(bf16[128,256]{1,0:T(8,128)(2,1)S(1)} %shard_map.53), channel_id=1, source_target_pairs={{0,8},{8,0},{16,24},{24,16},{1,9},{9,1},{17,25},{25,17},{2,10},{10... | collective-permute-start | bytes 196616 | tf_op jit(solution)/shard_map/ppermute | solution.py:414

commit v7 on v6

--- a/solution.py
+++ b/solution.py
@@ -115,7 +115,7 @@
     return slots * FIRST // 16
 
 
-def pack_body(a_codes, b_codes, a_ref, b_ref, a_out, b_out, mixed_out, second_out, sems):
+def pack_body(a_tags, b_tags, a_ref, b_ref, a_out, b_out, mixed_out, second_out, a_codes, b_codes, sems):
     a_rows, b_rows = a_ref.shape[0], b_ref.shape[0]
     width = a_ref.shape[1]
     second = second_out.shape[0] - CODE_ROWS
@@ -123,6 +123,8 @@
     copies = [
         pltpu.make_async_copy(b_ref, b_out.at[pl.ds(0, b_rows)], sems.at[0]),
         pltpu.make_async_copy(a_ref, a_out.at[pl.ds(0, a_rows)], sems.at[1]),
+        pltpu.make_async_copy(a_tags, a_codes, sems.at[2]),
+        pltpu.make_async_copy(b_tags, b_codes, sems.at[3]),
     ]
     for copy in copies:
         copy.start()
@@ -134,6 +136,8 @@
             values = jnp.where(lanes == slot, codes_ref[slot], values)
         return values.astype(jnp.float32).astype(jnp.bfloat16)
 
+    copies[2].wait()
+    copies[3].wait()
     a_tail, b_tail = code_rows(a_codes), code_rows(b_codes)
     a_out[pl.ds(a_rows, CODE_ROWS), :] = a_tail
     for index in range(3):
@@ -163,9 +167,13 @@
     return pl.pallas_call(
         pack_body,
         out_shape=tuple(jax.ShapeDtypeStruct((rows, width), jnp.bfloat16) for rows in sizes),
-        in_specs=spaces("s", "s", "h", "h"),
+        in_specs=spaces("h", "h", "h", "h"),
         out_specs=tuple(spaces("v", "v", "v", "v")),
-        scratch_shapes=[pltpu.SemaphoreType.DMA((2,))],
+        scratch_shapes=[
+            pltpu.SMEM(a_codes.shape, jnp.int32),
+            pltpu.SMEM(b_codes.shape, jnp.int32),
+            pltpu.SemaphoreType.DMA((4,)),
+        ],
         compiler_params=pltpu.CompilerParams(vmem_limit_bytes=8 << 20),
     )(*(pltpu.with_memory_space_constraint(x, pltpu.HBM) for x in (a_codes, b_codes, a_flat, b_flat)))
 
@@ -249,6 +257,32 @@
         scratch_shapes=code_scratch(),
         compiler_params=pltpu.CompilerParams(vmem_limit_bytes=12 << 20),
     )(own, across, first)
+
+
+def more_body(slots, far, beside, dense_in, dense, staged, codes, sem):
+    cut = first_slots(slots)
+    del dense_in
+
+    @pl.when(in_middle())
+    def _():
+        col = lax.axis_index("col")
+        copy = fetch_codes((far, beside), staged, codes, sem)
+        copy.start()
+        copy.wait()
+        put_blocks(dense, far, codes, 0, cut, slots - cut, slots, col)
+        put_blocks(dense, beside, codes, 1, cut, slots - cut, slots, col)
+
+
+def more(far, beside, dense, slots):
+    return pl.pallas_call(
+        functools.partial(more_body, slots),
+        out_shape=jax.ShapeDtypeStruct(dense.shape, dense.dtype),
+        in_specs=spaces("v", "v", "v"),
+        out_specs=spaces("v")[0],
+        scratch_shapes=code_scratch(),
+        input_output_aliases={2: 0},
+        compiler_params=pltpu.CompilerParams(vmem_limit_bytes=12 << 20),
+    )(far, beside, dense)
 
 
 def multiply_group(dense, total, packs, codes, line, slots, row):
@@ -274,7 +308,7 @@
             total[pl.ds(pl.multiple_of(spot * width, width), width), :] += part
 
 
-def product_body(a_slots, slots, first_column, own_0, own_1, end_0, end_1, dense_in, first, second, beside,
+def product_body(a_slots, slots, first_column, own_0, own_1, end_0, end_1, dense_in, first,
                  dense, keep, send, total, staged, codes, sem):
     cut = first_slots(slots)
     rows, columns = keep.shape[0] // 2, keep.shape[1]
@@ -288,15 +322,13 @@
 
     @pl.when(in_middle())
     def _():
-        copy = fetch_codes((end_0, end_1, own_0, own_1, first, beside), staged, codes, sem)
+        copy = fetch_codes((end_0, end_1, own_0, own_1, first), staged, codes, sem)
         copy.start()
         total[...] = jnp.zeros_like(total)
         copy.wait()
         col, row = lax.axis_index("col"), lax.axis_index("row")
         if place:
             put_blocks(dense, first, codes, 4, 0, cut, slots, col)
-            put_blocks(dense, second, codes, 4, cut, slots - cut, slots, col)
-            put_blocks(dense, beside, codes, 5, cut, slots - cut, slots, col)
         next_row = jnp.where(row == 1, 0, 3)
         part = dense.at[:, pl.ds(first_column, columns)]
         multiply_group(part, total.at[0], (end_0, end_1), codes, 0, a_slots, next_row)
@@ -306,18 +338,18 @@
             send[pl.ds(group * rows, rows), :] = total[group, pl.ds(rows, rows), :]
 
 
-def product(own, end, dense, late, first_column, columns, a_slots, slots):
+def product(own, end, dense, first, first_column, columns, a_slots, slots):
     width = own[0].shape[1]
     half = jax.ShapeDtypeStruct((4 * width, columns), jnp.float32)
     return pl.pallas_call(
         functools.partial(product_body, a_slots, slots, first_column),
         out_shape=(jax.ShapeDtypeStruct(dense.shape, dense.dtype), half, half),
-        in_specs=spaces(*"vvvvvvvv"),
+        in_specs=spaces(*"vvvvvv"),
         out_specs=tuple(spaces(*"vvv")),
         scratch_shapes=[pltpu.VMEM((2, 5 * width, columns), jnp.float32)] + code_scratch(),
         input_output_aliases={4: 0},
         compiler_params=pltpu.CompilerParams(vmem_limit_bytes=20 << 20),
-    )(*own, *end, dense, *late)
+    )(*own, *end, dense, first)
 
 
 def fold_body(keep, got, end_near, end_far, own_near, own_far):
@@ -404,10 +436,10 @@
     columns = CB * a_blocks.shape[1]
     cut = columns * CUT // 4
     own, end = (a_pack, a_other), (a_end, a_end_other)
-    late = (far_first, far_second, end_second)
-    dense, keep, send = product(own, end, dense, late, cut, columns - cut, a_slots, slots)
+    dense = more(far_second, end_second, dense, slots)
+    dense, keep, send = product(own, end, dense, far_first, cut, columns - cut, a_slots, slots)
     got = lax.ppermute(send, "layer", CORES)
-    _, left_keep, left_send = product(own, end, dense, late, 0, cut, a_slots, slots)
+    _, left_keep, left_send = product(own, end, dense, far_first, 0, cut, a_slots, slots)
     left_got = lax.ppermute(left_send, "layer", CORES)
     rest_near, rest_far, right, right_far = fold(keep, got, 0)
     rest_got = lax.ppermute(rest_far, ("row", "layer"), CHIPS)

time: 46.7 us -> 45.8 us (0.981)
  Pallas kernels: 2.9 us -> 2.25 us
    pallas_call x1, Pallas kernels: 1.81 us -> 1.16 us  [pack(): pl.pallas_call(pack_body, out_shape=tuple((jax.ShapeDtypeStruct((rows, wi...]
where the time goes in v7:
time: 45.8 us; the launch traced here: 45.6 us
  starting transfers between devices  22.6 us (49%)
  waiting for transfers between devices  20.6 us (45%)
  Pallas kernels  2.25 us (5%)
    ppermute x1, starting transfers between devices, middle_shards(): got_far = lax.ppermute(far, ('row', 'layer'), ACROSS)  5.9 us
    ppermute x1, waiting for transfers between devices, middle_shards(): end_second = lax.ppermute(b_late, 'row', BESIDE)  4.88 us
    ppermute x1, waiting for transfers between devices, middle_shards(): a_other = lax.ppermute(a_pack, 'col', COLS)  4.7 us
    ppermute x1, waiting for transfers between devices, middle_shards(): far_second = lax.ppermute(b_second, 'row', BEYOND)  3.57 us
    ppermute x1, starting transfers between devices, middle_shards(): settled = lax.ppermute(settle(rest_near, rest_got), 'row', BESIDE)  3.25 us
    ppermute x1, starting transfers between devices, middle_shards(): end_mixed = lax.ppermute(mixed, 'row', BESIDE)  3.09 us
    ppermute x1, starting transfers between devices, middle_shards(): far_second = lax.ppermute(b_second, 'row', BEYOND)  2.59 us
    ppermute x1, waiting for transfers between devices, middle_shards(): got_near = lax.ppermute(near, 'row', BESIDE)  2.48 us
  transfers between devices with their start and end apart: 15, of which 8 were waited for; matrix products, arithmetic and copies ran while one was open for 0% of the time, Pallas kernels for 1%

profile of v7, /device:TPU:0, one launch (start us, length us, event | category | flops | bytes accessed | tf_op | source)
XLA Modules:
  0.0 45.6 jit_solution(6229524424464151043)
XLA Ops:
  0.0 1.2 %shard_map.46 = (bf16[1040,128]{1,0:T(8,128)(2,1)S(1)}, bf16[2096,128]{1,0:T(8,128)(2,1)S(1)}, bf16[2080,128]{1,0:T(8,128)(2,1)S(1)}, bf16[1040,128]{1,0:T(8,128)(2,1)S(1)}) custom-call(s32[8]{0:T(128)} %a_tags.1, s32[16]{0:T(128)} %b_tags.1, bf16[1024,128]{1,0:T(8,128)(2,1)} %bitcast.3, bf16[2048,128]{1,0:T(8,128)(2,1)} %bitcast.2), custom_call_target="tpu_custom_call" | custom-call | tf_op jit(solution)/shard_map/pallas_call | solution.py:167
  1.2 3.1 %collective-permute-start = (bf16[2080,128]{1,0:T(8,128)(2,1)S(1)}, bf16[2080,128]{1,0:T(8,128)(2,1)S(1)}, u32[]{:S(2)}, u32[]{:S(2)}) collective-permute-start(bf16[2080,128]{1,0:T(8,128)(2,1)S(1)} %get-tuple-element.29), channel_id=1, source_target_pairs={{0,8},{8,0},{16,24},{24,16},{1,9},{9,1},{17,25},{25,17},{2,10},{10... | collective-permute-start | bytes 1597448 | tf_op jit(solution)/shard_map/ppermute | solution.py:425
  4.3 0.0 collective-permute-start.5
  4.3 1.5 %collective-permute-start.1 = (bf16[1040,128]{1,0:T(8,128)(2,1)S(1)}, bf16[1040,128]{1,0:T(8,128)(2,1)S(1)}, u32[]{:S(2)}, u32[]{:S(2)}) collective-permute-start(bf16[1040,128]{1,0:T(8,128)(2,1)S(1)} %get-tuple-element.28.own_0), channel_id=1, source_target_pairs={{0,4},{4,0},{1,5},{5,1},{2,6},{6,2},{3,7},{7,3},{8,12},{12,8},{9,1... | collective-permute-start | bytes 798728 | tf_op jit(solution)/shard_map/ppermute | solution.py:427
  5.8 2.6 %collective-permute-start.3 = (bf16[1040,128]{1,0:T(8,128)(2,1)S(1)}, bf16[1040,128]{1,0:T(8,128)(2,1)S(1)}, u32[]{:S(2)}, u32[]{:S(2)}) collective-permute-start(bf16[1040,128]{1,0:T(8,128)(2,1)S(1)} %get-tuple-element.35), channel_id=1, source_target_pairs={{0,16},{16,24},{24,8},{8,0},{1,17},{17,25},{25,9},{9,1},{2,18},{18... | collective-permute-start | bytes 798728 | tf_op jit(solution)/shard_map/ppermute | solution.py:426
  8.4 4.7 %collective-permute-done.1.own_1 = bf16[1040,128]{1,0:T(8,128)(2,1)S(1)} collective-permute-done((bf16[1040,128]{1,0:T(8,128)(2,1)S(1)}, bf16[1040,128]{1,0:T(8,128)(2,1)S(1)}, u32[]{:S(2)}, u32[]{:S(2)}) %collective-permute-start.1) | collective-permute-done | bytes 266272 | tf_op jit(solution)/shard_map/ppermute | solution.py:427
  13.1 1.9 %collective-permute-start.4 = (bf16[1040,128]{1,0:T(8,128)(2,1)S(1)}, bf16[1040,128]{1,0:T(8,128)(2,1)S(1)}, u32[]{:S(2)}, u32[]{:S(2)}) collective-permute-start(bf16[1040,128]{1,0:T(8,128)(2,1)S(1)} %get-tuple-element.35), channel_id=1, source_target_pairs={{0,8},{8,0},{16,24},{24,16},{1,9},{9,1},{17,25},{25,17},{2,10},{10... | collective-permute-start | bytes 798728 | tf_op jit(solution)/shard_map/ppermute | solution.py:429
  15.0 2.2 %collective-permute-done.mixed = bf16[2080,128]{1,0:T(8,128)(2,1)S(1)} collective-permute-done((bf16[2080,128]{1,0:T(8,128)(2,1)S(1)}, bf16[2080,128]{1,0:T(8,128)(2,1)S(1)}, u32[]{:S(2)}, u32[]{:S(2)}) %collective-permute-start) | collective-permute-done | bytes 532512 | tf_op jit(solution)/shard_map/ppermute | solution.py:425
  17.2 2.1 %collective-permute-start.2 = (bf16[1040,128]{1,0:T(8,128)(2,1)S(1)}, bf16[1040,128]{1,0:T(8,128)(2,1)S(1)}, u32[]{:S(2)}, u32[]{:S(2)}) collective-permute-start(bf16[1040,128]{1,0:T(8,128)(2,1)S(1)} %get-tuple-element.34.end_0), channel_id=1, source_target_pairs={{0,4},{4,0},{1,5},{5,1},{2,6},{6,2},{3,7},{7,3},{8,12},{12,8},{9,1... | collective-permute-start | bytes 798728 | tf_op jit(solution)/shard_map/ppermute | solution.py:433
  19.3 0.0 collective-permute-start.6
  19.3 3.6 %collective-permute-done.3.far = bf16[1040,128]{1,0:T(8,128)(2,1)S(1)} collective-permute-done((bf16[1040,128]{1,0:T(8,128)(2,1)S(1)}, bf16[1040,128]{1,0:T(8,128)(2,1)S(1)}, u32[]{:S(2)}, u32[]{:S(2)}) %collective-permute-start.3) | collective-permute-done | bytes 266272 | tf_op jit(solution)/shard_map/ppermute | solution.py:426
  22.9 4.9 %collective-permute-done.4.beside = bf16[1040,128]{1,0:T(8,128)(2,1)S(1)} collective-permute-done((bf16[1040,128]{1,0:T(8,128)(2,1)S(1)}, bf16[1040,128]{1,0:T(8,128)(2,1)S(1)}, u32[]{:S(2)}, u32[]{:S(2)}) %collective-permute-start.4) | collective-permute-done | bytes 266272 | tf_op jit(solution)/shard_map/ppermute | solution.py:429
  27.8 0.0 collective-permute-done.2.end_1
  27.8 0.0 collective-permute-done.6.first
  27.8 0.1 shard_map.50
  27.9 0.1 collective-permute-start.9
  28.0 0.1 shard_map.51
  28.1 0.5 %collective-permute-start.7 = (f32[512,256]{1,0:T(8,128)S(1)}, f32[512,256]{1,0:T(8,128)S(1)}, u32[]{:S(2)}, u32[]{:S(2)}) collective-permute-start(f32[512,256]{1,0:T(8,128)S(1)} %get-tuple-element.40), channel_id=1, source_target_pairs={{0,1},{1,0},{2,3},{3,2},{4,5},{5,4},{6,7},{7,6},{8,9},{9,8},{10,11... | collective-permute-start | bytes 1572872 | tf_op jit(solution)/shard_map/ppermute | solution.py:443
  28.6 1.2 %collective-permute-done.9.got = f32[512,256]{1,0:T(8,128)S(1)} collective-permute-done((f32[512,256]{1,0:T(8,128)S(1)}, f32[512,256]{1,0:T(8,128)S(1)}, u32[]{:S(2)}, u32[]{:S(2)}) %collective-permute-start.9) | collective-permute-done | bytes 524320 | tf_op jit(solution)/shard_map/ppermute | solution.py:441
  29.9 0.1 shard_map.53
  29.9 0.2 collective-permute-start.13
  30.1 0.5 %collective-permute-done.7.got = f32[512,256]{1,0:T(8,128)S(1)} collective-permute-done((f32[512,256]{1,0:T(8,128)S(1)}, f32[512,256]{1,0:T(8,128)S(1)}, u32[]{:S(2)}, u32[]{:S(2)}) %collective-permute-start.7) | collective-permute-done | bytes 524320 | tf_op jit(solution)/shard_map/ppermute | solution.py:443
  30.6 0.1 shard_map.52
  30.7 5.9 %collective-permute-start.12 = (f32[136,256]{1,0:T(8,128)S(1)}, f32[136,256]{1,0:T(8,128)S(1)}, u32[]{:S(2)}, u32[]{:S(2)}) collective-permute-start(f32[136,256]{1,0:T(8,128)S(1)} %get-tuple-element.48), channel_id=1, source_target_pairs={{0,8},{1,9},{2,10},{3,11},{8,2},{9,3},{10,0},{11,1},{16,26},{17,27... | collective-permute-start | bytes 417800 | tf_op jit(solution)/shard_map/ppermute | solution.py:450
  36.6 1.5 %collective-permute-start.11 = (f32[128,256]{1,0:T(8,128)S(1)}, f32[128,256]{1,0:T(8,128)S(1)}, u32[]{:S(2)}, u32[]{:S(2)}) collective-permute-start(f32[128,256]{1,0:T(8,128)S(1)} %get-tuple-element.47), channel_id=1, source_target_pairs={{0,8},{8,0},{16,24},{24,16},{1,9},{9,1},{17,25},{25,17},{2,10},{10... | collective-permute-start | bytes 393224 | tf_op jit(solution)/shard_map/ppermute | solution.py:449
  38.1 0.0 collective-permute-start.8
  38.1 3.2 %collective-permute-start.14 = (bf16[128,256]{1,0:T(8,128)(2,1)S(1)}, bf16[128,256]{1,0:T(8,128)(2,1)S(1)}, u32[]{:S(2)}, u32[]{:S(2)}) collective-permute-start(bf16[128,256]{1,0:T(8,128)(2,1)S(1)} %shard_map.54), channel_id=1, source_target_pairs={{0,8},{8,0},{16,24},{24,16},{1,9},{9,1},{17,25},{25,17},{2,10},{10... | collective-permute-start | bytes 196616 | tf_op jit(solution)/shard_map/ppermute | solution.py:446
  41.4 2.5 %collective-permute-done.11.near = f32[128,256]{1,0:T(8,128)S(1)} collective-permute-done((f32[128,256]{1,0:T(8,128)S(1)}, f32[128,256]{1,0:T(8,128)S(1)}, u32[]{:S(2)}, u32[]{:S(2)}) %collective-permute-start.11) | collective-permute-done | bytes 131104 | tf_op jit(solution)/shard_map/ppermute | solution.py:449
  43.8 0.0 collective-permute-done.8.left_got
  43.9 0.0 collective-permute-done.12.far
  43.9 1.1 %collective-permute-done.14.settled = bf16[128,256]{1,0:T(8,128)(2,1)S(1)} collective-permute-done((bf16[128,256]{1,0:T(8,128)(2,1)S(1)}, bf16[128,256]{1,0:T(8,128)(2,1)S(1)}, u32[]{:S(2)}, u32[]{:S(2)}) %collective-permute-start.14) | collective-permute-done | bytes 65568 | tf_op jit(solution)/shard_map/ppermute | solution.py:446
  44.9 0.7 %shard_map.55 = bf16[128,512]{1,0:T(8,128)(2,1)} custom-call(f32[128,256]{1,0:T(8,128)S(1)} %get-tuple-element.41.left, f32[128,256]{1,0:T(8,128)S(1)} %collective-permute-done.8.left_got, f32[128,256]{1,0:T(8,128)S(1)} %get-tuple-element.45.right, f32[128,256]{1,0:T(8,128)S(1)} %collective-permute-done.10.right_got, ...), custom_call_target="tpu_custom_call" | custom-call | tf_op jit(solution)/shard_map/pallas_call | solution.py:402
  (8 shorter events, 0.1 us)
Async XLA Ops:
  1.2 16.0 %collective-permute-start = (bf16[2080,128]{1,0:T(8,128)(2,1)S(1)}, bf16[2080,128]{1,0:T(8,128)(2,1)S(1)}, u32[]{:S(2)}, u32[]{:S(2)}) collective-permute-start(bf16[2080,128]{1,0:T(8,128)(2,1)S(1)} %get-tuple-element.29), channel_id=1, source_target_pairs={{0,8},{8,0},{16,24},{24,16},{1,9},{9,1},{17,25},{25,17},{2,10},{10... | collective-permute-start | bytes 1597448 | tf_op jit(solution)/shard_map/ppermute | solution.py:425
  4.3 15.0 %collective-permute-start.5 = (bf16[2096,128]{1,0:T(8,128)(2,1)S(1)}, bf16[2096,128]{1,0:T(8,128)(2,1)S(1)}, u32[]{:S(2)}, u32[]{:S(2)}) collective-permute-start(bf16[2096,128]{1,0:T(8,128)(2,1)S(1)} %get-tuple-element.36.own), channel_id=1, source_target_pairs={{0,1},{1,0},{2,3},{3,2},{8,16},{9,17},{10,18},{11,19},{16,8},{17,9... | collective-permute-start | bytes 1609736 | tf_op jit(solution)/shard_map/ppermute | solution.py:424
  4.3 8.8 %collective-permute-start.1 = (bf16[1040,128]{1,0:T(8,128)(2,1)S(1)}, bf16[1040,128]{1,0:T(8,128)(2,1)S(1)}, u32[]{:S(2)}, u32[]{:S(2)}) collective-permute-start(bf16[1040,128]{1,0:T(8,128)(2,1)S(1)} %get-tuple-element.28.own_0), channel_id=1, source_target_pairs={{0,4},{4,0},{1,5},{5,1},{2,6},{6,2},{3,7},{7,3},{8,12},{12,8},{9,1... | collective-permute-start | bytes 798728 | tf_op jit(solution)/shard_map/ppermute | solution.py:427
  5.8 17.1 %collective-permute-start.3 = (bf16[1040,128]{1,0:T(8,128)(2,1)S(1)}, bf16[1040,128]{1,0:T(8,128)(2,1)S(1)}, u32[]{:S(2)}, u32[]{:S(2)}) collective-permute-start(bf16[1040,128]{1,0:T(8,128)(2,1)S(1)} %get-tuple-element.35), channel_id=1, source_target_pairs={{0,16},{16,24},{24,8},{8,0},{1,17},{17,25},{25,9},{9,1},{2,18},{18... | collective-permute-start | bytes 798728 | tf_op jit(solution)/shard_map/ppermute | solution.py:426
  13.1 14.7 %collective-permute-start.4 = (bf16[1040,128]{1,0:T(8,128)(2,1)S(1)}, bf16[1040,128]{1,0:T(8,128)(2,1)S(1)}, u32[]{:S(2)}, u32[]{:S(2)}) collective-permute-start(bf16[1040,128]{1,0:T(8,128)(2,1)S(1)} %get-tuple-element.35), channel_id=1, source_target_pairs={{0,8},{8,0},{16,24},{24,16},{1,9},{9,1},{17,25},{25,17},{2,10},{10... | collective-permute-start | bytes 798728 | tf_op jit(solution)/shard_map/ppermute | solution.py:429
  17.2 10.6 %collective-permute-start.2 = (bf16[1040,128]{1,0:T(8,128)(2,1)S(1)}, bf16[1040,128]{1,0:T(8,128)(2,1)S(1)}, u32[]{:S(2)}, u32[]{:S(2)}) collective-permute-start(bf16[1040,128]{1,0:T(8,128)(2,1)S(1)} %get-tuple-element.34.end_0), channel_id=1, source_target_pairs={{0,4},{4,0},{1,5},{5,1},{2,6},{6,2},{3,7},{7,3},{8,12},{12,8},{9,1... | collective-permute-start | bytes 798728 | tf_op jit(solution)/shard_map/ppermute | solution.py:433
  19.3 8.5 %collective-permute-start.6 = (bf16[1040,128]{1,0:T(8,128)(2,1)S(1)}, bf16[1040,128]{1,0:T(8,128)(2,1)S(1)}, u32[]{:S(2)}, u32[]{:S(2)}) collective-permute-start(bf16[1040,128]{1,0:T(8,128)(2,1)S(1)} %get-tuple-element.37.first), channel_id=1, source_target_pairs={{0,1},{1,0},{2,3},{3,2},{8,16},{9,17},{10,18},{11,19},{16,8},{17,9... | collective-permute-start | bytes 798728 | tf_op jit(solution)/shard_map/ppermute | solution.py:431
  27.9 2.0 %collective-permute-start.9 = (f32[512,256]{1,0:T(8,128)S(1)}, f32[512,256]{1,0:T(8,128)S(1)}, u32[]{:S(2)}, u32[]{:S(2)}) collective-permute-start(f32[512,256]{1,0:T(8,128)S(1)} %get-tuple-element.44), channel_id=1, source_target_pairs={{0,1},{1,0},{2,3},{3,2},{4,5},{5,4},{6,7},{7,6},{8,9},{9,8},{10,11... | collective-permute-start | bytes 1572872 | tf_op jit(solution)/shard_map/ppermute | solution.py:441
  28.1 2.5 %collective-permute-start.7 = (f32[512,256]{1,0:T(8,128)S(1)}, f32[512,256]{1,0:T(8,128)S(1)}, u32[]{:S(2)}, u32[]{:S(2)}) collective-permute-start(f32[512,256]{1,0:T(8,128)S(1)} %get-tuple-element.40), channel_id=1, source_target_pairs={{0,1},{1,0},{2,3},{3,2},{4,5},{5,4},{6,7},{7,6},{8,9},{9,8},{10,11... | collective-permute-start | bytes 1572872 | tf_op jit(solution)/shard_map/ppermute | solution.py:443
  29.9 8.2 %collective-permute-start.13 = (f32[128,256]{1,0:T(8,128)S(1)}, f32[128,256]{1,0:T(8,128)S(1)}, u32[]{:S(2)}, u32[]{:S(2)}) collective-permute-start(f32[128,256]{1,0:T(8,128)S(1)} %get-tuple-element.50), channel_id=1, source_target_pairs={{0,1},{1,0},{2,3},{3,2},{8,10},{9,11},{10,8},{11,9},{16,18},{17,19... | collective-permute-start | bytes 393224 | tf_op jit(solution)/shard_map/ppermute | solution.py:445
  30.7 13.2 %collective-permute-start.12 = (f32[136,256]{1,0:T(8,128)S(1)}, f32[136,256]{1,0:T(8,128)S(1)}, u32[]{:S(2)}, u32[]{:S(2)}) collective-permute-start(f32[136,256]{1,0:T(8,128)S(1)} %get-tuple-element.48), channel_id=1, source_target_pairs={{0,8},{1,9},{2,10},{3,11},{8,2},{9,3},{10,0},{11,1},{16,26},{17,27... | collective-permute-start | bytes 417800 | tf_op jit(solution)/shard_map/ppermute | solution.py:450
  36.6 4.8 %collective-permute-start.10 = (f32[128,256]{1,0:T(8,128)S(1)}, f32[128,256]{1,0:T(8,128)S(1)}, u32[]{:S(2)}, u32[]{:S(2)}) collective-permute-start(f32[128,256]{1,0:T(8,128)S(1)} %get-tuple-element.46), channel_id=1, source_target_pairs={{0,1},{1,0},{2,3},{3,2},{8,10},{9,11},{10,8},{11,9},{16,18},{17,19... | collective-permute-start | bytes 393224 | tf_op jit(solution)/shard_map/ppermute | solution.py:447
  36.6 7.2 %collective-permute-start.11 = (f32[128,256]{1,0:T(8,128)S(1)}, f32[128,256]{1,0:T(8,128)S(1)}, u32[]{:S(2)}, u32[]{:S(2)}) collective-permute-start(f32[128,256]{1,0:T(8,128)S(1)} %get-tuple-element.47), channel_id=1, source_target_pairs={{0,8},{8,0},{16,24},{24,16},{1,9},{9,1},{17,25},{25,17},{2,10},{10... | collective-permute-start | bytes 393224 | tf_op jit(solution)/shard_map/ppermute | solution.py:449
  38.1 5.8 %collective-permute-start.8 = (f32[128,256]{1,0:T(8,128)S(1)}, f32[128,256]{1,0:T(8,128)S(1)}, u32[]{:S(2)}, u32[]{:S(2)}) collective-permute-start(f32[128,256]{1,0:T(8,128)S(1)} %get-tuple-element.42), channel_id=1, source_target_pairs={{0,1},{1,0},{2,3},{3,2},{8,10},{9,11},{10,8},{11,9},{16,18},{17,19... | collective-permute-start | bytes 393224 | tf_op jit(solution)/shard_map/ppermute | solution.py:451
  38.1 6.8 %collective-permute-start.14 = (bf16[128,256]{1,0:T(8,128)(2,1)S(1)}, bf16[128,256]{1,0:T(8,128)(2,1)S(1)}, u32[]{:S(2)}, u32[]{:S(2)}) collective-permute-start(bf16[128,256]{1,0:T(8,128)(2,1)S(1)} %shard_map.54), channel_id=1, source_target_pairs={{0,8},{8,0},{16,24},{24,16},{1,9},{9,1},{17,25},{25,17},{2,10},{10... | collective-permute-start | bytes 196616 | tf_op jit(solution)/shard_map/ppermute | solution.py:446

commit v8 on v7

--- a/solution.py
+++ b/solution.py
@@ -285,31 +285,32 @@
     )(far, beside, dense)
 
 
-def multiply_group(dense, total, packs, codes, line, slots, row):
-    width = packs[0].shape[1]
+def multiply_groups(dense, totals, groups, codes, slots, rows):
+    width = groups[0][0].shape[1]
     pieces, owners = 2, 2
     core = lax.rem(lax.axis_index("layer"), 2)
     for source in range(2):
         for slot in range(slots):
-            code = codes[line + source, slot]
-            live = (code >= 0).astype(jnp.int32)
-            safe = jnp.maximum(code, 0)
-            owner = slot // (slots // owners)
-            piece = lax.rem(row + owner, owners) + owners * lax.rem(safe // KB, pieces)
-            inner = piece * KB + lax.rem(safe, KB)
-            block_row = safe // (pieces * KB)
-            sent = (lax.rem(block_row, 2) != core).astype(jnp.int32)
-            spot = live * (sent * 2 + block_row // 2) + (1 - live) * 4
-            part = jnp.dot(
-                packs[source][pl.ds(slot * width, width), :],
-                dense[pl.ds(pl.multiple_of(inner * width, width), width), :],
-                preferred_element_type=jnp.float32,
-            )
-            total[pl.ds(pl.multiple_of(spot * width, width), width), :] += part
+            for group, (total, packs, row) in enumerate(zip(totals, groups, rows)):
+                code = codes[2 * group + source, slot]
+                live = (code >= 0).astype(jnp.int32)
+                safe = jnp.maximum(code, 0)
+                owner = slot // (slots // owners)
+                piece = lax.rem(row + owner, owners) + owners * lax.rem(safe // KB, pieces)
+                inner = piece * KB + lax.rem(safe, KB)
+                block_row = safe // (pieces * KB)
+                sent = (lax.rem(block_row, 2) != core).astype(jnp.int32)
+                spot = live * (sent * 2 + block_row // 2) + (1 - live) * 4
+                part = jnp.dot(
+                    packs[source][pl.ds(slot * width, width), :],
+                    dense[pl.ds(pl.multiple_of(inner * width, width), width), :],
+                    preferred_element_type=jnp.float32,
+                )
+                total[pl.ds(pl.multiple_of(spot * width, width), width), :] += part
 
 
 def product_body(a_slots, slots, first_column, own_0, own_1, end_0, end_1, dense_in, first,
-                 dense, keep, send, total, staged, codes, sem):
+                 dense, keep, send, end_total, own_total, staged, codes, sem):
     cut = first_slots(slots)
     rows, columns = keep.shape[0] // 2, keep.shape[1]
     place = first_column > 0
@@ -324,18 +325,18 @@
     def _():
         copy = fetch_codes((end_0, end_1, own_0, own_1, first), staged, codes, sem)
         copy.start()
-        total[...] = jnp.zeros_like(total)
+        for total in (end_total, own_total):
+            total[pl.ds(0, 2 * rows), :] = jnp.zeros((2 * rows, columns), total.dtype)
         copy.wait()
         col, row = lax.axis_index("col"), lax.axis_index("row")
         if place:
             put_blocks(dense, first, codes, 4, 0, cut, slots, col)
         next_row = jnp.where(row == 1, 0, 3)
         part = dense.at[:, pl.ds(first_column, columns)]
-        multiply_group(part, total.at[0], (end_0, end_1), codes, 0, a_slots, next_row)
-        multiply_group(part, total.at[1], (own_0, own_1), codes, 2, a_slots, row)
-        for group in range(2):
-            keep[pl.ds(group * rows, rows), :] = total[group, pl.ds(0, rows), :]
-            send[pl.ds(group * rows, rows), :] = total[group, pl.ds(rows, rows), :]
+        multiply_groups(part, (end_total, own_total), ((end_0, end_1), (own_0, own_1)), codes, a_slots, (next_row, row))
+        for group, total in enumerate((end_total, own_total)):
+            keep[pl.ds(group * rows, rows), :] = total[pl.ds(0, rows), :]
+            send[pl.ds(group * rows, rows), :] = total[pl.ds(rows, rows), :]
 
 
 def product(own, end, dense, first, first_column, columns, a_slots, slots):
@@ -346,7 +347,7 @@
         out_shape=(jax.ShapeDtypeStruct(dense.shape, dense.dtype), half, half),
         in_specs=spaces(*"vvvvvv"),
         out_specs=tuple(spaces(*"vvv")),
-        scratch_shapes=[pltpu.VMEM((2, 5 * width, columns), jnp.float32)] + code_scratch(),
+        scratch_shapes=[pltpu.VMEM((5 * width, columns), jnp.float32)] * 2 + code_scratch(),
         input_output_aliases={4: 0},
         compiler_params=pltpu.CompilerParams(vmem_limit_bytes=20 << 20),
     )(*own, *end, dense, first)

time: 45.8 us -> 45.7 us (level)
  no operation moved by 1% of the time
where the time goes in v8:
time: 45.7 us; the launch traced here: 45.5 us
  starting transfers between devices  22.5 us (49%)
  waiting for transfers between devices  20.6 us (45%)
  Pallas kernels  2.25 us (5%)
    ppermute x1, starting transfers between devices, middle_shards(): got_far = lax.ppermute(far, ('row', 'layer'), ACROSS)  5.79 us
    ppermute x1, waiting for transfers between devices, middle_shards(): end_second = lax.ppermute(b_late, 'row', BESIDE)  4.88 us
    ppermute x1, waiting for transfers between devices, middle_shards(): a_other = lax.ppermute(a_pack, 'col', COLS)  4.7 us
    ppermute x1, waiting for transfers between devices, middle_shards(): far_second = lax.ppermute(b_second, 'row', BEYOND)  3.57 us
    ppermute x1, starting transfers between devices, middle_shards(): settled = lax.ppermute(settle(rest_near, rest_got), 'row', BESIDE)  3.22 us
    ppermute x1, starting transfers between devices, middle_shards(): end_mixed = lax.ppermute(mixed, 'row', BESIDE)  3.09 us
    ppermute x1, starting transfers between devices, middle_shards(): far_second = lax.ppermute(b_second, 'row', BEYOND)  2.59 us
    ppermute x1, waiting for transfers between devices, middle_shards(): got_near = lax.ppermute(near, 'row', BESIDE)  2.51 us
  transfers between devices with their start and end apart: 15, of which 8 were waited for; matrix products, arithmetic and copies ran while one was open for 0% of the time, Pallas kernels for 1%

profile of v8, /device:TPU:0, one launch (start us, length us, event | category | flops | bytes accessed | tf_op | source)
XLA Modules:
  0.0 45.5 jit_solution(18086899357152512387)
XLA Ops:
  0.0 1.2 %shard_map.46 = (bf16[1040,128]{1,0:T(8,128)(2,1)S(1)}, bf16[2096,128]{1,0:T(8,128)(2,1)S(1)}, bf16[2080,128]{1,0:T(8,128)(2,1)S(1)}, bf16[1040,128]{1,0:T(8,128)(2,1)S(1)}) custom-call(s32[8]{0:T(128)} %a_tags.1, s32[16]{0:T(128)} %b_tags.1, bf16[1024,128]{1,0:T(8,128)(2,1)} %bitcast.3, bf16[2048,128]{1,0:T(8,128)(2,1)} %bitcast.2), custom_call_target="tpu_custom_call" | custom-call | tf_op jit(solution)/shard_map/pallas_call | solution.py:167
  1.2 3.1 %collective-permute-start = (bf16[2080,128]{1,0:T(8,128)(2,1)S(1)}, bf16[2080,128]{1,0:T(8,128)(2,1)S(1)}, u32[]{:S(2)}, u32[]{:S(2)}) collective-permute-start(bf16[2080,128]{1,0:T(8,128)(2,1)S(1)} %get-tuple-element.29), channel_id=1, source_target_pairs={{0,8},{8,0},{16,24},{24,16},{1,9},{9,1},{17,25},{25,17},{2,10},{10... | collective-permute-start | bytes 1597448 | tf_op jit(solution)/shard_map/ppermute | solution.py:426
  4.3 0.0 collective-permute-start.5
  4.3 1.5 %collective-permute-start.1 = (bf16[1040,128]{1,0:T(8,128)(2,1)S(1)}, bf16[1040,128]{1,0:T(8,128)(2,1)S(1)}, u32[]{:S(2)}, u32[]{:S(2)}) collective-permute-start(bf16[1040,128]{1,0:T(8,128)(2,1)S(1)} %get-tuple-element.28.own_0), channel_id=1, source_target_pairs={{0,4},{4,0},{1,5},{5,1},{2,6},{6,2},{3,7},{7,3},{8,12},{12,8},{9,1... | collective-permute-start | bytes 798728 | tf_op jit(solution)/shard_map/ppermute | solution.py:428
  5.8 2.6 %collective-permute-start.3 = (bf16[1040,128]{1,0:T(8,128)(2,1)S(1)}, bf16[1040,128]{1,0:T(8,128)(2,1)S(1)}, u32[]{:S(2)}, u32[]{:S(2)}) collective-permute-start(bf16[1040,128]{1,0:T(8,128)(2,1)S(1)} %get-tuple-element.35), channel_id=1, source_target_pairs={{0,16},{16,24},{24,8},{8,0},{1,17},{17,25},{25,9},{9,1},{2,18},{18... | collective-permute-start | bytes 798728 | tf_op jit(solution)/shard_map/ppermute | solution.py:427
  8.4 4.7 %collective-permute-done.1.own_1 = bf16[1040,128]{1,0:T(8,128)(2,1)S(1)} collective-permute-done((bf16[1040,128]{1,0:T(8,128)(2,1)S(1)}, bf16[1040,128]{1,0:T(8,128)(2,1)S(1)}, u32[]{:S(2)}, u32[]{:S(2)}) %collective-permute-start.1) | collective-permute-done | bytes 266272 | tf_op jit(solution)/shard_map/ppermute | solution.py:428
  13.1 1.9 %collective-permute-start.4 = (bf16[1040,128]{1,0:T(8,128)(2,1)S(1)}, bf16[1040,128]{1,0:T(8,128)(2,1)S(1)}, u32[]{:S(2)}, u32[]{:S(2)}) collective-permute-start(bf16[1040,128]{1,0:T(8,128)(2,1)S(1)} %get-tuple-element.35), channel_id=1, source_target_pairs={{0,8},{8,0},{16,24},{24,16},{1,9},{9,1},{17,25},{25,17},{2,10},{10... | collective-permute-start | bytes 798728 | tf_op jit(solution)/shard_map/ppermute | solution.py:430
  15.0 2.2 %collective-permute-done.mixed = bf16[2080,128]{1,0:T(8,128)(2,1)S(1)} collective-permute-done((bf16[2080,128]{1,0:T(8,128)(2,1)S(1)}, bf16[2080,128]{1,0:T(8,128)(2,1)S(1)}, u32[]{:S(2)}, u32[]{:S(2)}) %collective-permute-start) | collective-permute-done | bytes 532512 | tf_op jit(solution)/shard_map/ppermute | solution.py:426
  17.2 2.1 %collective-permute-start.2 = (bf16[1040,128]{1,0:T(8,128)(2,1)S(1)}, bf16[1040,128]{1,0:T(8,128)(2,1)S(1)}, u32[]{:S(2)}, u32[]{:S(2)}) collective-permute-start(bf16[1040,128]{1,0:T(8,128)(2,1)S(1)} %get-tuple-element.34.end_0), channel_id=1, source_target_pairs={{0,4},{4,0},{1,5},{5,1},{2,6},{6,2},{3,7},{7,3},{8,12},{12,8},{9,1... | collective-permute-start | bytes 798728 | tf_op jit(solution)/shard_map/ppermute | solution.py:434
  19.3 3.6 %collective-permute-done.3.far = bf16[1040,128]{1,0:T(8,128)(2,1)S(1)} collective-permute-done((bf16[1040,128]{1,0:T(8,128)(2,1)S(1)}, bf16[1040,128]{1,0:T(8,128)(2,1)S(1)}, u32[]{:S(2)}, u32[]{:S(2)}) %collective-permute-start.3) | collective-permute-done | bytes 266272 | tf_op jit(solution)/shard_map/ppermute | solution.py:427
  22.9 4.9 %collective-permute-done.4.beside = bf16[1040,128]{1,0:T(8,128)(2,1)S(1)} collective-permute-done((bf16[1040,128]{1,0:T(8,128)(2,1)S(1)}, bf16[1040,128]{1,0:T(8,128)(2,1)S(1)}, u32[]{:S(2)}, u32[]{:S(2)}) %collective-permute-start.4) | collective-permute-done | bytes 266272 | tf_op jit(solution)/shard_map/ppermute | solution.py:430
  27.8 0.0 collective-permute-done.2.end_1
  27.8 0.0 collective-permute-done.6.first
  27.8 0.1 shard_map.50
  27.9 0.1 collective-permute-start.9
  28.0 0.1 shard_map.51
  28.1 0.5 %collective-permute-start.7 = (f32[512,256]{1,0:T(8,128)S(1)}, f32[512,256]{1,0:T(8,128)S(1)}, u32[]{:S(2)}, u32[]{:S(2)}) collective-permute-start(f32[512,256]{1,0:T(8,128)S(1)} %get-tuple-element.40), channel_id=1, source_target_pairs={{0,1},{1,0},{2,3},{3,2},{4,5},{5,4},{6,7},{7,6},{8,9},{9,8},{10,11... | collective-permute-start | bytes 1572872 | tf_op jit(solution)/shard_map/ppermute | solution.py:444
  28.6 1.2 %collective-permute-done.9.got = f32[512,256]{1,0:T(8,128)S(1)} collective-permute-done((f32[512,256]{1,0:T(8,128)S(1)}, f32[512,256]{1,0:T(8,128)S(1)}, u32[]{:S(2)}, u32[]{:S(2)}) %collective-permute-start.9) | collective-permute-done | bytes 524320 | tf_op jit(solution)/shard_map/ppermute | solution.py:442
  29.9 0.1 shard_map.53
  29.9 0.2 collective-permute-start.13
  30.1 0.5 %collective-permute-done.7.got = f32[512,256]{1,0:T(8,128)S(1)} collective-permute-done((f32[512,256]{1,0:T(8,128)S(1)}, f32[512,256]{1,0:T(8,128)S(1)}, u32[]{:S(2)}, u32[]{:S(2)}) %collective-permute-start.7) | collective-permute-done | bytes 524320 | tf_op jit(solution)/shard_map/ppermute | solution.py:444
  30.6 0.1 shard_map.52
  30.7 5.8 %collective-permute-start.12 = (f32[136,256]{1,0:T(8,128)S(1)}, f32[136,256]{1,0:T(8,128)S(1)}, u32[]{:S(2)}, u32[]{:S(2)}) collective-permute-start(f32[136,256]{1,0:T(8,128)S(1)} %get-tuple-element.48), channel_id=1, source_target_pairs={{0,8},{1,9},{2,10},{3,11},{8,2},{9,3},{10,0},{11,1},{16,26},{17,27... | collective-permute-start | bytes 417800 | tf_op jit(solution)/shard_map/ppermute | solution.py:451
  36.5 1.5 %collective-permute-start.11 = (f32[128,256]{1,0:T(8,128)S(1)}, f32[128,256]{1,0:T(8,128)S(1)}, u32[]{:S(2)}, u32[]{:S(2)}) collective-permute-start(f32[128,256]{1,0:T(8,128)S(1)} %get-tuple-element.47), channel_id=1, source_target_pairs={{0,8},{8,0},{16,24},{24,16},{1,9},{9,1},{17,25},{25,17},{2,10},{10... | collective-permute-start | bytes 393224 | tf_op jit(solution)/shard_map/ppermute | solution.py:450
  38.0 0.0 collective-permute-start.8
  38.0 0.0 collective-permute-done.13.got
  38.0 3.2 %collective-permute-start.14 = (bf16[128,256]{1,0:T(8,128)(2,1)S(1)}, bf16[128,256]{1,0:T(8,128)(2,1)S(1)}, u32[]{:S(2)}, u32[]{:S(2)}) collective-permute-start(bf16[128,256]{1,0:T(8,128)(2,1)S(1)} %shard_map.54), channel_id=1, source_target_pairs={{0,8},{8,0},{16,24},{24,16},{1,9},{9,1},{17,25},{25,17},{2,10},{10... | collective-permute-start | bytes 196616 | tf_op jit(solution)/shard_map/ppermute | solution.py:447
  41.2 0.0 collective-permute-done.10.right_got
  41.2 2.5 %collective-permute-done.11.near = f32[128,256]{1,0:T(8,128)S(1)} collective-permute-done((f32[128,256]{1,0:T(8,128)S(1)}, f32[128,256]{1,0:T(8,128)S(1)}, u32[]{:S(2)}, u32[]{:S(2)}) %collective-permute-start.11) | collective-permute-done | bytes 131104 | tf_op jit(solution)/shard_map/ppermute | solution.py:450
  43.7 0.0 collective-permute-done.8.left_got
  43.7 1.0 %collective-permute-done.14.settled = bf16[128,256]{1,0:T(8,128)(2,1)S(1)} collective-permute-done((bf16[128,256]{1,0:T(8,128)(2,1)S(1)}, bf16[128,256]{1,0:T(8,128)(2,1)S(1)}, u32[]{:S(2)}, u32[]{:S(2)}) %collective-permute-start.14) | collective-permute-done | bytes 65568 | tf_op jit(solution)/shard_map/ppermute | solution.py:447
  44.8 0.7 %shard_map.55 = bf16[128,512]{1,0:T(8,128)(2,1)} custom-call(f32[128,256]{1,0:T(8,128)S(1)} %get-tuple-element.41.left, f32[128,256]{1,0:T(8,128)S(1)} %collective-permute-done.8.left_got, f32[128,256]{1,0:T(8,128)S(1)} %get-tuple-element.45.right, f32[128,256]{1,0:T(8,128)S(1)} %collective-permute-done.10.right_got, ...), custom_call_target="tpu_custom_call" | custom-call | tf_op jit(solution)/shard_map/pallas_call | solution.py:403
  (8 shorter events, 0.1 us)
Async XLA Ops:
  1.2 16.0 %collective-permute-start = (bf16[2080,128]{1,0:T(8,128)(2,1)S(1)}, bf16[2080,128]{1,0:T(8,128)(2,1)S(1)}, u32[]{:S(2)}, u32[]{:S(2)}) collective-permute-start(bf16[2080,128]{1,0:T(8,128)(2,1)S(1)} %get-tuple-element.29), channel_id=1, source_target_pairs={{0,8},{8,0},{16,24},{24,16},{1,9},{9,1},{17,25},{25,17},{2,10},{10... | collective-permute-start | bytes 1597448 | tf_op jit(solution)/shard_map/ppermute | solution.py:426
  4.3 15.0 %collective-permute-start.5 = (bf16[2096,128]{1,0:T(8,128)(2,1)S(1)}, bf16[2096,128]{1,0:T(8,128)(2,1)S(1)}, u32[]{:S(2)}, u32[]{:S(2)}) collective-permute-start(bf16[2096,128]{1,0:T(8,128)(2,1)S(1)} %get-tuple-element.36.own), channel_id=1, source_target_pairs={{0,1},{1,0},{2,3},{3,2},{8,16},{9,17},{10,18},{11,19},{16,8},{17,9... | collective-permute-start | bytes 1609736 | tf_op jit(solution)/shard_map/ppermute | solution.py:425
  4.3 8.8 %collective-permute-start.1 = (bf16[1040,128]{1,0:T(8,128)(2,1)S(1)}, bf16[1040,128]{1,0:T(8,128)(2,1)S(1)}, u32[]{:S(2)}, u32[]{:S(2)}) collective-permute-start(bf16[1040,128]{1,0:T(8,128)(2,1)S(1)} %get-tuple-element.28.own_0), channel_id=1, source_target_pairs={{0,4},{4,0},{1,5},{5,1},{2,6},{6,2},{3,7},{7,3},{8,12},{12,8},{9,1... | collective-permute-start | bytes 798728 | tf_op jit(solution)/shard_map/ppermute | solution.py:428
  5.8 17.1 %collective-permute-start.3 = (bf16[1040,128]{1,0:T(8,128)(2,1)S(1)}, bf16[1040,128]{1,0:T(8,128)(2,1)S(1)}, u32[]{:S(2)}, u32[]{:S(2)}) collective-permute-start(bf16[1040,128]{1,0:T(8,128)(2,1)S(1)} %get-tuple-element.35), channel_id=1, source_target_pairs={{0,16},{16,24},{24,8},{8,0},{1,17},{17,25},{25,9},{9,1},{2,18},{18... | collective-permute-start | bytes 798728 | tf_op jit(solution)/shard_map/ppermute | solution.py:427
  13.1 14.7 %collective-permute-start.4 = (bf16[1040,128]{1,0:T(8,128)(2,1)S(1)}, bf16[1040,128]{1,0:T(8,128)(2,1)S(1)}, u32[]{:S(2)}, u32[]{:S(2)}) collective-permute-start(bf16[1040,128]{1,0:T(8,128)(2,1)S(1)} %get-tuple-element.35), channel_id=1, source_target_pairs={{0,8},{8,0},{16,24},{24,16},{1,9},{9,1},{17,25},{25,17},{2,10},{10... | collective-permute-start | bytes 798728 | tf_op jit(solution)/shard_map/ppermute | solution.py:430
  17.2 10.6 %collective-permute-start.2 = (bf16[1040,128]{1,0:T(8,128)(2,1)S(1)}, bf16[1040,128]{1,0:T(8,128)(2,1)S(1)}, u32[]{:S(2)}, u32[]{:S(2)}) collective-permute-start(bf16[1040,128]{1,0:T(8,128)(2,1)S(1)} %get-tuple-element.34.end_0), channel_id=1, source_target_pairs={{0,4},{4,0},{1,5},{5,1},{2,6},{6,2},{3,7},{7,3},{8,12},{12,8},{9,1... | collective-permute-start | bytes 798728 | tf_op jit(solution)/shard_map/ppermute | solution.py:434
  19.3 8.5 %collective-permute-start.6 = (bf16[1040,128]{1,0:T(8,128)(2,1)S(1)}, bf16[1040,128]{1,0:T(8,128)(2,1)S(1)}, u32[]{:S(2)}, u32[]{:S(2)}) collective-permute-start(bf16[1040,128]{1,0:T(8,128)(2,1)S(1)} %get-tuple-element.37.first), channel_id=1, source_target_pairs={{0,1},{1,0},{2,3},{3,2},{8,16},{9,17},{10,18},{11,19},{16,8},{17,9... | collective-permute-start | bytes 798728 | tf_op jit(solution)/shard_map/ppermute | solution.py:432
  27.9 2.0 %collective-permute-start.9 = (f32[512,256]{1,0:T(8,128)S(1)}, f32[512,256]{1,0:T(8,128)S(1)}, u32[]{:S(2)}, u32[]{:S(2)}) collective-permute-start(f32[512,256]{1,0:T(8,128)S(1)} %get-tuple-element.44), channel_id=1, source_target_pairs={{0,1},{1,0},{2,3},{3,2},{4,5},{5,4},{6,7},{7,6},{8,9},{9,8},{10,11... | collective-permute-start | bytes 1572872 | tf_op jit(solution)/shard_map/ppermute | solution.py:442
  28.1 2.5 %collective-permute-start.7 = (f32[512,256]{1,0:T(8,128)S(1)}, f32[512,256]{1,0:T(8,128)S(1)}, u32[]{:S(2)}, u32[]{:S(2)}) collective-permute-start(f32[512,256]{1,0:T(8,128)S(1)} %get-tuple-element.40), channel_id=1, source_target_pairs={{0,1},{1,0},{2,3},{3,2},{4,5},{5,4},{6,7},{7,6},{8,9},{9,8},{10,11... | collective-permute-start | bytes 1572872 | tf_op jit(solution)/shard_map/ppermute | solution.py:444
  29.9 8.0 %collective-permute-start.13 = (f32[128,256]{1,0:T(8,128)S(1)}, f32[128,256]{1,0:T(8,128)S(1)}, u32[]{:S(2)}, u32[]{:S(2)}) collective-permute-start(f32[128,256]{1,0:T(8,128)S(1)} %get-tuple-element.50), channel_id=1, source_target_pairs={{0,1},{1,0},{2,3},{3,2},{8,10},{9,11},{10,8},{11,9},{16,18},{17,19... | collective-permute-start | bytes 393224 | tf_op jit(solution)/shard_map/ppermute | solution.py:446
  30.7 13.0 %collective-permute-start.12 = (f32[136,256]{1,0:T(8,128)S(1)}, f32[136,256]{1,0:T(8,128)S(1)}, u32[]{:S(2)}, u32[]{:S(2)}) collective-permute-start(f32[136,256]{1,0:T(8,128)S(1)} %get-tuple-element.48), channel_id=1, source_target_pairs={{0,8},{1,9},{2,10},{3,11},{8,2},{9,3},{10,0},{11,1},{16,26},{17,27... | collective-permute-start | bytes 417800 | tf_op jit(solution)/shard_map/ppermute | solution.py:451
  36.5 4.7 %collective-permute-start.10 = (f32[128,256]{1,0:T(8,128)S(1)}, f32[128,256]{1,0:T(8,128)S(1)}, u32[]{:S(2)}, u32[]{:S(2)}) collective-permute-start(f32[128,256]{1,0:T(8,128)S(1)} %get-tuple-element.46), channel_id=1, source_target_pairs={{0,1},{1,0},{2,3},{3,2},{8,10},{9,11},{10,8},{11,9},{16,18},{17,19... | collective-permute-start | bytes 393224 | tf_op jit(solution)/shard_map/ppermute | solution.py:448
  36.5 7.3 %collective-permute-start.11 = (f32[128,256]{1,0:T(8,128)S(1)}, f32[128,256]{1,0:T(8,128)S(1)}, u32[]{:S(2)}, u32[]{:S(2)}) collective-permute-start(f32[128,256]{1,0:T(8,128)S(1)} %get-tuple-element.47), channel_id=1, source_target_pairs={{0,8},{8,0},{16,24},{24,16},{1,9},{9,1},{17,25},{25,17},{2,10},{10... | collective-permute-start | bytes 393224 | tf_op jit(solution)/shard_map/ppermute | solution.py:450
  38.0 5.8 %collective-permute-start.8 = (f32[128,256]{1,0:T(8,128)S(1)}, f32[128,256]{1,0:T(8,128)S(1)}, u32[]{:S(2)}, u32[]{:S(2)}) collective-permute-start(f32[128,256]{1,0:T(8,128)S(1)} %get-tuple-element.42), channel_id=1, source_target_pairs={{0,1},{1,0},{2,3},{3,2},{8,10},{9,11},{10,8},{11,9},{16,18},{17,19... | collective-permute-start | bytes 393224 | tf_op jit(solution)/shard_map/ppermute | solution.py:452
  38.0 6.8 %collective-permute-start.14 = (bf16[128,256]{1,0:T(8,128)(2,1)S(1)}, bf16[128,256]{1,0:T(8,128)(2,1)S(1)}, u32[]{:S(2)}, u32[]{:S(2)}) collective-permute-start(bf16[128,256]{1,0:T(8,128)(2,1)S(1)} %shard_map.54), channel_id=1, source_target_pairs={{0,8},{8,0},{16,24},{24,16},{1,9},{9,1},{17,25},{25,17},{2,10},{10... | collective-permute-start | bytes 196616 | tf_op jit(solution)/shard_map/ppermute | solution.py:447

commit v9 on v8

--- a/solution.py
+++ b/solution.py
@@ -220,16 +220,13 @@
     owners = 4
     for index in range(count):
         code = codes[line, first_slot + index]
-
-        @pl.when(code >= 0)
-        def _():
-            piece = lax.rem((first_slot + index) // (slots // owners) + col, owners)
-            inner = piece * KB + code // CB
-            column = lax.rem(code, CB)
-            dense[
-                pl.ds(pl.multiple_of(inner * width, width), width),
-                pl.ds(pl.multiple_of(column * width, width), width),
-            ] = source[pl.ds(index * width, width), :]
+        piece = lax.rem((first_slot + index) // (slots // owners) + col, owners)
+        inner = jnp.where(code >= 0, piece * KB + code // CB, dense.shape[0] // width - 1)
+        column = lax.rem(jnp.maximum(code, 0), CB)
+        dense[
+            pl.ds(pl.multiple_of(inner * width, width), width),
+            pl.ds(pl.multiple_of(column * width, width), width),
+        ] = source[pl.ds(index * width, width), :]
 
 
 def early_body(slots, own, across, first, dense, staged, codes, sem):
@@ -251,7 +248,7 @@
     width = own.shape[1]
     return pl.pallas_call(
         functools.partial(early_body, slots),
-        out_shape=jax.ShapeDtypeStruct((4 * KB * width, CB * width), jnp.bfloat16),
+        out_shape=jax.ShapeDtypeStruct(((4 * KB + 1) * width, CB * width), jnp.bfloat16),
         in_specs=spaces("v", "v", "v"),
         out_specs=spaces("v")[0],
         scratch_shapes=code_scratch(),

time: 45.7 us -> 45.6 us (level)
  no operation moved by 1% of the time
where the time goes in v9:
time: 45.6 us; the launch traced here: 45.5 us
  starting transfers between devices  22.5 us (49%)
  waiting for transfers between devices  20.6 us (45%)
  Pallas kernels  2.25 us (5%)
    ppermute x1, starting transfers between devices, middle_shards(): got_far = lax.ppermute(far, ('row', 'layer'), ACROSS)  5.71 us
    ppermute x1, waiting for transfers between devices, middle_shards(): end_second = lax.ppermute(b_late, 'row', BESIDE)  4.88 us
    ppermute x1, waiting for transfers between devices, middle_shards(): a_other = lax.ppermute(a_pack, 'col', COLS)  4.7 us
    ppermute x1, waiting for transfers between devices, middle_shards(): far_second = lax.ppermute(b_second, 'row', BEYOND)  3.57 us
    ppermute x1, starting transfers between devices, middle_shards(): settled = lax.ppermute(settle(rest_near, rest_got), 'row', BESIDE)  3.27 us
    ppermute x1, starting transfers between devices, middle_shards(): end_mixed = lax.ppermute(mixed, 'row', BESIDE)  3.09 us
    ppermute x1, starting transfers between devices, middle_shards(): far_second = lax.ppermute(b_second, 'row', BEYOND)  2.59 us
    ppermute x1, waiting for transfers between devices, middle_shards(): got_near = lax.ppermute(near, 'row', BESIDE)  2.45 us
  transfers between devices with their start and end apart: 15, of which 8 were waited for; matrix products, arithmetic and copies ran while one was open for 0% of the time, Pallas kernels for 1%

profile of v9, /device:TPU:0, one launch (start us, length us, event | category | flops | bytes accessed | tf_op | source)
XLA Modules:
  0.0 45.5 jit_solution(162840855606906269)
XLA Ops:
  0.0 1.2 %shard_map.46 = (bf16[1040,128]{1,0:T(8,128)(2,1)S(1)}, bf16[2096,128]{1,0:T(8,128)(2,1)S(1)}, bf16[2080,128]{1,0:T(8,128)(2,1)S(1)}, bf16[1040,128]{1,0:T(8,128)(2,1)S(1)}) custom-call(s32[8]{0:T(128)} %a_tags.1, s32[16]{0:T(128)} %b_tags.1, bf16[1024,128]{1,0:T(8,128)(2,1)} %bitcast.3, bf16[2048,128]{1,0:T(8,128)(2,1)} %bitcast.2), custom_call_target="tpu_custom_call" | custom-call | tf_op jit(solution)/shard_map/pallas_call | solution.py:167
  1.2 3.1 %collective-permute-start = (bf16[2080,128]{1,0:T(8,128)(2,1)S(1)}, bf16[2080,128]{1,0:T(8,128)(2,1)S(1)}, u32[]{:S(2)}, u32[]{:S(2)}) collective-permute-start(bf16[2080,128]{1,0:T(8,128)(2,1)S(1)} %get-tuple-element.29), channel_id=1, source_target_pairs={{0,8},{8,0},{16,24},{24,16},{1,9},{9,1},{17,25},{25,17},{2,10},{10... | collective-permute-start | bytes 1597448 | tf_op jit(solution)/shard_map/ppermute | solution.py:423
  4.3 1.5 %collective-permute-start.1 = (bf16[1040,128]{1,0:T(8,128)(2,1)S(1)}, bf16[1040,128]{1,0:T(8,128)(2,1)S(1)}, u32[]{:S(2)}, u32[]{:S(2)}) collective-permute-start(bf16[1040,128]{1,0:T(8,128)(2,1)S(1)} %get-tuple-element.28.own_0), channel_id=1, source_target_pairs={{0,4},{4,0},{1,5},{5,1},{2,6},{6,2},{3,7},{7,3},{8,12},{12,8},{9,1... | collective-permute-start | bytes 798728 | tf_op jit(solution)/shard_map/ppermute | solution.py:425
  5.8 2.6 %collective-permute-start.3 = (bf16[1040,128]{1,0:T(8,128)(2,1)S(1)}, bf16[1040,128]{1,0:T(8,128)(2,1)S(1)}, u32[]{:S(2)}, u32[]{:S(2)}) collective-permute-start(bf16[1040,128]{1,0:T(8,128)(2,1)S(1)} %get-tuple-element.35), channel_id=1, source_target_pairs={{0,16},{16,24},{24,8},{8,0},{1,17},{17,25},{25,9},{9,1},{2,18},{18... | collective-permute-start | bytes 798728 | tf_op jit(solution)/shard_map/ppermute | solution.py:424
  8.4 4.7 %collective-permute-done.1.own_1 = bf16[1040,128]{1,0:T(8,128)(2,1)S(1)} collective-permute-done((bf16[1040,128]{1,0:T(8,128)(2,1)S(1)}, bf16[1040,128]{1,0:T(8,128)(2,1)S(1)}, u32[]{:S(2)}, u32[]{:S(2)}) %collective-permute-start.1) | collective-permute-done | bytes 266272 | tf_op jit(solution)/shard_map/ppermute | solution.py:425
  13.1 1.9 %collective-permute-start.4 = (bf16[1040,128]{1,0:T(8,128)(2,1)S(1)}, bf16[1040,128]{1,0:T(8,128)(2,1)S(1)}, u32[]{:S(2)}, u32[]{:S(2)}) collective-permute-start(bf16[1040,128]{1,0:T(8,128)(2,1)S(1)} %get-tuple-element.35), channel_id=1, source_target_pairs={{0,8},{8,0},{16,24},{24,16},{1,9},{9,1},{17,25},{25,17},{2,10},{10... | collective-permute-start | bytes 798728 | tf_op jit(solution)/shard_map/ppermute | solution.py:427
  15.0 2.2 %collective-permute-done.mixed = bf16[2080,128]{1,0:T(8,128)(2,1)S(1)} collective-permute-done((bf16[2080,128]{1,0:T(8,128)(2,1)S(1)}, bf16[2080,128]{1,0:T(8,128)(2,1)S(1)}, u32[]{:S(2)}, u32[]{:S(2)}) %collective-permute-start) | collective-permute-done | bytes 532512 | tf_op jit(solution)/shard_map/ppermute | solution.py:423
  17.2 2.1 %collective-permute-start.2 = (bf16[1040,128]{1,0:T(8,128)(2,1)S(1)}, bf16[1040,128]{1,0:T(8,128)(2,1)S(1)}, u32[]{:S(2)}, u32[]{:S(2)}) collective-permute-start(bf16[1040,128]{1,0:T(8,128)(2,1)S(1)} %get-tuple-element.34.end_0), channel_id=1, source_target_pairs={{0,4},{4,0},{1,5},{5,1},{2,6},{6,2},{3,7},{7,3},{8,12},{12,8},{9,1... | collective-permute-start | bytes 798728 | tf_op jit(solution)/shard_map/ppermute | solution.py:431
  19.3 3.6 %collective-permute-done.3.far = bf16[1040,128]{1,0:T(8,128)(2,1)S(1)} collective-permute-done((bf16[1040,128]{1,0:T(8,128)(2,1)S(1)}, bf16[1040,128]{1,0:T(8,128)(2,1)S(1)}, u32[]{:S(2)}, u32[]{:S(2)}) %collective-permute-start.3) | collective-permute-done | bytes 266272 | tf_op jit(solution)/shard_map/ppermute | solution.py:424
  22.9 4.9 %collective-permute-done.4.beside = bf16[1040,128]{1,0:T(8,128)(2,1)S(1)} collective-permute-done((bf16[1040,128]{1,0:T(8,128)(2,1)S(1)}, bf16[1040,128]{1,0:T(8,128)(2,1)S(1)}, u32[]{:S(2)}, u32[]{:S(2)}) %collective-permute-start.4) | collective-permute-done | bytes 266272 | tf_op jit(solution)/shard_map/ppermute | solution.py:427
  27.8 0.0 collective-permute-done.2.end_1
  27.8 0.0 collective-permute-done.6.first
  27.8 0.1 shard_map.50
  27.9 0.1 collective-permute-start.9
  28.0 0.1 shard_map.51
  28.1 0.5 %collective-permute-start.7 = (f32[512,256]{1,0:T(8,128)S(1)}, f32[512,256]{1,0:T(8,128)S(1)}, u32[]{:S(2)}, u32[]{:S(2)}) collective-permute-start(f32[512,256]{1,0:T(8,128)S(1)} %get-tuple-element.40), channel_id=1, source_target_pairs={{0,1},{1,0},{2,3},{3,2},{4,5},{5,4},{6,7},{7,6},{8,9},{9,8},{10,11... | collective-permute-start | bytes 1572872 | tf_op jit(solution)/shard_map/ppermute | solution.py:441
  28.6 1.2 %collective-permute-done.9.got = f32[512,256]{1,0:T(8,128)S(1)} collective-permute-done((f32[512,256]{1,0:T(8,128)S(1)}, f32[512,256]{1,0:T(8,128)S(1)}, u32[]{:S(2)}, u32[]{:S(2)}) %collective-permute-start.9) | collective-permute-done | bytes 524320 | tf_op jit(solution)/shard_map/ppermute | solution.py:439
  29.9 0.1 shard_map.53
  29.9 0.2 collective-permute-start.13
  30.2 0.5 %collective-permute-done.7.got = f32[512,256]{1,0:T(8,128)S(1)} collective-permute-done((f32[512,256]{1,0:T(8,128)S(1)}, f32[512,256]{1,0:T(8,128)S(1)}, u32[]{:S(2)}, u32[]{:S(2)}) %collective-permute-start.7) | collective-permute-done | bytes 524320 | tf_op jit(solution)/shard_map/ppermute | solution.py:441
  30.6 0.1 shard_map.52
  30.7 5.7 %collective-permute-start.12 = (f32[136,256]{1,0:T(8,128)S(1)}, f32[136,256]{1,0:T(8,128)S(1)}, u32[]{:S(2)}, u32[]{:S(2)}) collective-permute-start(f32[136,256]{1,0:T(8,128)S(1)} %get-tuple-element.48), channel_id=1, source_target_pairs={{0,8},{1,9},{2,10},{3,11},{8,2},{9,3},{10,0},{11,1},{16,26},{17,27... | collective-permute-start | bytes 417800 | tf_op jit(solution)/shard_map/ppermute | solution.py:448
  36.4 0.0 collective-permute-start.10
  36.4 1.5 %collective-permute-start.11 = (f32[128,256]{1,0:T(8,128)S(1)}, f32[128,256]{1,0:T(8,128)S(1)}, u32[]{:S(2)}, u32[]{:S(2)}) collective-permute-start(f32[128,256]{1,0:T(8,128)S(1)} %get-tuple-element.47), channel_id=1, source_target_pairs={{0,8},{8,0},{16,24},{24,16},{1,9},{9,1},{17,25},{25,17},{2,10},{10... | collective-permute-start | bytes 393224 | tf_op jit(solution)/shard_map/ppermute | solution.py:447
  37.9 0.0 collective-permute-done.13.got
  37.9 3.3 %collective-permute-start.14 = (bf16[128,256]{1,0:T(8,128)(2,1)S(1)}, bf16[128,256]{1,0:T(8,128)(2,1)S(1)}, u32[]{:S(2)}, u32[]{:S(2)}) collective-permute-start(bf16[128,256]{1,0:T(8,128)(2,1)S(1)} %shard_map.54), channel_id=1, source_target_pairs={{0,8},{8,0},{16,24},{24,16},{1,9},{9,1},{17,25},{25,17},{2,10},{10... | collective-permute-start | bytes 196616 | tf_op jit(solution)/shard_map/ppermute | solution.py:444
  41.2 0.0 collective-permute-done.10.right_got
  41.2 2.4 %collective-permute-done.11.near = f32[128,256]{1,0:T(8,128)S(1)} collective-permute-done((f32[128,256]{1,0:T(8,128)S(1)}, f32[128,256]{1,0:T(8,128)S(1)}, u32[]{:S(2)}, u32[]{:S(2)}) %collective-permute-start.11) | collective-permute-done | bytes 131104 | tf_op jit(solution)/shard_map/ppermute | solution.py:447
  43.7 0.0 collective-permute-done.8.left_got
  43.7 0.0 collective-permute-done.12.far
  43.7 1.1 %collective-permute-done.14.settled = bf16[128,256]{1,0:T(8,128)(2,1)S(1)} collective-permute-done((bf16[128,256]{1,0:T(8,128)(2,1)S(1)}, bf16[128,256]{1,0:T(8,128)(2,1)S(1)}, u32[]{:S(2)}, u32[]{:S(2)}) %collective-permute-start.14) | collective-permute-done | bytes 65568 | tf_op jit(solution)/shard_map/ppermute | solution.py:444
  44.8 0.7 %shard_map.55 = bf16[128,512]{1,0:T(8,128)(2,1)} custom-call(f32[128,256]{1,0:T(8,128)S(1)} %get-tuple-element.41.left, f32[128,256]{1,0:T(8,128)S(1)} %collective-permute-done.8.left_got, f32[128,256]{1,0:T(8,128)S(1)} %get-tuple-element.45.right, f32[128,256]{1,0:T(8,128)S(1)} %collective-permute-done.10.right_got, ...), custom_call_target="tpu_custom_call" | custom-call | tf_op jit(solution)/shard_map/pallas_call | solution.py:400
  (8 shorter events, 0.1 us)
Async XLA Ops:
  1.2 16.0 %collective-permute-start = (bf16[2080,128]{1,0:T(8,128)(2,1)S(1)}, bf16[2080,128]{1,0:T(8,128)(2,1)S(1)}, u32[]{:S(2)}, u32[]{:S(2)}) collective-permute-start(bf16[2080,128]{1,0:T(8,128)(2,1)S(1)} %get-tuple-element.29), channel_id=1, source_target_pairs={{0,8},{8,0},{16,24},{24,16},{1,9},{9,1},{17,25},{25,17},{2,10},{10... | collective-permute-start | bytes 1597448 | tf_op jit(solution)/shard_map/ppermute | solution.py:423
  4.3 15.0 %collective-permute-start.5 = (bf16[2096,128]{1,0:T(8,128)(2,1)S(1)}, bf16[2096,128]{1,0:T(8,128)(2,1)S(1)}, u32[]{:S(2)}, u32[]{:S(2)}) collective-permute-start(bf16[2096,128]{1,0:T(8,128)(2,1)S(1)} %get-tuple-element.36.own), channel_id=1, source_target_pairs={{0,1},{1,0},{2,3},{3,2},{8,16},{9,17},{10,18},{11,19},{16,8},{17,9... | collective-permute-start | bytes 1609736 | tf_op jit(solution)/shard_map/ppermute | solution.py:422
  4.3 8.8 %collective-permute-start.1 = (bf16[1040,128]{1,0:T(8,128)(2,1)S(1)}, bf16[1040,128]{1,0:T(8,128)(2,1)S(1)}, u32[]{:S(2)}, u32[]{:S(2)}) collective-permute-start(bf16[1040,128]{1,0:T(8,128)(2,1)S(1)} %get-tuple-element.28.own_0), channel_id=1, source_target_pairs={{0,4},{4,0},{1,5},{5,1},{2,6},{6,2},{3,7},{7,3},{8,12},{12,8},{9,1... | collective-permute-start | bytes 798728 | tf_op jit(solution)/shard_map/ppermute | solution.py:425
  5.8 17.1 %collective-permute-start.3 = (bf16[1040,128]{1,0:T(8,128)(2,1)S(1)}, bf16[1040,128]{1,0:T(8,128)(2,1)S(1)}, u32[]{:S(2)}, u32[]{:S(2)}) collective-permute-start(bf16[1040,128]{1,0:T(8,128)(2,1)S(1)} %get-tuple-element.35), channel_id=1, source_target_pairs={{0,16},{16,24},{24,8},{8,0},{1,17},{17,25},{25,9},{9,1},{2,18},{18... | collective-permute-start | bytes 798728 | tf_op jit(solution)/shard_map/ppermute | solution.py:424
  13.1 14.7 %collective-permute-start.4 = (bf16[1040,128]{1,0:T(8,128)(2,1)S(1)}, bf16[1040,128]{1,0:T(8,128)(2,1)S(1)}, u32[]{:S(2)}, u32[]{:S(2)}) collective-permute-start(bf16[1040,128]{1,0:T(8,128)(2,1)S(1)} %get-tuple-element.35), channel_id=1, source_target_pairs={{0,8},{8,0},{16,24},{24,16},{1,9},{9,1},{17,25},{25,17},{2,10},{10... | collective-permute-start | bytes 798728 | tf_op jit(solution)/shard_map/ppermute | solution.py:427
  17.2 10.6 %collective-permute-start.2 = (bf16[1040,128]{1,0:T(8,128)(2,1)S(1)}, bf16[1040,128]{1,0:T(8,128)(2,1)S(1)}, u32[]{:S(2)}, u32[]{:S(2)}) collective-permute-start(bf16[1040,128]{1,0:T(8,128)(2,1)S(1)} %get-tuple-element.34.end_0), channel_id=1, source_target_pairs={{0,4},{4,0},{1,5},{5,1},{2,6},{6,2},{3,7},{7,3},{8,12},{12,8},{9,1... | collective-permute-start | bytes 798728 | tf_op jit(solution)/shard_map/ppermute | solution.py:431
  19.3 8.5 %collective-permute-start.6 = (bf16[1040,128]{1,0:T(8,128)(2,1)S(1)}, bf16[1040,128]{1,0:T(8,128)(2,1)S(1)}, u32[]{:S(2)}, u32[]{:S(2)}) collective-permute-start(bf16[1040,128]{1,0:T(8,128)(2,1)S(1)} %get-tuple-element.37.first), channel_id=1, source_target_pairs={{0,1},{1,0},{2,3},{3,2},{8,16},{9,17},{10,18},{11,19},{16,8},{17,9... | collective-permute-start | bytes 798728 | tf_op jit(solution)/shard_map/ppermute | solution.py:429
  27.9 2.0 %collective-permute-start.9 = (f32[512,256]{1,0:T(8,128)S(1)}, f32[512,256]{1,0:T(8,128)S(1)}, u32[]{:S(2)}, u32[]{:S(2)}) collective-permute-start(f32[512,256]{1,0:T(8,128)S(1)} %get-tuple-element.44), channel_id=1, source_target_pairs={{0,1},{1,0},{2,3},{3,2},{4,5},{5,4},{6,7},{7,6},{8,9},{9,8},{10,11... | collective-permute-start | bytes 1572872 | tf_op jit(solution)/shard_map/ppermute | solution.py:439
  28.1 2.5 %collective-permute-start.7 = (f32[512,256]{1,0:T(8,128)S(1)}, f32[512,256]{1,0:T(8,128)S(1)}, u32[]{:S(2)}, u32[]{:S(2)}) collective-permute-start(f32[512,256]{1,0:T(8,128)S(1)} %get-tuple-element.40), channel_id=1, source_target_pairs={{0,1},{1,0},{2,3},{3,2},{4,5},{5,4},{6,7},{7,6},{8,9},{9,8},{10,11... | collective-permute-start | bytes 1572872 | tf_op jit(solution)/shard_map/ppermute | solution.py:441
  29.9 8.0 %collective-permute-start.13 = (f32[128,256]{1,0:T(8,128)S(1)}, f32[128,256]{1,0:T(8,128)S(1)}, u32[]{:S(2)}, u32[]{:S(2)}) collective-permute-start(f32[128,256]{1,0:T(8,128)S(1)} %get-tuple-element.50), channel_id=1, source_target_pairs={{0,1},{1,0},{2,3},{3,2},{8,10},{9,11},{10,8},{11,9},{16,18},{17,19... | collective-permute-start | bytes 393224 | tf_op jit(solution)/shard_map/ppermute | solution.py:443
  30.7 13.0 %collective-permute-start.12 = (f32[136,256]{1,0:T(8,128)S(1)}, f32[136,256]{1,0:T(8,128)S(1)}, u32[]{:S(2)}, u32[]{:S(2)}) collective-permute-start(f32[136,256]{1,0:T(8,128)S(1)} %get-tuple-element.48), channel_id=1, source_target_pairs={{0,8},{1,9},{2,10},{3,11},{8,2},{9,3},{10,0},{11,1},{16,26},{17,27... | collective-permute-start | bytes 417800 | tf_op jit(solution)/shard_map/ppermute | solution.py:448
  36.4 4.8 %collective-permute-start.10 = (f32[128,256]{1,0:T(8,128)S(1)}, f32[128,256]{1,0:T(8,128)S(1)}, u32[]{:S(2)}, u32[]{:S(2)}) collective-permute-start(f32[128,256]{1,0:T(8,128)S(1)} %get-tuple-element.46), channel_id=1, source_target_pairs={{0,1},{1,0},{2,3},{3,2},{8,10},{9,11},{10,8},{11,9},{16,18},{17,19... | collective-permute-start | bytes 393224 | tf_op jit(solution)/shard_map/ppermute | solution.py:445
  36.4 7.2 %collective-permute-start.11 = (f32[128,256]{1,0:T(8,128)S(1)}, f32[128,256]{1,0:T(8,128)S(1)}, u32[]{:S(2)}, u32[]{:S(2)}) collective-permute-start(f32[128,256]{1,0:T(8,128)S(1)} %get-tuple-element.47), channel_id=1, source_target_pairs={{0,8},{8,0},{16,24},{24,16},{1,9},{9,1},{17,25},{25,17},{2,10},{10... | collective-permute-start | bytes 393224 | tf_op jit(solution)/shard_map/ppermute | solution.py:447
  37.9 5.8 %collective-permute-start.8 = (f32[128,256]{1,0:T(8,128)S(1)}, f32[128,256]{1,0:T(8,128)S(1)}, u32[]{:S(2)}, u32[]{:S(2)}) collective-permute-start(f32[128,256]{1,0:T(8,128)S(1)} %get-tuple-element.42), channel_id=1, source_target_pairs={{0,1},{1,0},{2,3},{3,2},{8,10},{9,11},{10,8},{11,9},{16,18},{17,19... | collective-permute-start | bytes 393224 | tf_op jit(solution)/shard_map/ppermute | solution.py:449
  37.9 6.8 %collective-permute-start.14 = (bf16[128,256]{1,0:T(8,128)(2,1)S(1)}, bf16[128,256]{1,0:T(8,128)(2,1)S(1)}, u32[]{:S(2)}, u32[]{:S(2)}) collective-permute-start(bf16[128,256]{1,0:T(8,128)(2,1)S(1)} %shard_map.54), channel_id=1, source_target_pairs={{0,8},{8,0},{16,24},{24,16},{1,9},{9,1},{17,25},{25,17},{2,10},{10... | collective-permute-start | bytes 196616 | tf_op jit(solution)/shard_map/ppermute | solution.py:444
